TPU v7x, 256 devices: a whole 4x4x8 slice. The times are simulated.
256 devices in a mesh: sec: 64 (over x, z, core), op: 4 (over y).
Axes of the slice: x: 4, y: 4, z: 8, core: 2. Of those that a mesh axis runs over, the one named last changes fastest.
Arguments:
- wavefunction: bfloat16 [4096, 128, 128], P('sec')
- vectors: bfloat16 [2, 4096, 128, 128], P(None, 'sec')
- left_env: bfloat16 [16, 1024, 128, 128], P('op', 'sec')
- right_env: bfloat16 [16, 1024, 128, 128], P('op', 'sec')
- left_pattern: int32 [16, 1024], P('op', 'sec'), may hold values 0 or 1
- right_pattern: int32 [16, 1024], P('op', 'sec'), may hold values 0 or 1
- block_left: int32 [4096], P('sec'), may hold values from 0 to 1023, as said below
- block_right: int32 [4096], replicated, may hold values from 0 to 1023, as said below
- left_dims: int32 [1024], P('sec'), may hold values from 32 to 128
- right_dims: int32 [1024], replicated, may hold values from 32 to 128
Outputs:
- sigma: bfloat16 [4096, 128, 128], P('sec', 'op')
- residual: bfloat16 [4096, 128, 128], P('sec', 'op')
- correlations: float32 [2], replicated
Inputs may be any that keep to these rules, and one draw needn't show every extreme that they name: Block b has a left sector with block_left[b] // 16 == b // 64. `block_right`: right sector j is owned by the index j // 16 of sec; of the 64 blocks of one index of sec, at most 2 have right sectors of one owner, and some owner has exactly 2 from every index of sec.
All inputs are finite; a program needn't handle non-finite values. No bound on the sum of `left_pattern` or of `right_pattern` on one device may be relied on, other than what follows from the above.
Results may differ from a plain program's by a relative error of at most 0.035.
Values may be sent and summed in bfloat16 or wider, within the bound.
No kernel may reach another device: no remote copies, remote signals or barrier semaphores. Data moves between devices by JAX's collectives and lax.ppermute only.
A program may use at most 192 MiB of HBM per device.

v0:
```python
import jax
import jax.numpy as jnp
from jax import lax
from jax.sharding import PartitionSpec as P


def pick_rows(table, labels, count):
    onehot = (labels[:, None] == jnp.arange(count, dtype=jnp.int32)[None, :]).astype(jnp.int32)
    return jnp.sum(onehot * table[None, :], axis=1)


def contract_right(received, sectors, right_table):

    def add_term(term_index, running):
        piece = lax.dynamic_index_in_dim(received, term_index, 1, keepdims=False)
        chosen = jnp.take(
            lax.dynamic_index_in_dim(right_table, term_index, 0, keepdims=False), sectors, axis=0
        )
        return running + jnp.einsum(
            "sik,slk->sil", piece, chosen, preferred_element_type=jnp.float32
        )

    start = jnp.zeros((received.shape[0], received.shape[2], right_table.shape[3]), jnp.float32)
    return lax.fori_loop(0, right_table.shape[0], add_term, start)


def local_products(psi_rows, vector_rows, sigma_part, psi_norm):
    cross_sum = jnp.sum(psi_rows.astype(jnp.float32) * sigma_part)
    norm_part = psi_norm.astype(jnp.float32)
    square_sum = jnp.sum(norm_part * norm_part)
    vector_sums = jnp.einsum("vbik,bik->v", vector_rows.astype(jnp.float32), sigma_part)
    return (cross_sum, square_sum, vector_sums)


def body(
    wavefunction,
    vectors,
    left_env,
    right_env,
    left_pattern,
    right_pattern,
    block_left,
    block_right,
    left_dims,
    right_dims,
):
    blocks = wavefunction.shape[0]
    width = wavefunction.shape[1]
    left_count = left_env.shape[1]
    right_count = right_env.shape[1]
    devices = lax.axis_size("sec")
    shares = lax.axis_size("op")
    capacity = 2 * blocks // devices
    slot_count = devices * capacity
    share_rows = width // shares
    here_index = lax.axis_index("sec")
    share_index = lax.axis_index("op")
    local_left = block_left - here_index * left_count
    every_owner = (block_right // right_count).reshape(devices, blocks)
    order_ids = jnp.arange(blocks, dtype=jnp.int32)
    earlier = order_ids[None, :] < order_ids[:, None]
    same_owner = every_owner[:, :, None] == every_owner[:, None, :]
    ranks = jnp.sum((same_owner & earlier[None]).astype(jnp.int32), axis=2)
    slot_table = every_owner * capacity + ranks
    send_slot = lax.dynamic_index_in_dim(slot_table, here_index, 0, keepdims=False)
    source_slots = jnp.arange(devices, dtype=jnp.int32)[:, None] * capacity + ranks
    arrival = jnp.where(every_owner == here_index, source_slots, slot_count).reshape(-1)
    recv_sector = (
        jnp.zeros((slot_count,), jnp.int32)
        .at[arrival]
        .set(block_right - here_index * right_count, mode="drop")
    )
    mine_right = lax.dynamic_slice_in_dim(block_right, here_index * blocks, blocks)
    positions = jnp.arange(width, dtype=jnp.int32)
    row_limit = pick_rows(left_dims, local_left, left_count)
    col_limit = pick_rows(right_dims, mine_right, right_dims.shape[0])
    live = (positions[None, :] < row_limit[:, None])[:, :, None] & (
        positions[None, :] < col_limit[:, None]
    )[:, None, :]
    amplitudes = jnp.where(live, wavefunction, jnp.zeros_like(wavefunction))
    left_table = left_env * left_pattern[:, :, None, None].astype(jnp.bfloat16)
    right_table = right_env * right_pattern[:, :, None, None].astype(jnp.bfloat16)
    left_chosen = jnp.take(left_table, local_left, axis=1)
    left_terms = jnp.einsum(
        "tbij,bjk->btik", left_chosen, amplitudes, preferred_element_type=jnp.float32
    ).astype(jnp.bfloat16)
    send_buffer = (
        jnp.zeros((slot_count,) + left_terms.shape[1:], jnp.bfloat16).at[send_slot].set(left_terms)
    )
    returned = lax.all_to_all(
        contract_right(
            lax.all_to_all(send_buffer, "sec", split_axis=0, concat_axis=0, tiled=True),
            recv_sector,
            right_table,
        ),
        "sec",
        split_axis=0,
        concat_axis=0,
        tiled=True,
    )
    mine = jnp.take(returned, send_slot, axis=0)
    psi_share = lax.dynamic_slice_in_dim(amplitudes, share_index * share_rows, share_rows, 1)
    vector_share = lax.dynamic_slice_in_dim(vectors, share_index * share_rows, share_rows, 2)
    masked = jnp.where(live, mine, jnp.zeros_like(mine))
    sigma_part = lax.psum_scatter(masked, "op", scatter_dimension=1, tiled=True)
    partial_sums = local_products(psi_share, vector_share, sigma_part, psi_share)
    cross_total, square_total, vector_total = lax.psum(
        (partial_sums[0], partial_sums[1], partial_sums[2]), ("sec", "op")
    )
    theta = cross_total / square_total
    residual = (sigma_part - theta * psi_share.astype(jnp.float32)).astype(jnp.bfloat16)
    return (sigma_part.astype(jnp.bfloat16), residual, vector_total)


def solution(mesh):
    placed = (
        P("sec", None, None),
        P(None, "sec", None, None),
        P("op", "sec", None, None),
        P("op", "sec", None, None),
        P("op", "sec"),
        P("op", "sec"),
        P("sec"),
        P(),
        P("sec"),
        P(),
    )
    return jax.shard_map(
        body,
        mesh=mesh,
        in_specs=placed,
        out_specs=(P("sec", "op", None), P("sec", "op", None), P()),
        check_vma=False,
    )
```

profile of v0, /device:TPU:32, one launch (start us, length us, event | category | flops | bytes accessed | tf_op | source)
XLA Modules:
  0.0 839.5 jit_solution(2145720313531389702)
XLA Ops:
  15.6 5.5 gather_fusion.1
  21.1 3.2 and_select_fusion.1
  24.3 9.8 %fusion.17 = bf16[64,4,128,128]{3,2,1,0:T(8,128)(2,1)} fusion(bf16[64,4,128,128]{3,2,1,0:T(8,128)(2,1)} %gather_fusion.1, pred[64]{0:T(512)(128)(4,1)S(1)} %get-tuple-element.143, bf16[64,128,128]{2,1,0:T(8,128)(2,1)S(1)} %and_select_fusion.1), kind=kOutput, calls=%fused_computation.24 | convolution fusion | flops 1082130432 | bytes 18874432 | tf_op jit(solution)/shard_map/tbij,bjk->btik/dot_general | solution.py:84
  34.1 6.3 broadcast_in_dim.85
  40.4 22.1 %scatter_fusion = bf16[128,4,128,128]{3,2,1,0:T(8,128)(2,1)} fusion(bf16[128,4,128,128]{3,2,1,0:T(8,128)(2,1)} %broadcast_in_dim.85, s32[64]{0:T(128)S(1)} %fusion.31, bf16[64,4,128,128]{3,2,1,0:T(8,128)(2,1)} %fusion.17), kind=kCustom, calls=%fused_computation.3 | custom fusion | bytes 25166080 | tf_op jit(solution)/shard_map/scatter | solution.py:88
  62.5 12.0 %all-to-all-start = ((bf16[128,4,128,128]{3,2,1,0:T(8,128)(2,1)}), bf16[128,4,128,128]{3,2,1,0:T(8,128)(2,1)}, u32[]{:S(2)}, u32[]{:S(2)}) async-start(bf16[128,4,128,128]{3,2,1,0:T(8,128)(2,1)} %scatter_fusion), calls=%async_computation | async-start | bytes 33554432 | tf_op jit(solution)/shard_map/all_to_all | solution.py:92
  74.7 15.5 %scatter_custom_fusion.1 = s32[128]{0:T(128)S(1)} fusion(s32[4096]{0:T(1024)S(1)} %get-tuple-element.148, s32[4096]{0:T(1024)S(1)} %get-tuple-element.147, s32[]{:T(128)} %constant.124.clone.1), kind=kCustom, calls=%fused_computation.72 | custom fusion | bytes 516 | tf_op jit(solution)/shard_map/scatter | solution.py:71
  92.0 346.3 %all-to-all-done = bf16[128,4,128,128]{3,2,1,0:T(8,128)(2,1)} async-done(((bf16[128,4,128,128]{3,2,1,0:T(8,128)(2,1)}), bf16[128,4,128,128]{3,2,1,0:T(8,128)(2,1)}, u32[]{:S(2)}, u32[]{:S(2)}) %all-to-all-start) | async-done | bytes 16777248 | tf_op jit(solution)/shard_map/all_to_all | solution.py:92
  438.3 58.6 %while.14 = (s32[]{:T(128)}, f32[128,128,128]{2,1,0:T(8,128)}, bf16[128,4,128,128]{3,2,1,0:T(8,128)(2,1)}, s32[128]{0:T(128)S(1)}, bf16[4,16,128,128]{3,2,1,0:T(8,128)(2,1)S(1)}, /*index=5*/s32[]{:T(128)}, s32[]{:T(128)}) while((s32[]{:T(128)}, f32[128,128,128]{2,1,0:T(8,128)}, bf16[128,4,128,128]{3,2,1,0:T(8,128)(2,1)}, ...), condition=%wide.region_6.7_spmd.clone, body=%wide.region_5.6_spmd.clone.sunk | while | flops 543164544 | bytes 34610520 | solution.py:24
  438.4 3.0 gather_fusion
  441.4 9.8 %select_add_fusion.2 = f32[128,128,128]{2,1,0:T(8,128)} fusion(f32[128,128,128]{2,1,0:T(8,128)} %get-tuple-element.190, pred[]{:T(512)S(6)} %compare.5, bf16[128,128,128]{2,1,0:T(8,128)(2,1)} %gather_fusion, pred[128]{0:T(512)(128)(4,1)S(1)} %compare_and_fusion.4, bf16[128,4,128,128]{3,2,1,0:T(8,128)(2,1)} %get-tuple-element.198, s32[]{:T(128)} %get-tuple-element.189), kind=kOutput, calls=%fused_computation.5.clone.1 | convolution fusion | flops 543162368 | bytes 25166464 | tf_op jit(solution)/shard_map/while/body/eval_jaxpr/sik,slk->sil/dot_general | solution.py:19
  451.3 3.0 gather_fusion
  454.3 12.2 %select_add_fusion.2 = f32[128,128,128]{2,1,0:T(8,128)} fusion(f32[128,128,128]{2,1,0:T(8,128)} %get-tuple-element.190, pred[]{:T(512)S(6)} %compare.5, bf16[128,128,128]{2,1,0:T(8,128)(2,1)} %gather_fusion, pred[128]{0:T(512)(128)(4,1)S(1)} %compare_and_fusion.4, bf16[128,4,128,128]{3,2,1,0:T(8,128)(2,1)} %get-tuple-element.198, s32[]{:T(128)} %get-tuple-element.189), kind=kOutput, calls=%fused_computation.5.clone.1 | convolution fusion | flops 543162368 | bytes 25166464 | tf_op jit(solution)/shard_map/while/body/eval_jaxpr/sik,slk->sil/dot_general | solution.py:19
  466.5 3.0 gather_fusion
  469.6 12.2 %select_add_fusion.2 = f32[128,128,128]{2,1,0:T(8,128)} fusion(f32[128,128,128]{2,1,0:T(8,128)} %get-tuple-element.190, pred[]{:T(512)S(6)} %compare.5, bf16[128,128,128]{2,1,0:T(8,128)(2,1)} %gather_fusion, pred[128]{0:T(512)(128)(4,1)S(1)} %compare_and_fusion.4, bf16[128,4,128,128]{3,2,1,0:T(8,128)(2,1)} %get-tuple-element.198, s32[]{:T(128)} %get-tuple-element.189), kind=kOutput, calls=%fused_computation.5.clone.1 | convolution fusion | flops 543162368 | bytes 25166464 | tf_op jit(solution)/shard_map/while/body/eval_jaxpr/sik,slk->sil/dot_general | solution.py:19
  481.8 3.0 gather_fusion
  484.8 12.2 %select_add_fusion.2 = f32[128,128,128]{2,1,0:T(8,128)} fusion(f32[128,128,128]{2,1,0:T(8,128)} %get-tuple-element.190, pred[]{:T(512)S(6)} %compare.5, bf16[128,128,128]{2,1,0:T(8,128)(2,1)} %gather_fusion, pred[128]{0:T(512)(128)(4,1)S(1)} %compare_and_fusion.4, bf16[128,4,128,128]{3,2,1,0:T(8,128)(2,1)} %get-tuple-element.198, s32[]{:T(128)} %get-tuple-element.189), kind=kOutput, calls=%fused_computation.5.clone.1 | convolution fusion | flops 543162368 | bytes 25166464 | tf_op jit(solution)/shard_map/while/body/eval_jaxpr/sik,slk->sil/dot_general | solution.py:19
  497.0 8.0 all-to-all-start.1
  505.2 183.8 %all-to-all-done.1 = f32[128,128,128]{2,1,0:T(8,128)} async-done(((f32[128,128,128]{2,1,0:T(8,128)}), f32[128,128,128]{2,1,0:T(8,128)}, u32[]{:S(2)}, u32[]{:S(2)}) %all-to-all-start.1) | async-done | bytes 8388640 | tf_op jit(solution)/shard_map/all_to_all | solution.py:90
  689.0 6.2 gather_fusion.2
  695.2 5.3 and_select_fusion
  702.9 45.8 %reduce-scatter.2.cloned.1.call-done = f32[64,32,128]{2,1,0:T(8,128)} async-done(((f32[64,128,128]{2,1,0:T(8,128)}), f32[64,32,128]{2,1,0:T(8,128)}) %reduce-scatter.2.cloned.1.call-update) | async-done | bytes 1048592 | tf_op jit(solution)/shard_map/reduce_scatter | solution.py:105
  748.7 4.6 convolution_bitcast_fusion
  754.2 75.9 %all-reduce = (f32[]{:T(128)}, f32[]{:T(128)}, f32[2]{0:T(128)}) all-reduce(f32[]{:T(128)} %get-tuple-element.127, f32[]{:T(128)} %get-tuple-element.126, f32[2]{0:T(128)S(1)} %convolution_bitcast_fusion), channel_id=1, replica_groups=mesh['sec'=64,'op'=4] {'sec','op'}, use_global_device_ids=true, to_apply=%region_9.10 | all-reduce | flops 4 | bytes 32 | tf_op jit(solution)/shard_map/psum | solution.py:107
  (54 shorter events, 15.3 us)
Async XLA Ops:
  24.3 9.8 %copy-start = (bf16[64,128,128]{2,1,0:T(8,128)(2,1)}, bf16[64,128,128]{2,1,0:T(8,128)(2,1)S(1)}, u32[]{:S(2)}) copy-start(bf16[64,128,128]{2,1,0:T(8,128)(2,1)S(1)} %and_select_fusion.1) | copy-start | bytes 6291460
  62.5 12.2 %copy-start.4 = (s32[4,16]{1,0:T(4,128)S(1)}, s32[4,16]{1,0:T(4,128)}, u32[]{:S(2)}) copy-start(s32[4,16]{1,0:T(4,128)} %param.17) | copy-start | bytes 772
  62.5 12.2 %copy-start.3 = (s32[4096]{0:T(1024)S(1)}, s32[4096]{0:T(1024)}, u32[]{:S(2)}) copy-start(s32[4096]{0:T(1024)} %param.19) | copy-start | bytes 49156
  62.5 375.9 %all-to-all-start = ((bf16[128,4,128,128]{3,2,1,0:T(8,128)(2,1)}), bf16[128,4,128,128]{3,2,1,0:T(8,128)(2,1)}, u32[]{:S(2)}, u32[]{:S(2)}) async-start(bf16[128,4,128,128]{3,2,1,0:T(8,128)(2,1)} %scatter_fusion), calls=%async_computation | async-start | bytes 33554432 | tf_op jit(solution)/shard_map/all_to_all | solution.py:92
  497.0 192.0 %all-to-all-start.1 = ((f32[128,128,128]{2,1,0:T(8,128)}), f32[128,128,128]{2,1,0:T(8,128)}, u32[]{:S(2)}, u32[]{:S(2)}) async-start(f32[128,128,128]{2,1,0:T(8,128)} %get-tuple-element.97), calls=%async_computation.1 | async-start | bytes 16777216 | tf_op jit(solution)/shard_map/all_to_all | solution.py:90
  505.0 243.7 %reduce-scatter.2.cloned.1.call-start = ((), (), s32[]{:S(2)}) async-start(), calls=%async_computation.3 | async-start | bytes 5242880 | tf_op jit(solution)/shard_map/reduce_scatter | solution.py:105
  702.9 50.4 %copy-start.1 = (bf16[64,128,128]{2,1,0:T(8,128)(2,1)S(1)}, bf16[64,128,128]{2,1,0:T(8,128)(2,1)}, u32[]{:S(2)}) copy-start(bf16[64,128,128]{2,1,0:T(8,128)(2,1)} %copy-done) | copy-start | bytes 6291460
  748.7 4.6 copy-start.2
Sparse Core Ops, SparseCore 0:
  700.6 48.0 reduce-scatter.1
where the time goes:
time: 842 us; the launch traced here: 839 us
  waiting for transfers between devices  576 us (68%)
  blocking collectives  75.9 us (9%)
  local copies, waits for them, and re-layouts  71.1 us (8%)
  matrix products  60.6 us (7%)
  starting transfers between devices  20.2 us (2%)
  other arithmetic  20.1 us (2%)
  between operations  15.5 us (2%)
    all_to_all x1, waiting for transfers between devices, body(): lax.all_to_all(send_buffer, 'sec', split_axis=0, concat_axis=0, tiled=True)  346 us
    all_to_all x1, waiting for transfers between devices, body(): lax.all_to_all(contract_right(lax.all_to_all(send_buffer, 'sec', split_ax...  184 us
    psum x1, blocking collectives, body(): lax.psum((partial_sums[0], partial_sums[1], partial_sums[2]), ('sec', 'op'))  75.9 us
    dot_general x4, matrix products, add_term(): jnp.einsum('sik,slk->sil', piece, chosen, preferred_element_type=jnp.floa...  46.3 us
    reduce_scatter x1, waiting for transfers between devices, body(): sigma_part = lax.psum_scatter(masked, 'op', scatter_dimension=1, tiled=True)  45.8 us
    scatter x1, local copies, waits for them, and re-layouts, body(): jnp.zeros((slot_count,) + left_terms.shape[1:], jnp.bfloat16).at[send_slot]  22.1 us
  transfers between devices with their start and end apart: 3, of which 3 were waited for; matrix products, arithmetic and copies ran while one was open for 2% of the time, Pallas kernels for 0%

commit v1 on v0

v1 whole, which is shorter than its diff:
```python
import jax
import jax.numpy as jnp
from jax import lax
from jax.experimental import pallas as pl
from jax.experimental.pallas import tpu as pltpu
from jax.sharding import PartitionSpec as P

NX, NZ, NC, NY = 4, 8, 2, 4
NG = NX * NC
BLOCKS, WIDTH, TERMS, SECTORS = 64, 128, 4, 16
ROWS = WIDTH // NY
VMEM = 48 * 1024 * 1024


def sec_index(x, z, c):
    return (x * NZ + z) * NC + c


GROUP_XC = [[sec_index(x, z, c) for x in range(NX) for c in range(NC)] for z in range(NZ)]
GROUP_Z = [[sec_index(x, z, c) for z in range(NZ)] for x in range(NX) for c in range(NC)]
RING_UP = [
    (sec_index(x, z, c), sec_index(x, (z + 1) % NZ, c))
    for x in range(NX)
    for z in range(NZ)
    for c in range(NC)
]
RING_DOWN = [(d, s) for s, d in RING_UP]
CHUNKS = ((0, 1, 7), (2, 6), (3, 5), (4,))


def smem():
    return pl.BlockSpec(memory_space=pltpu.SMEM)


def vmem():
    return pl.BlockSpec(memory_space=pltpu.VMEM)


def pack_kernel(place, block_left, block_right, left_dims, right_dims, psi, send, meta, route, rlim, clim, count):
    sec = place[0]
    z_here = place[1]

    def clear(i, carry):
        count[i] = 0
        return carry

    lax.fori_loop(0, NX * NZ * NC, clear, 0)

    def clear_meta(i, carry):
        meta[i] = -1
        return carry

    lax.fori_loop(0, NG * NZ * 2, clear_meta, 0)
    rows = lax.broadcasted_iota(jnp.int32, (WIDTH, WIDTH), 0)
    cols = lax.broadcasted_iota(jnp.int32, (WIDTH, WIDTH), 1)

    def one(b, carry):
        left = block_left[b] - sec * SECTORS
        right = block_right[sec * BLOCKS + b]
        owner = lax.shift_right_logical(right, 4)
        rank = count[owner]
        count[owner] = rank + 1
        x_r = lax.shift_right_logical(owner, 4)
        z_r = lax.shift_right_logical(owner, 1) & 7
        group = x_r * 2 + (owner & 1)
        delta = (z_r - z_here) & 7
        slot = group * 16 + delta * 2 + rank
        meta[slot] = left * 16 + (right & 15)
        route[b] = slot
        rl = left_dims[left]
        cl = right_dims[right]
        rlim[b] = rl
        clim[b] = cl
        block = psi[b].astype(jnp.float32)
        live = (rows < rl) & (cols < cl)
        send[slot] = jnp.where(live, block, 0.0).astype(jnp.bfloat16)
        return carry

    lax.fori_loop(0, BLOCKS, one, 0)


def pack(place, block_left, block_right, left_dims, right_dims, psi):
    slots = NG * NZ * 2
    return pl.pallas_call(
        pack_kernel,
        in_specs=[smem(), smem(), smem(), smem(), smem(), vmem()],
        out_specs=[vmem(), smem(), smem(), smem(), smem()],
        out_shape=[
            jax.ShapeDtypeStruct((slots, WIDTH, WIDTH), jnp.bfloat16),
            jax.ShapeDtypeStruct((slots,), jnp.int32),
            jax.ShapeDtypeStruct((BLOCKS,), jnp.int32),
            jax.ShapeDtypeStruct((BLOCKS,), jnp.int32),
            jax.ShapeDtypeStruct((BLOCKS,), jnp.int32),
        ],
        scratch_shapes=[pltpu.SMEM((NX * NZ * NC,), jnp.int32)],
        compiler_params=pltpu.CompilerParams(vmem_limit_bytes=VMEM),
        cost_estimate=pl.CostEstimate(flops=0, bytes_accessed=24 * 2**20, transcendentals=0),
        name="pack",
    )(place, block_left, block_right, left_dims, right_dims, psi)


def contract(deltas, psi_slots, left_all, rights, meta):
    width = len(deltas)
    steps = NG * width * 2

    def split(i):
        return i // (2 * width), (i // 2) % width, i % 2

    def delta_of(k):
        value = deltas[0]
        for n in range(1, width):
            value = jnp.where(k == n, deltas[n], value)
        return value

    def code(i, meta):
        g, k, r = split(i)
        return meta[g * 16 + delta_of(k) * 2 + r]

    def psi_map(i, meta):
        g, k, r = split(i)
        return (g, delta_of(k), r, 0, 0)

    def left_map(i, meta):
        g, k, r = split(i)
        return (g, 0, lax.shift_right_logical(jnp.maximum(code(i, meta), 0), 4), 0, 0)

    def right_map(n):
        def index(i, meta):
            g, k, r = split(i)
            at = g * 2 * width + n * 2 + jnp.where(k == n, r, jnp.where(k > n, 1, 0))
            return (0, jnp.maximum(code(at, meta), 0) & 15, 0, 0)

        return index

    def out_map(i, meta):
        g, k, r = split(i)
        return (g, k, r, 0, 0)

    def kernel(meta, psi, left, *rest):
        right_refs, out = rest[:-1], rest[-1]
        i = pl.program_id(0)
        g, k, r = split(i)

        def work(low, high):
            amp = psi[0, 0, 0]
            terms = lax.dot_general(
                left[0, :, 0].reshape(TERMS * WIDTH, WIDTH),
                amp,
                (((1,), (0,)), ((), ())),
                preferred_element_type=jnp.float32,
            ).astype(jnp.bfloat16)
            total = None
            for a in range(TERMS):
                ref = low if a < 2 else high
                part = lax.dot_general(
                    terms[a * WIDTH : (a + 1) * WIDTH],
                    ref[a % 2, 0],
                    (((1,), (1,)), ((), ())),
                    preferred_element_type=jnp.float32,
                )
                total = part if total is None else total + part
            out[0, 0, 0] = total

        valid = code(i, meta) >= 0
        for n in range(width):

            @pl.when(valid & (k == n))
            def _():
                work(right_refs[2 * n], right_refs[2 * n + 1])

    right_specs = []
    for n in range(width):
        right_specs += [pl.BlockSpec((2, 1, WIDTH, WIDTH), right_map(n))] * 2
    return pl.pallas_call(
        kernel,
        grid_spec=pltpu.PrefetchScalarGridSpec(
            num_scalar_prefetch=1,
            grid=(steps,),
            in_specs=[
                pl.BlockSpec((1, 1, 1, WIDTH, WIDTH), psi_map),
                pl.BlockSpec((1, TERMS, 1, WIDTH, WIDTH), left_map),
            ]
            + right_specs,
            out_specs=pl.BlockSpec((1, 1, 1, WIDTH, WIDTH), out_map),
        ),
        out_shape=jax.ShapeDtypeStruct((NG, width, 2, WIDTH, WIDTH), jnp.float32),
        compiler_params=pltpu.CompilerParams(vmem_limit_bytes=VMEM),
        cost_estimate=pl.CostEstimate(
            flops=steps * 2 * TERMS * 2 * WIDTH**3, bytes_accessed=steps * 352 * 1024, transcendentals=0
        ),
        name="contract",
    )(meta, psi_slots, left_all, *[half for pair in rights for half in pair])


def finish_kernel(place, route, rlim, clim, psi, vectors, *rest):
    returned, (sigma16, sigma32, sums) = rest[: len(CHUNKS)], rest[len(CHUNKS) :]
    first_row = place[2] * ROWS
    rows = lax.broadcasted_iota(jnp.int32, (ROWS, WIDTH), 0) + first_row
    cols = lax.broadcasted_iota(jnp.int32, (ROWS, WIDTH), 1)

    def one(b, carry):
        cross, square, first, second = carry
        slot = route[b]
        group = lax.shift_right_logical(slot, 4)
        delta = lax.shift_right_logical(slot, 1) & 7
        rank = slot & 1
        for n, deltas in enumerate(CHUNKS):
            for k, d in enumerate(deltas):

                @pl.when(delta == d)
                def _():
                    sigma32[b] = returned[n][group, k, rank]

        live = (rows < rlim[b]) & (cols < clim[b])
        value = jnp.where(live, sigma32[b], 0.0)
        amp = jnp.where(live, psi[b].astype(jnp.float32), 0.0)
        sigma32[b] = value
        sigma16[b] = value.astype(jnp.bfloat16)
        return (
            cross + amp * value,
            square + amp * amp,
            first + vectors[0, b].astype(jnp.float32) * value,
            second + vectors[1, b].astype(jnp.float32) * value,
        )

    zero = jnp.zeros((ROWS, WIDTH), jnp.float32)
    totals = lax.fori_loop(0, BLOCKS, one, (zero, zero, zero, zero))
    for n in range(4):
        sums[n] = jnp.sum(totals[n].reshape(ROWS // 8, 8, WIDTH), axis=0)


def finish(place, route, rlim, clim, psi, vectors, returned):
    def whole(shape):
        return pl.BlockSpec(shape, lambda i, *_: (0,) * len(shape))

    part = (BLOCKS, ROWS, WIDTH)
    return pl.pallas_call(
        finish_kernel,
        grid_spec=pltpu.PrefetchScalarGridSpec(
            num_scalar_prefetch=4,
            grid=(1,),
            in_specs=[
                pl.BlockSpec(part, lambda i, place, *_: (0, place[2], 0)),
                pl.BlockSpec((2,) + part, lambda i, place, *_: (0, 0, place[2], 0)),
            ]
            + [whole(r.shape) for r in returned],
            out_specs=[whole(part), whole(part), whole((4, 8, WIDTH))],
        ),
        out_shape=[
            jax.ShapeDtypeStruct(part, jnp.bfloat16),
            jax.ShapeDtypeStruct(part, jnp.float32),
            jax.ShapeDtypeStruct((4, 8, WIDTH), jnp.float32),
        ],
        compiler_params=pltpu.CompilerParams(vmem_limit_bytes=VMEM),
        cost_estimate=pl.CostEstimate(flops=0, bytes_accessed=10 * 2**20, transcendentals=0),
        name="finish",
    )(place, route, rlim, clim, psi, vectors, *returned)


def residual_kernel(place, rlim, clim, psi, sigma32, theta, out):
    first_row = place[2] * ROWS
    rows = lax.broadcasted_iota(jnp.int32, (ROWS, WIDTH), 0) + first_row
    cols = lax.broadcasted_iota(jnp.int32, (ROWS, WIDTH), 1)
    scale = theta[...]

    def one(b, carry):
        live = (rows < rlim[b]) & (cols < clim[b])
        amp = jnp.where(live, psi[b].astype(jnp.float32), 0.0)
        out[b] = (sigma32[b] - scale * amp).astype(jnp.bfloat16)
        return carry

    lax.fori_loop(0, BLOCKS, one, 0)


def make_residual(place, rlim, clim, psi, sigma32, theta):
    part = (BLOCKS, ROWS, WIDTH)
    return pl.pallas_call(
        residual_kernel,
        grid_spec=pltpu.PrefetchScalarGridSpec(
            num_scalar_prefetch=3,
            grid=(1,),
            in_specs=[
                pl.BlockSpec(part, lambda i, place, *_: (0, place[2], 0)),
                pl.BlockSpec(part, lambda i, *_: (0, 0, 0)),
                pl.BlockSpec((1, WIDTH), lambda i, *_: (0, 0)),
            ],
            out_specs=pl.BlockSpec(part, lambda i, *_: (0, 0, 0)),
        ),
        out_shape=jax.ShapeDtypeStruct(part, jnp.bfloat16),
        compiler_params=pltpu.CompilerParams(vmem_limit_bytes=VMEM),
        name="residual",
    )(place, rlim, clim, psi, sigma32, theta)


def exchange_groups(x):
    return lax.all_to_all(x, "sec", 0, 0, axis_index_groups=GROUP_XC)


def body(
    wavefunction,
    vectors,
    left_env,
    right_env,
    left_pattern,
    right_pattern,
    block_left,
    block_right,
    left_dims,
    right_dims,
):
    sec = lax.axis_index("sec").astype(jnp.int32)
    op = lax.axis_index("op").astype(jnp.int32)
    place = jnp.stack([sec, (sec // NC) % NZ, op]).astype(jnp.int32)

    right_table = right_env * right_pattern[:, :, None, None].astype(jnp.bfloat16)
    left_table = left_env * left_pattern[:, :, None, None].astype(jnp.bfloat16)
    halves = (right_table[:2], right_table[2:])
    rights = {0: halves}
    up, down = halves, halves
    for step in range(1, 4):
        up = tuple(lax.ppermute(h, "sec", RING_UP) for h in up)
        down = tuple(lax.ppermute(h, "sec", RING_DOWN) for h in down)
        rights[NZ - step] = up
        rights[step] = down
    rights[4] = (lax.ppermute(up[0], "sec", RING_UP), lax.ppermute(down[1], "sec", RING_DOWN))

    left_all = lax.all_gather(left_table, "sec", axis_index_groups=GROUP_XC)
    send, meta, route, rlim, clim = pack(place, block_left, block_right, left_dims, right_dims, wavefunction)
    psi_slots = exchange_groups(send.reshape(NG, NZ, 2, WIDTH, WIDTH))
    meta_all = exchange_groups(meta.reshape(NG, NZ * 2)).reshape(-1)

    returned = []
    for deltas in CHUNKS:
        partial = contract(deltas, psi_slots, left_all, [rights[d] for d in deltas], meta_all)
        summed = lax.psum_scatter(
            partial.reshape(-1, WIDTH, WIDTH), "op", scatter_dimension=1, tiled=True
        )
        returned.append(exchange_groups(summed.reshape(NG, len(deltas), 2, ROWS, WIDTH)))

    sigma16, sigma32, sums = finish(place, route, rlim, clim, wavefunction, vectors, returned)
    values = jnp.sum(sums, axis=(1, 2))
    values = lax.psum(values, "sec", axis_index_groups=GROUP_XC)
    values = lax.psum(values, "op")
    values = lax.psum(values, "sec", axis_index_groups=GROUP_Z)
    theta = values[0] / values[1]
    residual = make_residual(
        place, rlim, clim, wavefunction, sigma32, jnp.full((1, WIDTH), 1.0, jnp.float32) * theta
    )
    return (sigma16, residual, values[2:])


def solution(mesh):
    placed = (
        P("sec", None, None),
        P(None, "sec", None, None),
        P("op", "sec", None, None),
        P("op", "sec", None, None),
        P("op", "sec"),
        P("op", "sec"),
        P("sec"),
        P(),
        P("sec"),
        P(),
    )
    return jax.shard_map(
        body,
        mesh=mesh,
        in_specs=placed,
        out_specs=(P("sec", "op", None), P("sec", "op", None), P()),
        check_vma=False,
    )
```

time: 842 us -> 420 us (0.50)
  waiting for transfers between devices: 576 us -> 155 us
  Pallas kernels: 0 us -> 106 us
  matrix products: 60.6 us -> 0 us
  local copies, waits for them, and re-layouts: 71.1 us -> 14.3 us
  blocking collectives: 75.9 us -> 92.1 us
  other arithmetic: 20.1 us -> 4.91 us
  starting transfers between devices: 20.2 us -> 29.8 us
    all_to_all x2, waiting for transfers between devices: 530 us -> 41.8 us  [exchange_groups(): return lax.all_to_all(x, 'sec', 0, 0, axis_index_groups=GROUP_XC)]
    pallas_call x0 -> x7, Pallas kernels: none -> 106 us  [the longest x4 91.4 us: contract(): pl.pallas_call(kernel, grid_spec=pltpu.PrefetchScalarGridSpec(num_scalar_...]
    ppermute x0 -> x14, waiting for transfers between devices: none -> 96 us  [the longest x6 50.1 us: body(): up = tuple((lax.ppermute(h, 'sec', RING_UP) for h in up))]
    dot_general x6 -> x0, matrix products: 60.6 us -> none  [the longest x4 46.3 us: add_term(): jnp.einsum('sik,slk->sil', piece, chosen, preferred_element_type=jnp.floa...]
    all_to_all x0 -> x4, blocking collectives: none -> 52.2 us  [exchange_groups(): return lax.all_to_all(x, 'sec', 0, 0, axis_index_groups=GROUP_XC)]
    reduce_scatter x1 -> x4, waiting for transfers between devices: 45.8 us -> 1.34 us  [body(): lax.psum_scatter(partial.reshape(-1, WIDTH, WIDTH), 'op', scatter_dimensi...]
    scatter x2 -> x0, local copies, waits for them, and re-layouts: 37.6 us -> none  [the longest x1 22.1 us: body(): jnp.zeros((slot_count,) + left_terms.shape[1:], jnp.bfloat16).at[send_slot]]
    psum x1 -> x3, blocking collectives: 75.9 us -> 39.9 us  [the longest x1 18.7 us: body(): values = lax.psum(values, 'sec', axis_index_groups=GROUP_Z)]
  transfers between devices with their start and end apart: 3 -> 21, of which waited for: 3 -> 12; matrix products, arithmetic and copies ran while one was open for 2% -> 1% of each run, Pallas kernels for 0% -> 23%
where the time goes in v1:
time: 420 us; the launch traced here: 417 us
  waiting for transfers between devices  155 us (37%)
  Pallas kernels  106 us (25%)
  blocking collectives  92.1 us (22%)
  starting transfers between devices  29.8 us (7%)
  between operations  15.2 us (4%)
  local copies, waits for them, and re-layouts  14.3 us (3%)
  other arithmetic  4.91 us (1%)
    pallas_call x4, Pallas kernels, contract(): pl.pallas_call(kernel, grid_spec=pltpu.PrefetchScalarGridSpec(num_scalar_...  91.4 us
    all_to_all x4, blocking collectives, exchange_groups(): return lax.all_to_all(x, 'sec', 0, 0, axis_index_groups=GROUP_XC)  52.2 us
    ppermute x6, waiting for transfers between devices, body(): up = tuple((lax.ppermute(h, 'sec', RING_UP) for h in up))  50.1 us
    ppermute x6, waiting for transfers between devices, body(): down = tuple((lax.ppermute(h, 'sec', RING_DOWN) for h in down))  45.9 us
    all_to_all x2, waiting for transfers between devices, exchange_groups(): return lax.all_to_all(x, 'sec', 0, 0, axis_index_groups=GROUP_XC)  41.8 us
    psum x1, blocking collectives, body(): values = lax.psum(values, 'sec', axis_index_groups=GROUP_Z)  18.7 us
    all_gather x1, waiting for transfers between devices, body(): left_all = lax.all_gather(left_table, 'sec', axis_index_groups=GROUP_XC)  15.4 us
    ppermute x6, starting transfers between devices, body(): down = tuple((lax.ppermute(h, 'sec', RING_DOWN) for h in down))  12.9 us
  transfers between devices with their start and end apart: 21, of which 12 were waited for; matrix products, arithmetic and copies ran while one was open for 1% of the time, Pallas kernels for 23%

profile of v1, /device:TPU:32, one launch (start us, length us, event | category | flops | bytes accessed | tf_op | source)
XLA Modules:
  0.0 416.5 jit_solution(525390865130064851)
XLA Ops:
  16.2 5.7 %pack.1 = (bf16[128,128,128]{2,1,0:T(8,128)(2,1)}, s32[128]{0:T(128)S(1)}, s32[64]{0:T(128)S(1)}, s32[64]{0:T(128)S(1)}, s32[64]{0:T(128)S(1)}) custom-call(s32[3]{0:T(128)S(1)} %pad_add_fusion.place, s32[64]{0:T(128)S(1)} %copy-done.15, s32[4096]{0:T(1024)S(1)} %copy-done.13, s32[16]{0:T(128)S(1)} %copy-done.16, s32[1024]{0:T(1024)S(1)} %copy-done.14, ...), custom_call_target="tpu_custom_call" | custom-call | bytes 25165824 | tf_op jit(solution)/shard_map/pack/pallas_call | solution.py:84
  22.0 9.4 %all_to_all.34 = s32[8,1,16]{2,1,0:T(1,128)S(1)} all-to-all(s32[8,1,16]{2,1,0:T(1,128)S(1)} %bitcast.28), channel_id=1, replica_groups={{0,4,64,68,128,132,192,196},{8,12,72,76,136,140,200,204},{16,20,80,84,1..., dimensions={0} | all-to-all | bytes 1024 | tf_op jit(solution)/shard_map/all_to_all | solution.py:296
  31.3 4.6 %all-to-all-start.1 = ((bf16[8,8,2,128,128]{4,3,2,1,0:T(8,128)(2,1)}), bf16[8,8,2,128,128]{4,3,2,1,0:T(8,128)(2,1)}, u32[]{:S(2)}, u32[]{:S(2)}) async-start(bf16[8,8,2,128,128]{4,3,2,1,0:T(8,128)(2,1)} %bitcast.23), calls=%async_computation.1 | async-start | bytes 8388608 | tf_op jit(solution)/shard_map/all_to_all | solution.py:296
  43.5 22.8 %collective-permute-done.6.rest_2_ = bf16[2,16,128,128]{3,2,1,0:T(8,128)(2,1)S(1)} collective-permute-done((bf16[2,16,128,128]{3,2,1,0:T(8,128)(2,1)}, bf16[2,16,128,128]{3,2,1,0:T(8,128)(2,1)S(1)}, u32[]{:S(2)}, u32[]{:S(2)}) %collective-permute-start.6) | collective-permute-done | bytes 1048608 | tf_op jit(solution)/shard_map/ppermute | solution.py:321
  71.3 19.9 %collective-permute-done.10.rest_2_ = bf16[2,16,128,128]{3,2,1,0:T(8,128)(2,1)} collective-permute-done((bf16[2,16,128,128]{3,2,1,0:T(8,128)(2,1)S(1)}, bf16[2,16,128,128]{3,2,1,0:T(8,128)(2,1)}, u32[]{:S(2)}, u32[]{:S(2)}) %collective-permute-start.10) | collective-permute-done | bytes 1048608 | tf_op jit(solution)/shard_map/ppermute | solution.py:321
  94.3 3.8 collective-permute-start
  99.3 31.5 %all-to-all-done.1.psi = bf16[8,8,2,128,128]{4,3,2,1,0:T(8,128)(2,1)} async-done(((bf16[8,8,2,128,128]{4,3,2,1,0:T(8,128)(2,1)}), bf16[8,8,2,128,128]{4,3,2,1,0:T(8,128)(2,1)}, u32[]{:S(2)}, u32[]{:S(2)}) %all-to-all-start.1) | async-done | bytes 4194336 | tf_op jit(solution)/shard_map/all_to_all | solution.py:296
  130.9 15.4 %all-gather.3.cloned.1.call-done = bf16[32,16,128,128]{3,2,1,0:T(8,128)(2,1)} async-done(((bf16[4,16,128,128]{3,2,1,0:T(8,128)(2,1)}), bf16[32,16,128,128]{3,2,1,0:T(8,128)(2,1)}) %all-gather.3.cloned.1.call-update) | async-done | bytes 16777232 | tf_op jit(solution)/shard_map/all_gather | solution.py:327
  146.2 11.8 %contract.7 = f32[8,1,2,128,128]{4,3,2,1,0:T(8,128)S(1)} custom-call(s32[128]{0:T(128)S(1)} %reshape.46.meta, bf16[8,8,2,128,128]{4,3,2,1,0:T(8,128)(2,1)} %all-to-all-done.1.psi, bf16[8,4,16,128,128]{4,3,2,1,0:T(8,128)(2,1)} %bitcast.16, bf16[2,16,128,128]{3,2,1,0:T(8,128)(2,1)} %collective-permute-done.12.rest_0_, ...), custom_call_target="tpu_custom_call" | custom-call | flops 536870912 | bytes 5767168 | tf_op jit(solution)/shard_map/contract/pallas_call | solution.py:174
  161.2 22.5 %collective-permute-done.4.rest_0_ = bf16[2,16,128,128]{3,2,1,0:T(8,128)(2,1)S(1)} collective-permute-done((bf16[2,16,128,128]{3,2,1,0:T(8,128)(2,1)}, bf16[2,16,128,128]{3,2,1,0:T(8,128)(2,1)S(1)}, u32[]{:S(2)}, u32[]{:S(2)}) %collective-permute-start.4) | collective-permute-done | bytes 1048608 | tf_op jit(solution)/shard_map/ppermute | solution.py:322
  188.2 21.4 %contract.5 = f32[8,2,2,128,128]{4,3,2,1,0:T(8,128)} custom-call(s32[128]{0:T(128)S(1)} %reshape.46.meta, bf16[8,8,2,128,128]{4,3,2,1,0:T(8,128)(2,1)} %all-to-all-done.1.psi, bf16[8,4,16,128,128]{4,3,2,1,0:T(8,128)(2,1)} %bitcast.17, bf16[2,16,128,128]{3,2,1,0:T(8,128)(2,1)S(1)} %collective-permute-done.4.rest_0_, bf16[2,16,128,128]{3,2,1,0:T(8,128)(2,1)S(1)} %copy-done.8, ...), custom_call_target="tpu_custom_call" | custom-call | flops 1073741824 | bytes 11534336 | tf_op jit(solution)/shard_map/contract/pallas_call | solution.py:174
  209.7 3.7 collective-permute-start.8
  213.4 23.0 %collective-permute-done.8.rest_0_ = bf16[2,16,128,128]{3,2,1,0:T(8,128)(2,1)S(1)} collective-permute-done((bf16[2,16,128,128]{3,2,1,0:T(8,128)(2,1)}, bf16[2,16,128,128]{3,2,1,0:T(8,128)(2,1)S(1)}, u32[]{:S(2)}, u32[]{:S(2)}) %collective-permute-start.8) | collective-permute-done | bytes 1048608 | tf_op jit(solution)/shard_map/ppermute | solution.py:322
  238.5 22.3 %contract.6 = f32[8,2,2,128,128]{4,3,2,1,0:T(8,128)} custom-call(s32[128]{0:T(128)S(1)} %reshape.46.meta, bf16[8,8,2,128,128]{4,3,2,1,0:T(8,128)(2,1)} %all-to-all-done.1.psi, bf16[8,4,16,128,128]{4,3,2,1,0:T(8,128)(2,1)} %bitcast.18, bf16[2,16,128,128]{3,2,1,0:T(8,128)(2,1)S(1)} %collective-permute-done.8.rest_0_, ...), custom_call_target="tpu_custom_call" | custom-call | flops 1073741824 | bytes 11534336 | tf_op jit(solution)/shard_map/contract/pallas_call | solution.py:174
  260.8 35.9 %contract.4 = f32[8,3,2,128,128]{4,3,2,1,0:T(8,128)} custom-call(s32[128]{0:T(128)S(1)} %reshape.46.meta, bf16[8,8,2,128,128]{4,3,2,1,0:T(8,128)(2,1)} %all-to-all-done.1.psi, bf16[8,4,16,128,128]{4,3,2,1,0:T(8,128)(2,1)} %bitcast.19, bf16[2,16,128,128]{3,2,1,0:T(8,128)(2,1)} %get-tuple-element.20.rest_0_, ...), custom_call_target="tpu_custom_call" | custom-call | flops 1610612736 | bytes 17301504 | tf_op jit(solution)/shard_map/contract/pallas_call | solution.py:174
  296.8 10.9 %all_to_all.35.rest_3_ = f32[8,1,2,32,128]{4,3,2,1,0:T(8,128)S(1)} all-to-all(f32[8,1,2,32,128]{4,3,2,1,0:T(8,128)} %bitcast.27), channel_id=1, replica_groups={{0,4,64,68,128,132,192,196},{8,12,72,76,136,140,200,204},{16,20,80,84,1..., dimensions={0} | all-to-all | bytes 524288 | tf_op jit(solution)/shard_map/all_to_all | solution.py:296
  307.7 3.5 all-to-all-start.3
  311.2 10.2 %all-to-all-done.3.rest_1_ = f32[8,2,2,32,128]{4,3,2,1,0:T(8,128)S(1)} async-done(((f32[8,2,2,32,128]{4,3,2,1,0:T(8,128)}), f32[8,2,2,32,128]{4,3,2,1,0:T(8,128)S(1)}, u32[]{:S(2)}, u32[]{:S(2)}) %all-to-all-start.3) | async-done | bytes 524320 | tf_op jit(solution)/shard_map/all_to_all | solution.py:296
  321.4 14.5 %all_to_all.36.rest_2_ = f32[8,2,2,32,128]{4,3,2,1,0:T(8,128)} all-to-all(f32[8,2,2,32,128]{4,3,2,1,0:T(8,128)} %bitcast.26), channel_id=1, replica_groups={{0,4,64,68,128,132,192,196},{8,12,72,76,136,140,200,204},{16,20,80,84,1..., dimensions={0} | all-to-all | bytes 1048576 | tf_op jit(solution)/shard_map/all_to_all | solution.py:296
  337.2 17.5 %all_to_all.37.rest_0_ = f32[8,3,2,32,128]{4,3,2,1,0:T(8,128)S(1)} all-to-all(f32[8,3,2,32,128]{4,3,2,1,0:T(8,128)} %bitcast.24), channel_id=1, replica_groups={{0,4,64,68,128,132,192,196},{8,12,72,76,136,140,200,204},{16,20,80,84,1..., dimensions={0} | all-to-all | bytes 1572864 | tf_op jit(solution)/shard_map/all_to_all | solution.py:296
  356.8 6.4 %finish.1 = (bf16[64,32,128]{2,1,0:T(8,128)(2,1)}, f32[64,32,128]{2,1,0:T(8,128)S(1)}, f32[4,8,128]{2,1,0:T(8,128)S(1)}) custom-call(s32[3]{0:T(128)S(1)} %pad_add_fusion.place, s32[64]{0:T(128)S(1)} %get-tuple-element.11.route, s32[64]{0:T(128)S(1)} %get-tuple-element.12.rlim, s32[64]{0:T(128)S(1)} %get-tuple-element.13.clim, ...), custom_call_target="tpu_custom_call" | custom-call | bytes 10485760 | tf_op jit(solution)/shard_map/finish/pallas_call | solution.py:237
  364.4 12.6 %psum.21 = f32[4]{0:T(128)S(1)} all-reduce(f32[4]{0:T(128)S(1)} %reduce_sum.9), channel_id=1, replica_groups={{0,4,64,68,128,132,192,196},{8,12,72,76,136,140,200,204},{16,20,80,84,1..., use_global_device_ids=true, to_apply=%region_5.6 | all-reduce | flops 4 | bytes 32 | tf_op jit(solution)/shard_map/psum | solution.py:342
  377.0 8.6 %psum.22 = f32[4]{0:T(128)S(1)} all-reduce(f32[4]{0:T(128)S(1)} %psum.21), channel_id=1, replica_groups=mesh['sec'=64,'op'=4] {'op'}, use_global_device_ids=true, to_apply=%region_6.7 | all-reduce | flops 4 | bytes 32 | tf_op jit(solution)/shard_map/psum | solution.py:343
  385.6 18.7 %psum.23 = f32[4]{0:T(128)S(1)} all-reduce(f32[4]{0:T(128)S(1)} %psum.22), channel_id=1, replica_groups={{0,8,16,24,32,40,48,56},{4,12,20,28,36,44,52,60},{64,72,80,88,96,104,11..., use_global_device_ids=true, to_apply=%region_7.8 | all-reduce | flops 4 | bytes 32 | tf_op jit(solution)/shard_map/psum | solution.py:344
  (89 shorter events, 44.6 us)
Async XLA Ops:
  7.2 139.1 %all-gather.3.cloned.1.call-start = ((), (), s32[]{:S(2)}) async-start(), calls=%async_computation.14 | async-start | bytes 18874368 | tf_op jit(solution)/shard_map/all_gather | solution.py:327
  14.1 25.2 %collective-permute-start.2 = (bf16[2,16,128,128]{3,2,1,0:T(8,128)(2,1)}, bf16[2,16,128,128]{3,2,1,0:T(8,128)(2,1)}, u32[]{:S(2)}, u32[]{:S(2)}) collective-permute-start(bf16[2,16,128,128]{3,2,1,0:T(8,128)(2,1)} %get-tuple-element.20.rest_0_), channel_id=1, source_target_pairs={{0,8},{4,12},{8,16},{12,20},{16,24},{20,28},{24,32},{28,36},{32,40... | collective-permute-start | bytes 3145736 | tf_op jit(solution)/shard_map/ppermute | solution.py:321
  16.0 25.2 %collective-permute-start.1 = (bf16[2,16,128,128]{3,2,1,0:T(8,128)(2,1)S(1)}, bf16[2,16,128,128]{3,2,1,0:T(8,128)(2,1)}, u32[]{:S(2)}, u32[]{:S(2)}) collective-permute-start(bf16[2,16,128,128]{3,2,1,0:T(8,128)(2,1)S(1)} %get-tuple-element.19.rest_1_), channel_id=1, source_target_pairs={{8,0},{12,4},{16,8},{20,12},{24,16},{28,20},{32,24},{36,28},{40,32... | collective-permute-start | bytes 3145736 | tf_op jit(solution)/shard_map/ppermute | solution.py:322
  31.3 99.5 %all-to-all-start.1 = ((bf16[8,8,2,128,128]{4,3,2,1,0:T(8,128)(2,1)}), bf16[8,8,2,128,128]{4,3,2,1,0:T(8,128)(2,1)}, u32[]{:S(2)}, u32[]{:S(2)}) async-start(bf16[8,8,2,128,128]{4,3,2,1,0:T(8,128)(2,1)} %bitcast.23), calls=%async_computation.1 | async-start | bytes 8388608 | tf_op jit(solution)/shard_map/all_to_all | solution.py:296
  35.9 260.9 %reduce-scatter.11.cloned.1.call-start = ((), (), s32[]{:S(2)}) async-start(), calls=%async_computation.13 | async-start | bytes 1310720 | tf_op jit(solution)/shard_map/reduce_scatter | solution.py:335
  39.3 27.0 %collective-permute-start.6 = (bf16[2,16,128,128]{3,2,1,0:T(8,128)(2,1)}, bf16[2,16,128,128]{3,2,1,0:T(8,128)(2,1)S(1)}, u32[]{:S(2)}, u32[]{:S(2)}) collective-permute-start(bf16[2,16,128,128]{3,2,1,0:T(8,128)(2,1)} %collective-permute-done.2.rest_4_), channel_id=1, source_target_pairs={{0,8},{4,12},{8,16},{12,20},{16,24},{20,28},{24,32},{28,36},{32,40... | collective-permute-start | bytes 3145736 | tf_op jit(solution)/shard_map/ppermute | solution.py:321
  41.2 26.1 %collective-permute-start.5 = (bf16[2,16,128,128]{3,2,1,0:T(8,128)(2,1)}, bf16[2,16,128,128]{3,2,1,0:T(8,128)(2,1)S(1)}, u32[]{:S(2)}, u32[]{:S(2)}) collective-permute-start(bf16[2,16,128,128]{3,2,1,0:T(8,128)(2,1)} %collective-permute-done.1.rest_3_), channel_id=1, source_target_pairs={{8,0},{12,4},{16,8},{20,12},{24,16},{28,20},{32,24},{36,28},{40,32... | collective-permute-start | bytes 3145736 | tf_op jit(solution)/shard_map/ppermute | solution.py:322
  66.3 24.8 %collective-permute-start.10 = (bf16[2,16,128,128]{3,2,1,0:T(8,128)(2,1)S(1)}, bf16[2,16,128,128]{3,2,1,0:T(8,128)(2,1)}, u32[]{:S(2)}, u32[]{:S(2)}) collective-permute-start(bf16[2,16,128,128]{3,2,1,0:T(8,128)(2,1)S(1)} %collective-permute-done.6.rest_2_), channel_id=1, source_target_pairs={{0,8},{4,12},{8,16},{12,20},{16,24},{20,28},{24,32},{28,36},{32,40... | collective-permute-start | bytes 3145736 | tf_op jit(solution)/shard_map/ppermute | solution.py:321
  67.3 24.2 %collective-permute-start.9 = (bf16[2,16,128,128]{3,2,1,0:T(8,128)(2,1)S(1)}, bf16[2,16,128,128]{3,2,1,0:T(8,128)(2,1)}, u32[]{:S(2)}, u32[]{:S(2)}) collective-permute-start(bf16[2,16,128,128]{3,2,1,0:T(8,128)(2,1)S(1)} %collective-permute-done.5.rest_1_), channel_id=1, source_target_pairs={{8,0},{12,4},{16,8},{20,12},{24,16},{28,20},{32,24},{36,28},{40,32... | collective-permute-start | bytes 3145736 | tf_op jit(solution)/shard_map/ppermute | solution.py:322
  91.2 39.7 %collective-permute-start.12 = (bf16[2,16,128,128]{3,2,1,0:T(8,128)(2,1)}, bf16[2,16,128,128]{3,2,1,0:T(8,128)(2,1)}, u32[]{:S(2)}, u32[]{:S(2)}) collective-permute-start(bf16[2,16,128,128]{3,2,1,0:T(8,128)(2,1)} %collective-permute-done.10.rest_2_), channel_id=1, source_target_pairs={{0,8},{4,12},{8,16},{12,20},{16,24},{20,28},{24,32},{28,36},{32,40... | collective-permute-start | bytes 3145736 | tf_op jit(solution)/shard_map/ppermute | solution.py:325
  91.5 39.4 %collective-permute-start.13 = (bf16[2,16,128,128]{3,2,1,0:T(8,128)(2,1)}, bf16[2,16,128,128]{3,2,1,0:T(8,128)(2,1)}, u32[]{:S(2)}, u32[]{:S(2)}) collective-permute-start(bf16[2,16,128,128]{3,2,1,0:T(8,128)(2,1)} %collective-permute-done.9.rest_1_), channel_id=1, source_target_pairs={{8,0},{12,4},{16,8},{20,12},{24,16},{28,20},{32,24},{36,28},{40,32... | collective-permute-start | bytes 3145736 | tf_op jit(solution)/shard_map/ppermute | solution.py:325
  94.3 64.9 %collective-permute-start = (bf16[2,16,128,128]{3,2,1,0:T(8,128)(2,1)}, bf16[2,16,128,128]{3,2,1,0:T(8,128)(2,1)}, u32[]{:S(2)}, u32[]{:S(2)}) collective-permute-start(bf16[2,16,128,128]{3,2,1,0:T(8,128)(2,1)} %get-tuple-element.20.rest_0_), channel_id=1, source_target_pairs={{8,0},{12,4},{16,8},{20,12},{24,16},{28,20},{32,24},{36,28},{40,32... | collective-permute-start | bytes 3145736 | tf_op jit(solution)/shard_map/ppermute | solution.py:322
  98.1 61.2 %collective-permute-start.3 = (bf16[2,16,128,128]{3,2,1,0:T(8,128)(2,1)S(1)}, bf16[2,16,128,128]{3,2,1,0:T(8,128)(2,1)}, u32[]{:S(2)}, u32[]{:S(2)}) collective-permute-start(bf16[2,16,128,128]{3,2,1,0:T(8,128)(2,1)S(1)} %get-tuple-element.19.rest_1_), channel_id=1, source_target_pairs={{0,8},{4,12},{8,16},{12,20},{16,24},{20,28},{24,32},{28,36},{32,40... | collective-permute-start | bytes 3145736 | tf_op jit(solution)/shard_map/ppermute | solution.py:321
  159.1 148.6 %reduce-scatter.7.cloned.1.call-start = ((), (), s32[]{:S(2)}) async-start(), calls=%async_computation.11 | async-start | bytes 2621440 | tf_op jit(solution)/shard_map/reduce_scatter | solution.py:335
  159.1 24.6 %collective-permute-start.4 = (bf16[2,16,128,128]{3,2,1,0:T(8,128)(2,1)}, bf16[2,16,128,128]{3,2,1,0:T(8,128)(2,1)S(1)}, u32[]{:S(2)}, u32[]{:S(2)}) collective-permute-start(bf16[2,16,128,128]{3,2,1,0:T(8,128)(2,1)} %collective-permute-done.rest_2_), channel_id=1, source_target_pairs={{8,0},{12,4},{16,8},{20,12},{24,16},{28,20},{32,24},{36,28},{40,32... | collective-permute-start | bytes 3145736 | tf_op jit(solution)/shard_map/ppermute | solution.py:322
  159.2 26.5 %collective-permute-start.7 = (bf16[2,16,128,128]{3,2,1,0:T(8,128)(2,1)}, bf16[2,16,128,128]{3,2,1,0:T(8,128)(2,1)S(1)}, u32[]{:S(2)}, u32[]{:S(2)}) collective-permute-start(bf16[2,16,128,128]{3,2,1,0:T(8,128)(2,1)} %collective-permute-done.3.rest_5_), channel_id=1, source_target_pairs={{0,8},{4,12},{8,16},{12,20},{16,24},{20,28},{24,32},{28,36},{32,40... | collective-permute-start | bytes 3145736 | tf_op jit(solution)/shard_map/ppermute | solution.py:321
  183.8 25.8 %copy-start.9 = (bf16[2,16,128,128]{3,2,1,0:T(8,128)(2,1)}, bf16[2,16,128,128]{3,2,1,0:T(8,128)(2,1)S(1)}, u32[]{:S(2)}) copy-start(bf16[2,16,128,128]{3,2,1,0:T(8,128)(2,1)S(1)} %collective-permute-done.4.rest_0_) | copy-start | bytes 3145732
  188.2 21.4 %copy-start.10 = (bf16[2,16,128,128]{3,2,1,0:T(8,128)(2,1)}, bf16[2,16,128,128]{3,2,1,0:T(8,128)(2,1)S(1)}, u32[]{:S(2)}) copy-start(bf16[2,16,128,128]{3,2,1,0:T(8,128)(2,1)S(1)} %collective-permute-done.7.rest_3_) | copy-start | bytes 3145732
  209.6 101.6 %reduce-scatter.9.cloned.1.call-start = ((), (), s32[]{:S(2)}) async-start(), calls=%async_computation.12 | async-start | bytes 2621440 | tf_op jit(solution)/shard_map/reduce_scatter | solution.py:335
  209.7 26.7 %collective-permute-start.8 = (bf16[2,16,128,128]{3,2,1,0:T(8,128)(2,1)}, bf16[2,16,128,128]{3,2,1,0:T(8,128)(2,1)S(1)}, u32[]{:S(2)}, u32[]{:S(2)}) collective-permute-start(bf16[2,16,128,128]{3,2,1,0:T(8,128)(2,1)} %copy-done.9), channel_id=1, source_target_pairs={{8,0},{12,4},{16,8},{20,12},{24,16},{28,20},{32,24},{36,28},{40,32... | collective-permute-start | bytes 3145736 | tf_op jit(solution)/shard_map/ppermute | solution.py:322
  213.4 25.1 %collective-permute-start.11 = (bf16[2,16,128,128]{3,2,1,0:T(8,128)(2,1)}, bf16[2,16,128,128]{3,2,1,0:T(8,128)(2,1)S(1)}, u32[]{:S(2)}, u32[]{:S(2)}) collective-permute-start(bf16[2,16,128,128]{3,2,1,0:T(8,128)(2,1)} %copy-done.10), channel_id=1, source_target_pairs={{0,8},{4,12},{8,16},{12,20},{16,24},{20,28},{24,32},{28,36},{32,40... | collective-permute-start | bytes 3145736 | tf_op jit(solution)/shard_map/ppermute | solution.py:321
  260.8 76.5 %reduce-scatter.5.cloned.1.call-start = ((), (), s32[]{:S(2)}) async-start(), calls=%async_computation.10 | async-start | bytes 3932160 | tf_op jit(solution)/shard_map/reduce_scatter | solution.py:335
  307.7 13.8 %all-to-all-start.3 = ((f32[8,2,2,32,128]{4,3,2,1,0:T(8,128)}), f32[8,2,2,32,128]{4,3,2,1,0:T(8,128)S(1)}, u32[]{:S(2)}, u32[]{:S(2)}) async-start(f32[8,2,2,32,128]{4,3,2,1,0:T(8,128)} %bitcast.25), calls=%async_computation.5 | async-start | bytes 1048576 | tf_op jit(solution)/shard_map/all_to_all | solution.py:296
  321.4 15.8 %copy-start.2 = (f32[8,2,2,32,128]{4,3,2,1,0:T(8,128)}, f32[8,2,2,32,128]{4,3,2,1,0:T(8,128)S(1)}, u32[]{:S(2)}) copy-start(f32[8,2,2,32,128]{4,3,2,1,0:T(8,128)S(1)} %all-to-all-done.3.rest_1_) | copy-start | bytes 1572868
  (16 other events, 28.4 us)
Sparse Core Ops, SparseCore 0:
  11.2 134.9 all-gather.2
  159.2 26.4 reduce-scatter.10
  209.8 34.4 reduce-scatter.6
  260.9 32.4 reduce-scatter.8
  296.9 40.3 reduce-scatter.4

commit v2 on v0

v2 whole, which is shorter than its diff:
```python
import jax
import jax.numpy as jnp
from jax import lax
from jax.experimental import pallas as pl
from jax.experimental.pallas import tpu as pltpu
from jax.sharding import PartitionSpec as P

NX, NZ, NC, NY = 4, 8, 2, 4
NG = NX * NC
DEVICES = NX * NZ * NC * NY
BLOCKS, WIDTH, TERMS, SECTORS = 64, 128, 4, 16
ROWS = WIDTH // NY
PIECE = 4 * WIDTH
HEAD = 16
BATCH = 4
DEPTH = 3 * BATCH
CODE_BITS = 13.0
VMEM = 48 * 1024 * 1024
NOTHING = pl.CostEstimate(flops=1024, bytes_accessed=1024, transcendentals=0)


def sec_index(x, z, c):
    return (x * NZ + z) * NC + c


GROUP_XC = [[sec_index(x, z, c) for x in range(NX) for c in range(NC)] for z in range(NZ)]
GROUP_XCY = [
    [sec_index(x, z, c) * NY + y for x in range(NX) for c in range(NC) for y in range(NY)]
    for z in range(NZ)
]
RING_UP = [
    (sec_index(x, z, c), sec_index(x, (z + 1) % NZ, c))
    for x in range(NX)
    for z in range(NZ)
    for c in range(NC)
]
RING_DOWN = [(d, s) for s, d in RING_UP]
OP_UP = [(y, (y + 1) % NY) for y in range(NY)]
OP_DOWN = [(d, s) for s, d in OP_UP]
NEAR, MIDDLE, FAR = (0, 1, 7, 2, 6), (3, 5), (4,)


def smem():
    return pl.BlockSpec(memory_space=pltpu.SMEM)


def vmem():
    return pl.BlockSpec(memory_space=pltpu.VMEM)


def anywhere():
    return pl.BlockSpec(memory_space=pl.ANY)


def pack_kernel(
    place, block_left, block_right, left_dims, right_dims, psi, send, route, rlim, clim, count, codes
):
    sec = place[0]
    z_here = place[1]
    op = place[2]

    def clear(i, carry):
        count[i] = 0
        return carry

    lax.fori_loop(0, NX * NZ * NC, clear, 0)
    codes[...] = jnp.zeros_like(codes)
    rows = lax.broadcasted_iota(jnp.int32, (WIDTH, WIDTH), 0)
    cols = lax.broadcasted_iota(jnp.int32, (WIDTH, WIDTH), 1)

    def one(b, carry):
        left = block_left[b] - sec * SECTORS
        right = block_right[sec * BLOCKS + b]
        owner = lax.shift_right_logical(right, 4)
        rank = count[owner]
        count[owner] = rank + 1
        x_r = lax.shift_right_logical(owner, 4)
        z_r = lax.shift_right_logical(owner, 1) & 7
        group = x_r * 2 + (owner & 1)
        delta = (z_r - z_here) & 7
        route[b] = group * 16 + delta * 2 + rank
        rl = left_dims[left]
        cl = right_dims[right]
        rlim[b] = rl
        clim[b] = cl

        @pl.when(lax.shift_right_logical(delta, 1) == op)
        def _():
            sub = (delta & 1) * 2 + rank
            block = psi[b].astype(jnp.float32)
            live = (rows < rl) & (cols < cl)
            start = pl.multiple_of(sub * WIDTH, WIDTH)
            send[group, pl.ds(start, WIDTH)] = jnp.where(live, block, 0.0).astype(jnp.bfloat16)
            code = (left * 16 + (right & 15) + 1).astype(jnp.float32)
            codes[group, pl.ds(sub, 1)] = jnp.full((1, WIDTH), 1.0, jnp.float32) * code

        return carry

    lax.fori_loop(0, BLOCKS, one, 0)
    send[:, PIECE:] = codes[...].astype(jnp.bfloat16)


def pack(place, block_left, block_right, left_dims, right_dims, psi):
    return pl.pallas_call(
        pack_kernel,
        in_specs=[smem(), smem(), smem(), smem(), smem(), vmem()],
        out_specs=[vmem(), smem(), smem(), smem()],
        out_shape=[
            jax.ShapeDtypeStruct((NG, PIECE + HEAD, WIDTH), jnp.bfloat16),
            jax.ShapeDtypeStruct((BLOCKS,), jnp.int32),
            jax.ShapeDtypeStruct((BLOCKS,), jnp.int32),
            jax.ShapeDtypeStruct((BLOCKS,), jnp.int32),
        ],
        scratch_shapes=[
            pltpu.SMEM((NX * NZ * NC,), jnp.int32),
            pltpu.VMEM((NG, HEAD, WIDTH), jnp.float32),
        ],
        compiler_params=pltpu.CompilerParams(vmem_limit_bytes=VMEM),
        cost_estimate=NOTHING,
        name="pack",
    )(place, block_left, block_right, left_dims, right_dims, psi)


def contract(deltas, place, meta, pieces, left_all, rights, carried=None):
    slots = len(deltas) * 2
    most = NG * slots
    rows_own = slots * ROWS + HEAD
    rows_out = rows_own + (0 if carried is None else carried.shape[2])
    split = [len(r) for r in rights]

    def kernel(place, meta, own, below, above, far_low, far_high, left, *rest):
        right_refs, rest = rest[: sum(split)], rest[sum(split) :]
        if carried is not None:
            earlier, rest = rest[0], rest[1:]
        out, listed, psi_buf, left_buf, right_buf, heads, sems = rest
        op = place[2]
        heads[...] = jnp.zeros_like(heads)

        count = jnp.int32(0)
        for k, d in enumerate(deltas):
            relative = (d // 2 - op) & 3

            def scan(i, count):
                g = lax.shift_right_logical(i, 1)
                r = i & 1
                sub = (d & 1) * 2 + r
                code = meta[relative * NG * 4 + g * 4 + sub]

                @pl.when(code > 0)
                def _():
                    listed[count] = (
                        (code - 1) + g * 256 + (k * 2 + r) * 2048 + sub * 65536 + relative * 262144
                    )

                return count + (code > 0).astype(jnp.int32)

            count = lax.fori_loop(0, NG * 2, scan, count)

        def fields(entry):
            return (
                lax.shift_right_logical(entry, 4) & 15,
                entry & 15,
                lax.shift_right_logical(entry, 8) & 7,
                lax.shift_right_logical(entry, 11) & 15,
                lax.shift_right_logical(entry, 16) & 3,
                lax.shift_right_logical(entry, 18) & 3,
            )

        def psi_copy(ref, g, sub, at):
            start = pl.multiple_of(sub * WIDTH, WIDTH)
            return pltpu.make_async_copy(ref.at[g, pl.ds(start, WIDTH)], psi_buf.at[at], sems.at[at, 0])

        def left_copy(g, i, at):
            return pltpu.make_async_copy(left.at[g, :, i], left_buf.at[at], sems.at[at, 1])

        def fetch(n):
            i, j, g, s, sub, relative = fields(listed[n])
            at = lax.rem(n, DEPTH)
            left_copy(g, i, at).start()

            @pl.when(relative == 0)
            def _():
                psi_copy(own, g, sub, at).start()

            @pl.when(relative == 1)
            def _():
                psi_copy(above, g, sub, at).start()

            @pl.when(relative == 3)
            def _():
                psi_copy(below, g, sub, at).start()

            @pl.when((relative == 2) & (g < 4))
            def _():
                psi_copy(far_low, g, sub, at).start()

            @pl.when((relative == 2) & (g >= 4))
            def _():
                psi_copy(far_high, g - 4, sub, at).start()

            k = lax.shift_right_logical(s, 1)
            first = 0
            for n_delta, parts in enumerate(split):
                refs = right_refs[first : first + parts]
                first += parts

                @pl.when(k == n_delta)
                def _():
                    share = TERMS // parts
                    for p, ref in enumerate(refs):
                        pltpu.make_async_copy(
                            ref.at[:, j], right_buf.at[at, pl.ds(p * share, share)], sems.at[at, 2 + p]
                        ).start()

        def arrive(at):
            psi_copy(own, 0, 0, at).wait()
            left_copy(0, 0, at).wait()
            share = TERMS // split[0]
            for p in range(split[0]):
                pltpu.make_async_copy(
                    right_refs[p].at[:, 0], right_buf.at[at, pl.ds(p * share, share)], sems.at[at, 2 + p]
                ).wait()

        def begin(n, carry):
            fetch(n)
            return carry

        lax.fori_loop(0, jnp.minimum(count, 2 * BATCH), begin, 0)
        if carried is not None:
            for g in range(NG):
                out[g, :, rows_own:] = earlier[g]

        def step(m, carry):
            for q in range(BATCH):
                n = (m + 2) * BATCH + q

                @pl.when(n < count)
                def _():
                    fetch(n)

            for q in range(BATCH):
                n = m * BATCH + q

                @pl.when(n < count)
                def _():
                    arrive(lax.rem(n, DEPTH))

            results = []
            for q in range(BATCH):
                n = jnp.minimum(m * BATCH + q, count - 1)
                at = lax.rem(n, DEPTH)
                i, j, g, s, sub, relative = fields(listed[n])
                terms = lax.dot_general(
                    left_buf[at].reshape(TERMS * WIDTH, WIDTH),
                    psi_buf[at],
                    (((1,), (0,)), ((), ())),
                    preferred_element_type=jnp.float32,
                ).astype(jnp.bfloat16)
                total = None
                for a in range(0, TERMS, 2):
                    lhs = jnp.concatenate(
                        [terms[a * WIDTH : (a + 1) * WIDTH], terms[(a + 1) * WIDTH : (a + 2) * WIDTH]], axis=1
                    )
                    rhs = jnp.concatenate([right_buf[at, a], right_buf[at, a + 1]], axis=1)
                    part = lax.dot_general(
                        lhs, rhs, (((1,), (1,)), ((), ())), preferred_element_type=jnp.float32
                    )
                    total = part if total is None else total + part
                peak = jnp.max(jnp.max(jnp.abs(total), axis=0, keepdims=True), axis=1, keepdims=True)
                exponent = jnp.clip(jnp.floor(jnp.log2(peak)), -100.0, 127.0)
                code = jnp.round(total * jnp.exp2(CODE_BITS - exponent)).astype(jnp.int32).astype(jnp.int16)
                results.append((g, s, code, exponent))
            for g, s, code, exponent in results:
                start = pl.multiple_of(s * ROWS, ROWS)
                for y in range(NY):
                    out[g, y, pl.ds(start, ROWS)] = code[y * ROWS : (y + 1) * ROWS]
                heads[g, pl.ds(s, 1)] = jnp.broadcast_to(exponent, (1, WIDTH)).astype(jnp.int32)
            return carry

        lax.fori_loop(0, (count + BATCH - 1) // BATCH, step, 0)
        for y in range(NY):
            out[:, y, slots * ROWS : rows_own] = heads[...].astype(jnp.int16)

    flat = [part for r in rights for part in r]
    return pl.pallas_call(
        kernel,
        in_specs=[smem(), smem()]
        + [anywhere()] * (len(pieces) + 1 + len(flat))
        + ([] if carried is None else [vmem()]),
        out_specs=vmem(),
        out_shape=jax.ShapeDtypeStruct((NG, NY, rows_out, WIDTH), jnp.int16),
        scratch_shapes=[
            pltpu.SMEM((most,), jnp.int32),
            pltpu.VMEM((DEPTH, WIDTH, WIDTH), jnp.bfloat16),
            pltpu.VMEM((DEPTH, TERMS, WIDTH, WIDTH), jnp.bfloat16),
            pltpu.VMEM((DEPTH, TERMS, WIDTH, WIDTH), jnp.bfloat16),
            pltpu.VMEM((NG, HEAD, WIDTH), jnp.int32),
            pltpu.SemaphoreType.DMA((DEPTH, 4)),
        ],
        compiler_params=pltpu.CompilerParams(vmem_limit_bytes=VMEM),
        cost_estimate=pl.CostEstimate(
            flops=most * 16 * TERMS * 2 * WIDTH**3, bytes_accessed=most * 2**20, transcendentals=0
        ),
        name="contract",
    )(place, meta, *pieces, left_all, *flat, *([] if carried is None else [carried]))


def first_rows(chunks):
    origins = [0]
    for deltas in chunks:
        origins.append(origins[-1] + len(deltas) * 2 * ROWS + HEAD)
    return origins


def decode_kernel(chunks, last, place, route, rlim, clim, psi, vectors, *rest):
    returned, rest = rest[0], rest[1:]
    before, rest = (rest[0], rest[1:]) if last else (None, rest)
    (sigma32, result), scales = rest[:2], rest[2:]
    first_row = place[2] * ROWS
    rows = lax.broadcasted_iota(jnp.int32, (ROWS, WIDTH), 0) + first_row
    cols = lax.broadcasted_iota(jnp.int32, (ROWS, WIDTH), 1)
    origins = first_rows(chunks)
    for n, deltas in enumerate(chunks):
        top = origins[n] + len(deltas) * 2 * ROWS
        head = returned[:, top : top + HEAD].astype(jnp.int32).astype(jnp.float32)
        scales[n][...] = jnp.exp2(head - CODE_BITS)
    if last:
        result[...] = before[...]
    else:
        result[...] = jnp.zeros_like(result)

    def one(b, carry):
        slot = route[b]
        group = lax.shift_right_logical(slot, 4)
        delta = lax.shift_right_logical(slot, 1) & 7
        rank = slot & 1
        live = (rows < rlim[b]) & (cols < clim[b])
        amp = jnp.where(live, psi[b].astype(jnp.float32), 0.0)
        if not last:
            result[1] += amp * amp
        for n, deltas in enumerate(chunks):
            here = delta == deltas[0]
            place_in = jnp.int32(0)
            for k, d in enumerate(deltas[1:]):
                here = here | (delta == d)
                place_in = jnp.where(delta == d, k + 1, place_in)

            @pl.when(here)
            def _():
                s = place_in * 2 + rank
                start = pl.multiple_of(origins[n] + s * ROWS, HEAD)
                total = None
                for y in range(NY):
                    code = returned[group * NY + y, pl.ds(start, ROWS)]
                    part = code.astype(jnp.int32).astype(jnp.float32) * scales[n][group * NY + y, pl.ds(s, 1)]
                    total = part if total is None else total + part
                value = jnp.where(live, total, 0.0)
                sigma32[b] = value
                result[0] += amp * value
                result[2] += vectors[0, b].astype(jnp.float32) * value
                result[3] += vectors[1, b].astype(jnp.float32) * value

        return carry

    lax.fori_loop(0, BLOCKS, one, 0)


def spread_kernel(sums, spread):
    lane = lax.broadcasted_iota(jnp.int32, (1, WIDTH), 1)
    line = jnp.zeros((1, WIDTH), jnp.float32)
    for n in range(4):
        column = jnp.sum(sums[n], axis=0, keepdims=True)
        line = jnp.where(lane == n, jnp.sum(column, axis=1, keepdims=True), line)
    spread[...] = jnp.broadcast_to(line, (DEVICES, WIDTH))


def decode(chunks, place, route, rlim, clim, psi, vectors, returned, before=None):
    def whole(shape):
        return pl.BlockSpec(shape, lambda i, *_: (0,) * len(shape))

    part = (BLOCKS, ROWS, WIDTH)
    last = before is not None
    sums = (4, ROWS, WIDTH)

    def kernel(*refs):
        if not last:
            decode_kernel(chunks, last, *refs)
            return
        tail = len(chunks) + 1
        decode_kernel(chunks, last, *refs[: -tail - 1], refs[-1], *refs[-tail:-1])
        spread_kernel(refs[-1], refs[-tail - 1])

    return pl.pallas_call(
        kernel,
        grid_spec=pltpu.PrefetchScalarGridSpec(
            num_scalar_prefetch=4,
            grid=(1,),
            in_specs=[
                pl.BlockSpec(part, lambda i, place, *_: (0, place[2], 0)),
                pl.BlockSpec((2,) + part, lambda i, place, *_: (0, 0, place[2], 0)),
            ]
            + [whole(returned.shape)]
            + ([whole(sums)] if last else []),
            out_specs=[whole(part), whole((DEVICES, WIDTH)) if last else whole(sums)],
            scratch_shapes=[pltpu.VMEM((NG * NY, HEAD, WIDTH), jnp.float32) for _ in chunks]
            + ([pltpu.VMEM(sums, jnp.float32)] if last else []),
        ),
        out_shape=[
            jax.ShapeDtypeStruct(part, jnp.float32),
            jax.ShapeDtypeStruct((DEVICES, WIDTH) if last else sums, jnp.float32),
        ],
        compiler_params=pltpu.CompilerParams(vmem_limit_bytes=VMEM),
        cost_estimate=NOTHING,
        name="decode_last" if last else "decode",
    )(place, route, rlim, clim, psi, vectors, returned, *([before] if last else []))


def residual_kernel(place, route, rlim, clim, psi, near, distant, gathered, sigma16, out, products):
    first_row = place[2] * ROWS
    rows = lax.broadcasted_iota(jnp.int32, (ROWS, WIDTH), 0) + first_row
    cols = lax.broadcasted_iota(jnp.int32, (ROWS, WIDTH), 1)
    line = jnp.sum(gathered[...], axis=0, keepdims=True)
    lane = lax.broadcasted_iota(jnp.int32, (1, WIDTH), 1)
    cross = jnp.sum(jnp.where(lane == 0, line, 0.0), axis=1, keepdims=True)
    square = jnp.sum(jnp.where(lane == 1, line, 0.0), axis=1, keepdims=True)
    theta = jnp.broadcast_to(cross / square, (1, WIDTH))
    products[...] = line

    def one(b, carry):
        delta = lax.shift_right_logical(route[b], 1) & 7
        early = delta == NEAR[0]
        for d in NEAR[1:]:
            early = early | (delta == d)
        live = (rows < rlim[b]) & (cols < clim[b])
        amp = jnp.where(live, psi[b].astype(jnp.float32), 0.0)

        def emit(value):
            sigma16[b] = value.astype(jnp.bfloat16)
            out[b] = (value - theta * amp).astype(jnp.bfloat16)

        @pl.when(early)
        def _():
            emit(near[b])

        @pl.when(jnp.logical_not(early))
        def _():
            emit(distant[b])

        return carry

    lax.fori_loop(0, BLOCKS, one, 0)


def make_residual(place, route, rlim, clim, psi, near, distant, gathered):
    part = (BLOCKS, ROWS, WIDTH)

    def whole(shape):
        return pl.BlockSpec(shape, lambda i, *_: (0,) * len(shape))

    return pl.pallas_call(
        residual_kernel,
        grid_spec=pltpu.PrefetchScalarGridSpec(
            num_scalar_prefetch=4,
            grid=(1,),
            in_specs=[
                pl.BlockSpec(part, lambda i, place, *_: (0, place[2], 0)),
                whole(part),
                whole(part),
                whole((DEVICES, WIDTH)),
            ],
            out_specs=[whole(part), whole(part), whole((1, WIDTH))],
        ),
        out_shape=[
            jax.ShapeDtypeStruct(part, jnp.bfloat16),
            jax.ShapeDtypeStruct(part, jnp.bfloat16),
            jax.ShapeDtypeStruct((1, WIDTH), jnp.float32),
        ],
        compiler_params=pltpu.CompilerParams(vmem_limit_bytes=VMEM),
        cost_estimate=NOTHING,
        name="residual",
    )(place, route, rlim, clim, psi, near, distant, gathered)


def after(x, *others):
    return lax.optimization_barrier((x,) + others)[0]


def body(
    wavefunction,
    vectors,
    left_env,
    right_env,
    left_pattern,
    right_pattern,
    block_left,
    block_right,
    left_dims,
    right_dims,
):
    sec = lax.axis_index("sec").astype(jnp.int32)
    op = lax.axis_index("op").astype(jnp.int32)
    place = jnp.stack([sec, (sec // NC) % NZ, op]).astype(jnp.int32)

    right_table = right_env * right_pattern[:, :, None, None].astype(jnp.bfloat16)
    left_env = after(left_env, right_table)
    left_table = left_env * left_pattern[:, :, None, None].astype(jnp.bfloat16)
    rights = {0: (right_table,)}

    def ring(up, down):
        return lax.ppermute(up, "sec", RING_UP), lax.ppermute(down, "sec", RING_DOWN)

    up, down = ring(right_table, right_table)
    left_all = lax.all_gather(left_table, "sec", axis_index_groups=GROUP_XC)
    send, route, rlim, clim = pack(place, block_left, block_right, left_dims, right_dims, wavefunction)
    own = lax.all_to_all(send, "sec", 0, 0, axis_index_groups=GROUP_XC)
    below = lax.ppermute(own, "op", OP_UP)
    above = lax.ppermute(own, "op", OP_DOWN)
    up, down = after(up, own), after(down, own)
    rights[7], rights[1] = (up,), (down,)

    up, down = ring(up, down)
    far_low = lax.ppermute(below[:4], "op", OP_UP)
    far_high = lax.ppermute(above[4:], "op", OP_DOWN)
    up, down = after(up, far_low, far_high), after(down, far_low, far_high)
    rights[6], rights[2] = (up,), (down,)
    pieces = (own, below, above, far_low, far_high)
    heads = [p[:, PIECE : PIECE + 4, 0] for p in (own, above, jnp.concatenate([far_low, far_high]), below)]
    meta = jnp.stack(heads).astype(jnp.int32).reshape(-1)

    up, down = ring(up, down)

    def give_back(coded):
        coded = coded.reshape((NG * NY,) + coded.shape[2:])
        return lax.all_to_all(coded, ("sec", "op"), 0, 0, axis_index_groups=GROUP_XCY)

    near_codes = contract(NEAR, place, meta, pieces, left_all, [rights[d] for d in NEAR])
    rights[5], rights[3] = (up,), (down,)
    up, down = after(up, near_codes), after(down, near_codes)
    rights[4] = ring(up[:2], down[2:])
    near, sums = decode(
        (NEAR,), place, route, rlim, clim, wavefunction, vectors, give_back(near_codes)
    )
    middle_codes = contract(MIDDLE, place, meta, pieces, left_all, [rights[d] for d in MIDDLE])
    codes = contract(
        FAR, place, after(meta, sums), pieces, left_all, [rights[d] for d in FAR], middle_codes
    )
    distant, spread = decode(
        (FAR, MIDDLE), place, route, rlim, clim, wavefunction, vectors, give_back(codes), sums
    )
    gathered = lax.all_to_all(spread, ("sec", "op"), 0, 0, tiled=True)
    sigma16, residual, products = make_residual(
        place, route, rlim, clim, wavefunction, near, distant, gathered
    )
    return (sigma16, residual, products[0, 2:4])


def solution(mesh):
    placed = (
        P("sec", None, None),
        P(None, "sec", None, None),
        P("op", "sec", None, None),
        P("op", "sec", None, None),
        P("op", "sec"),
        P("op", "sec"),
        P("sec"),
        P(),
        P("sec"),
        P(),
    )
    return jax.shard_map(
        body,
        mesh=mesh,
        in_specs=placed,
        out_specs=(P("sec", "op", None), P("sec", "op", None), P()),
        check_vma=False,
    )
```

time: 842 us -> 266 us (0.32)
  waiting for transfers between devices: 576 us -> 78.3 us
  matrix products: 60.6 us -> 0 us
  local copies, waits for them, and re-layouts: 71.1 us -> 13 us
  Pallas kernels: 0 us -> 40.8 us
  other arithmetic: 20.1 us -> 6.28 us
    all_to_all x2 -> x1, waiting for transfers between devices: 530 us -> 4.17 us  [give_back(): lax.all_to_all(coded, ('sec', 'op'), 0, 0, axis_index_groups=GROUP_XCY)]
    all_to_all x0 -> x3, blocking collectives: none -> 82.8 us  [the longest x1 33 us: give_back(): lax.all_to_all(coded, ('sec', 'op'), 0, 0, axis_index_groups=GROUP_XCY)]
    psum x1 -> x0, blocking collectives: 75.9 us -> none  [body(): lax.psum((partial_sums[0], partial_sums[1], partial_sums[2]), ('sec', 'op'))]
    ppermute x0 -> x12, waiting for transfers between devices: none -> 74.1 us  [the longest x1 22.2 us: body(): above = lax.ppermute(own, 'op', OP_DOWN)]
    dot_general x6 -> x0, matrix products: 60.6 us -> none  [the longest x4 46.3 us: add_term(): jnp.einsum('sik,slk->sil', piece, chosen, preferred_element_type=jnp.floa...]
    reduce_scatter x1 -> x0, waiting for transfers between devices: 45.8 us -> none  [body(): sigma_part = lax.psum_scatter(masked, 'op', scatter_dimension=1, tiled=True)]
    pallas_call x0 -> x7, Pallas kernels: none -> 40.8 us  [the longest x3 26.1 us: contract(): pl.pallas_call(kernel, in_specs=[smem(), smem()] + [anywhere()] * (len(pi...]
    scatter x2 -> x0, local copies, waits for them, and re-layouts: 37.6 us -> none  [the longest x1 22.1 us: body(): jnp.zeros((slot_count,) + left_terms.shape[1:], jnp.bfloat16).at[send_slot]]
  transfers between devices with their start and end apart: 3 -> 14, of which waited for: 3 -> 10; matrix products, arithmetic and copies ran while one was open for 2% -> 4% of each run, Pallas kernels for 0% -> 11%
where the time goes in v2:
time: 266 us; the launch traced here: 264 us
  blocking collectives  82.8 us (31%)
  waiting for transfers between devices  78.3 us (29%)
  Pallas kernels  40.8 us (15%)
  starting transfers between devices  28.4 us (11%)
  between operations  14.2 us (5%)
  local copies, waits for them, and re-layouts  13 us (5%)
  other arithmetic  6.28 us (2%)
    all_to_all x1, blocking collectives, give_back(): lax.all_to_all(coded, ('sec', 'op'), 0, 0, axis_index_groups=GROUP_XCY)  33 us
    pallas_call x3, Pallas kernels, contract(): pl.pallas_call(kernel, in_specs=[smem(), smem()] + [anywhere()] * (len(pi...  26.1 us
    all_to_all x1, blocking collectives, body(): own = lax.all_to_all(send, 'sec', 0, 0, axis_index_groups=GROUP_XC)  26 us
    all_to_all x1, blocking collectives, body(): gathered = lax.all_to_all(spread, ('sec', 'op'), 0, 0, tiled=True)  23.9 us
    ppermute x1, waiting for transfers between devices, body(): above = lax.ppermute(own, 'op', OP_DOWN)  22.2 us
    ppermute x4, waiting for transfers between devices, ring(): lax.ppermute(up, 'sec', RING_UP)  22.1 us
    ppermute x4, waiting for transfers between devices, ring(): lax.ppermute(down, 'sec', RING_DOWN)  18 us
    ppermute x4, starting transfers between devices, ring(): lax.ppermute(down, 'sec', RING_DOWN)  11.1 us
  transfers between devices with their start and end apart: 14, of which 10 were waited for; matrix products, arithmetic and copies ran while one was open for 4% of the time, Pallas kernels for 11%

profile of v2, /device:TPU:32, one launch (start us, length us, event | category | flops | bytes accessed | tf_op | source)
XLA Modules:
  0.0 263.7 jit_solution(613778473358791039)
XLA Ops:
  7.9 3.3 %broadcast_multiply_fusion.1.rest_0_ = bf16[4,16,128,128]{3,2,1,0:T(8,128)(2,1)} fusion(bf16[4,16,128,128]{3,2,1,0:T(8,128)(2,1)} %param.13, bf16[4,16]{1,0:T(4,128)(2,1)S(1)} %convert_element_type.17), kind=kLoop, calls=%fused_computation.1 | loop fusion | flops 1048576 | bytes 4194432 | tf_op jit(solution)/shard_map/mul | solution.py:504
  15.0 3.4 %pack.1 = (bf16[8,528,128]{2,1,0:T(8,128)(2,1)S(1)}, s32[64]{0:T(128)S(1)}, s32[64]{0:T(128)S(1)}, s32[64]{0:T(128)S(1)}) custom-call(s32[3]{0:T(128)S(1)} %pad_add_fusion.place.refs_0_, s32[64]{0:T(128)S(1)} %copy-done.11, s32[4096]{0:T(1024)S(1)} %copy-done.9, s32[16]{0:T(128)S(1)} %copy-done.12, s32[1024]{0:T(1024)S(1)} %copy-done.10, ...), custom_call_target="tpu_custom_call" | custom-call | flops 1024 | bytes 1024 | tf_op jit(solution)/shard_map/pack/pallas_call | solution.py:104
  18.3 26.0 %all_to_all.26.own = bf16[8,528,128]{2,1,0:T(8,128)(2,1)S(1)} all-to-all(bf16[8,528,128]{2,1,0:T(8,128)(2,1)S(1)} %get-tuple-element.25), channel_id=1, replica_groups={{0,4,64,68,128,132,192,196},{8,12,72,76,136,140,200,204},{16,20,80,84,1..., dimensions={0} | all-to-all | bytes 2162688 | tf_op jit(solution)/shard_map/all_to_all | solution.py:515
  44.3 16.4 %collective-permute-done.4.rest_1_ = bf16[4,16,128,128]{3,2,1,0:T(8,128)(2,1)} collective-permute-done((bf16[4,16,128,128]{3,2,1,0:T(8,128)(2,1)}, bf16[4,16,128,128]{3,2,1,0:T(8,128)(2,1)}, u32[]{:S(2)}, u32[]{:S(2)}) %collective-permute-start.4) | collective-permute-done | bytes 2097184 | tf_op jit(solution)/shard_map/ppermute | solution.py:510
  60.7 3.3 %collective-permute-start.6 = (bf16[4,16,128,128]{3,2,1,0:T(8,128)(2,1)}, bf16[4,16,128,128]{3,2,1,0:T(8,128)(2,1)}, u32[]{:S(2)}, u32[]{:S(2)}) collective-permute-start(bf16[4,16,128,128]{3,2,1,0:T(8,128)(2,1)} %collective-permute-done.4.rest_1_), channel_id=1, source_target_pairs={{8,0},{12,4},{16,8},{20,12},{24,16},{28,20},{32,24},{36,28},{40,32... | collective-permute-start | bytes 6291464 | tf_op jit(solution)/shard_map/ppermute | solution.py:510
  64.5 3.0 %collective-permute-start = (bf16[8,528,128]{2,1,0:T(8,128)(2,1)S(1)}, bf16[8,528,128]{2,1,0:T(8,128)(2,1)S(1)}, u32[]{:S(2)}, u32[]{:S(2)}) collective-permute-start(bf16[8,528,128]{2,1,0:T(8,128)(2,1)S(1)} %all_to_all.26.own), channel_id=1, source_target_pairs={{1,0},{2,1},{3,2},{0,3},{5,4},{6,5},{7,6},{4,7},{9,8},{10,9},{11,1... | collective-permute-start | bytes 3244040 | tf_op jit(solution)/shard_map/ppermute | solution.py:517
  67.5 22.2 %collective-permute-done.above = bf16[8,528,128]{2,1,0:T(8,128)(2,1)S(1)} collective-permute-done((bf16[8,528,128]{2,1,0:T(8,128)(2,1)S(1)}, bf16[8,528,128]{2,1,0:T(8,128)(2,1)S(1)}, u32[]{:S(2)}, u32[]{:S(2)}) %collective-permute-start) | collective-permute-done | bytes 1081376 | tf_op jit(solution)/shard_map/ppermute | solution.py:517
  90.6 3.7 %collective-permute-start.3 = (bf16[4,528,128]{2,1,0:T(8,128)(2,1)}, bf16[4,528,128]{2,1,0:T(8,128)(2,1)}, u32[]{:S(2)}, u32[]{:S(2)}) collective-permute-start(bf16[4,528,128]{2,1,0:T(8,128)(2,1)} %slice.39), channel_id=1, source_target_pairs={{1,0},{2,1},{3,2},{0,3},{5,4},{6,5},{7,6},{4,7},{9,8},{10,9},{11,1... | collective-permute-start | bytes 1622024 | tf_op jit(solution)/shard_map/ppermute | solution.py:523
  97.3 7.2 %collective-permute-done.3.far_high = bf16[4,528,128]{2,1,0:T(8,128)(2,1)} collective-permute-done((bf16[4,528,128]{2,1,0:T(8,128)(2,1)}, bf16[4,528,128]{2,1,0:T(8,128)(2,1)}, u32[]{:S(2)}, u32[]{:S(2)}) %collective-permute-start.3) | collective-permute-done | bytes 540704 | tf_op jit(solution)/shard_map/ppermute | solution.py:523
  104.5 4.6 %collective-permute-done.2.far_low = bf16[4,528,128]{2,1,0:T(8,128)(2,1)} collective-permute-done((bf16[4,528,128]{2,1,0:T(8,128)(2,1)}, bf16[4,528,128]{2,1,0:T(8,128)(2,1)}, u32[]{:S(2)}, u32[]{:S(2)}) %collective-permute-start.2) | collective-permute-done | bytes 540704 | tf_op jit(solution)/shard_map/ppermute | solution.py:522
  112.5 3.0 %collective-permute-start.10 = (bf16[4,16,128,128]{3,2,1,0:T(8,128)(2,1)}, bf16[4,16,128,128]{3,2,1,0:T(8,128)(2,1)}, u32[]{:S(2)}, u32[]{:S(2)}) collective-permute-start(bf16[4,16,128,128]{3,2,1,0:T(8,128)(2,1)} %collective-permute-done.6.rest_3_), channel_id=1, source_target_pairs={{8,0},{12,4},{16,8},{20,12},{24,16},{28,20},{32,24},{36,28},{40,32... | collective-permute-start | bytes 6291464 | tf_op jit(solution)/shard_map/ppermute | solution.py:510
  117.9 14.3 %contract.3 = s16[8,4,336,128]{3,2,1,0:T(8,128)(2,1)} custom-call(s32[3]{0:T(128)S(1)} %pad_add_fusion.place.refs_0_, s32[128]{0:T(128)S(1)} %reshape.24.meta, bf16[8,528,128]{2,1,0:T(8,128)(2,1)S(1)} %all_to_all.26.own, bf16[8,528,128]{2,1,0:T(8,128)(2,1)S(1)} %copy-done.5, bf16[8,528,128]{2,1,0:T(8,128)(2,1)S(1)} %copy-done.2, ...), custom_call_target="tpu_custom_call" | custom-call | flops 21474836480 | bytes 83886080 | tf_op jit(solution)/shard_map/contract/pallas_call | solution.py:285
  132.3 10.3 %all-to-all-start.1 = ((s16[32,336,128]{2,1,0:T(8,128)(2,1)}), s16[32,336,128]{2,1,0:T(8,128)(2,1)}, u32[]{:S(2)}, u32[]{:S(2)}) async-start(s16[32,336,128]{2,1,0:T(8,128)(2,1)} %bitcast.22), calls=%async_computation.1 | async-start | bytes 5505024 | tf_op jit(solution)/shard_map/all_to_all | solution.py:534
  142.6 16.7 %collective-permute-done.8.rest_1_ = bf16[4,16,128,128]{3,2,1,0:T(8,128)(2,1)} collective-permute-done((bf16[4,16,128,128]{3,2,1,0:T(8,128)(2,1)}, bf16[4,16,128,128]{3,2,1,0:T(8,128)(2,1)}, u32[]{:S(2)}, u32[]{:S(2)}) %collective-permute-start.8) | collective-permute-done | bytes 2097184 | tf_op jit(solution)/shard_map/ppermute | solution.py:510
  164.0 3.0 %collective-permute-start.11 = (bf16[2,16,128,128]{3,2,1,0:T(8,128)(2,1)}, bf16[2,16,128,128]{3,2,1,0:T(8,128)(2,1)}, u32[]{:S(2)}, u32[]{:S(2)}) collective-permute-start(bf16[2,16,128,128]{3,2,1,0:T(8,128)(2,1)} %slice.34), channel_id=1, source_target_pairs={{8,0},{12,4},{16,8},{20,12},{24,16},{28,20},{32,24},{36,28},{40,32... | collective-permute-start | bytes 3145736 | tf_op jit(solution)/shard_map/ppermute | solution.py:510
  166.9 5.7 %contract.4.rest_2_ = s16[8,4,144,128]{3,2,1,0:T(8,128)(2,1)S(1)} custom-call(s32[3]{0:T(128)S(1)} %pad_add_fusion.place.refs_0_, s32[128]{0:T(128)S(1)} %reshape.24.meta, bf16[8,528,128]{2,1,0:T(8,128)(2,1)S(1)} %all_to_all.26.own, bf16[8,528,128]{2,1,0:T(8,128)(2,1)S(1)} %copy-done.6, bf16[8,528,128]{2,1,0:T(8,128)(2,1)S(1)} %copy-done.3, ...), custom_call_target="tpu_custom_call" | custom-call | flops 8589934592 | bytes 33554432 | tf_op jit(solution)/shard_map/contract/pallas_call | solution.py:285
  173.7 4.2 %all-to-all-done.1.refs_6_ = s16[32,336,128]{2,1,0:T(8,128)(2,1)} async-done(((s16[32,336,128]{2,1,0:T(8,128)(2,1)}), s16[32,336,128]{2,1,0:T(8,128)(2,1)}, u32[]{:S(2)}, u32[]{:S(2)}) %all-to-all-start.1) | async-done | bytes 2752544 | tf_op jit(solution)/shard_map/all_to_all | solution.py:534
  177.9 4.5 %decode.1 = (f32[64,32,128]{2,1,0:T(8,128)S(1)}, f32[4,32,128]{2,1,0:T(8,128)S(1)}) custom-call(s32[3]{0:T(128)S(1)} %pad_add_fusion.place.refs_0_, s32[64]{0:T(128)S(1)} %get-tuple-element.22.refs_1_.route, s32[64]{0:T(128)S(1)} %get-tuple-element.23.refs_2_.rlim, s32[64]{0:T(128)S(1)} %get-tuple-element.24.refs_3_.clim, bf16[64,128,128]{2,1,0:T(8,128)(2,1)S(1)} %copy-done, ...), custom_call_target="tpu_custom_call" | custom-call | flops 1024 | bytes 1024 | tf_op jit(solution)/shard_map/decode/pallas_call | solution.py:393
  182.5 2.6 collective-permute-done.9.rest_0_
  186.7 6.0 %contract.5 = s16[8,4,224,128]{3,2,1,0:T(8,128)(2,1)} custom-call(s32[3]{0:T(128)S(1)} %pad_add_fusion.place.refs_0_, s32[128]{0:T(128)S(1)} %reshape.24.meta, bf16[8,528,128]{2,1,0:T(8,128)(2,1)S(1)} %all_to_all.26.own, bf16[8,528,128]{2,1,0:T(8,128)(2,1)S(1)} %copy-done.7, bf16[8,528,128]{2,1,0:T(8,128)(2,1)} %copy-done.1, ...), custom_call_target="tpu_custom_call" | custom-call | flops 4294967296 | bytes 16777216 | tf_op jit(solution)/shard_map/contract/pallas_call | solution.py:285
  192.7 33.0 %all_to_all.27.refs_6_ = s16[32,224,128]{2,1,0:T(8,128)(2,1)S(1)} all-to-all(s16[32,224,128]{2,1,0:T(8,128)(2,1)} %bitcast.21), channel_id=1, replica_groups={{0,1,2,3,4,5,6,7,64,65,66,67,68,69,70,71,128,129,130,131,132,133,134,13..., dimensions={0} | all-to-all | bytes 3670016 | tf_op jit(solution)/shard_map/all_to_all | solution.py:534
  225.7 3.7 %decode_last.1 = (f32[64,32,128]{2,1,0:T(8,128)S(1)}, f32[256,128]{1,0:T(8,128)S(1)}) custom-call(s32[3]{0:T(128)S(1)} %pad_add_fusion.place.refs_0_, s32[64]{0:T(128)S(1)} %get-tuple-element.22.refs_1_.route, s32[64]{0:T(128)S(1)} %get-tuple-element.23.refs_2_.rlim, s32[64]{0:T(128)S(1)} %get-tuple-element.24.refs_3_.clim, ...), custom_call_target="tpu_custom_call" | custom-call | flops 1024 | bytes 1024 | tf_op jit(solution)/shard_map/decode_last/pallas_call | solution.py:393
  229.4 23.9 %all_to_all.28 = f32[256,1,128]{2,1,0:T(1,128)S(1)} all-to-all(f32[256,1,128]{2,1,0:T(1,128)S(1)} %bitcast.17), channel_id=1, replica_groups=mesh['sec'=64,'op'=4] {'sec','op'}, dimensions={0} | all-to-all | bytes 262144 | tf_op jit(solution)/shard_map/all_to_all | solution.py:550
  253.2 3.1 %residual.1 = (bf16[64,32,128]{2,1,0:T(8,128)(2,1)}, bf16[64,32,128]{2,1,0:T(8,128)(2,1)}, f32[1,128]{1,0:T(1,128)S(1)}) custom-call(s32[3]{0:T(128)S(1)} %pad_add_fusion.place.refs_0_, s32[64]{0:T(128)S(1)} %get-tuple-element.22.refs_1_.route, s32[64]{0:T(128)S(1)} %get-tuple-element.23.refs_2_.rlim, s32[64]{0:T(128)S(1)} %get-tuple-element.24.refs_3_.clim, ...), custom_call_target="tpu_custom_call" | custom-call | flops 1024 | bytes 1024 | tf_op jit(solution)/shard_map/residual/pallas_call | solution.py:460
  (66 shorter events, 22.6 us)
Async XLA Ops:
  7.2 108.3 %all-gather.3.cloned.1.call-start = ((), (), s32[]{:S(2)}) async-start(), calls=%async_computation.4 | async-start | bytes 18874368 | tf_op jit(solution)/shard_map/all_gather | solution.py:513
  7.9 3.3 %copy-start.14 = (s32[4,16]{1,0:T(4,128)S(1)}, s32[4,16]{1,0:T(4,128)}, u32[]{:S(2)}) copy-start(s32[4,16]{1,0:T(4,128)} %param.14) | copy-start | bytes 772
  7.9 3.3 %copy-start.13 = (bf16[4,16,128,128]{3,2,1,0:T(8,128)(2,1)S(1)}, bf16[4,16,128,128]{3,2,1,0:T(8,128)(2,1)}, u32[]{:S(2)}) copy-start(bf16[4,16,128,128]{3,2,1,0:T(8,128)(2,1)} %param.12) | copy-start | bytes 6291460
  12.7 2.2 copy-start.9
  12.7 2.2 copy-start.10
  12.7 2.2 copy-start.11
  12.7 2.2 copy-start.12
  12.7 47.9 %collective-permute-start.4 = (bf16[4,16,128,128]{3,2,1,0:T(8,128)(2,1)}, bf16[4,16,128,128]{3,2,1,0:T(8,128)(2,1)}, u32[]{:S(2)}, u32[]{:S(2)}) collective-permute-start(bf16[4,16,128,128]{3,2,1,0:T(8,128)(2,1)} %broadcast_multiply_fusion.1.rest_0_), channel_id=1, source_target_pairs={{8,0},{12,4},{16,8},{20,12},{24,16},{28,20},{32,24},{36,28},{40,32... | collective-permute-start | bytes 6291464 | tf_op jit(solution)/shard_map/ppermute | solution.py:510
  14.7 49.8 %collective-permute-start.5 = (bf16[4,16,128,128]{3,2,1,0:T(8,128)(2,1)}, bf16[4,16,128,128]{3,2,1,0:T(8,128)(2,1)}, u32[]{:S(2)}, u32[]{:S(2)}) collective-permute-start(bf16[4,16,128,128]{3,2,1,0:T(8,128)(2,1)} %broadcast_multiply_fusion.1.rest_0_), channel_id=1, source_target_pairs={{0,8},{4,12},{8,16},{12,20},{16,24},{20,28},{24,32},{28,36},{32,40... | collective-permute-start | bytes 6291464 | tf_op jit(solution)/shard_map/ppermute | solution.py:510
  60.7 49.5 %collective-permute-start.6 = (bf16[4,16,128,128]{3,2,1,0:T(8,128)(2,1)}, bf16[4,16,128,128]{3,2,1,0:T(8,128)(2,1)}, u32[]{:S(2)}, u32[]{:S(2)}) collective-permute-start(bf16[4,16,128,128]{3,2,1,0:T(8,128)(2,1)} %collective-permute-done.4.rest_1_), channel_id=1, source_target_pairs={{8,0},{12,4},{16,8},{20,12},{24,16},{28,20},{32,24},{36,28},{40,32... | collective-permute-start | bytes 6291464 | tf_op jit(solution)/shard_map/ppermute | solution.py:510
  64.5 48.0 %collective-permute-start.7 = (bf16[4,16,128,128]{3,2,1,0:T(8,128)(2,1)}, bf16[4,16,128,128]{3,2,1,0:T(8,128)(2,1)}, u32[]{:S(2)}, u32[]{:S(2)}) collective-permute-start(bf16[4,16,128,128]{3,2,1,0:T(8,128)(2,1)} %collective-permute-done.5.rest_2_), channel_id=1, source_target_pairs={{0,8},{4,12},{8,16},{12,20},{16,24},{20,28},{24,32},{28,36},{32,40... | collective-permute-start | bytes 6291464 | tf_op jit(solution)/shard_map/ppermute | solution.py:510
  64.5 25.3 %collective-permute-start = (bf16[8,528,128]{2,1,0:T(8,128)(2,1)S(1)}, bf16[8,528,128]{2,1,0:T(8,128)(2,1)S(1)}, u32[]{:S(2)}, u32[]{:S(2)}) collective-permute-start(bf16[8,528,128]{2,1,0:T(8,128)(2,1)S(1)} %all_to_all.26.own), channel_id=1, source_target_pairs={{1,0},{2,1},{3,2},{0,3},{5,4},{6,5},{7,6},{4,7},{9,8},{10,9},{11,1... | collective-permute-start | bytes 3244040 | tf_op jit(solution)/shard_map/ppermute | solution.py:517
  67.5 26.8 %collective-permute-start.1 = (bf16[8,528,128]{2,1,0:T(8,128)(2,1)S(1)}, bf16[8,528,128]{2,1,0:T(8,128)(2,1)S(1)}, u32[]{:S(2)}, u32[]{:S(2)}) collective-permute-start(bf16[8,528,128]{2,1,0:T(8,128)(2,1)S(1)} %all_to_all.26.own), channel_id=1, source_target_pairs={{0,1},{1,2},{2,3},{3,0},{4,5},{5,6},{6,7},{7,4},{8,9},{9,10},{10,1... | collective-permute-start | bytes 3244040 | tf_op jit(solution)/shard_map/ppermute | solution.py:516
  89.7 4.6 %copy-start.1 = (bf16[8,528,128]{2,1,0:T(8,128)(2,1)}, bf16[8,528,128]{2,1,0:T(8,128)(2,1)S(1)}, u32[]{:S(2)}) copy-start(bf16[8,528,128]{2,1,0:T(8,128)(2,1)S(1)} %collective-permute-done.above) | copy-start | bytes 3244036
  90.6 13.9 %collective-permute-start.3 = (bf16[4,528,128]{2,1,0:T(8,128)(2,1)}, bf16[4,528,128]{2,1,0:T(8,128)(2,1)}, u32[]{:S(2)}, u32[]{:S(2)}) collective-permute-start(bf16[4,528,128]{2,1,0:T(8,128)(2,1)} %slice.39), channel_id=1, source_target_pairs={{1,0},{2,1},{3,2},{0,3},{5,4},{6,5},{7,6},{4,7},{9,8},{10,9},{11,1... | collective-permute-start | bytes 1622024 | tf_op jit(solution)/shard_map/ppermute | solution.py:523
  95.5 13.6 %collective-permute-start.2 = (bf16[4,528,128]{2,1,0:T(8,128)(2,1)}, bf16[4,528,128]{2,1,0:T(8,128)(2,1)}, u32[]{:S(2)}, u32[]{:S(2)}) collective-permute-start(bf16[4,528,128]{2,1,0:T(8,128)(2,1)} %slice.38), channel_id=1, source_target_pairs={{0,1},{1,2},{2,3},{3,0},{4,5},{5,6},{6,7},{7,4},{8,9},{9,10},{10,1... | collective-permute-start | bytes 1622024 | tf_op jit(solution)/shard_map/ppermute | solution.py:522
  112.5 46.8 %collective-permute-start.8 = (bf16[4,16,128,128]{3,2,1,0:T(8,128)(2,1)}, bf16[4,16,128,128]{3,2,1,0:T(8,128)(2,1)}, u32[]{:S(2)}, u32[]{:S(2)}) collective-permute-start(bf16[4,16,128,128]{3,2,1,0:T(8,128)(2,1)} %collective-permute-done.7.rest_4_), channel_id=1, source_target_pairs={{0,8},{4,12},{8,16},{12,20},{16,24},{20,28},{24,32},{28,36},{32,40... | collective-permute-start | bytes 6291464 | tf_op jit(solution)/shard_map/ppermute | solution.py:510
  112.5 49.1 %collective-permute-start.10 = (bf16[4,16,128,128]{3,2,1,0:T(8,128)(2,1)}, bf16[4,16,128,128]{3,2,1,0:T(8,128)(2,1)}, u32[]{:S(2)}, u32[]{:S(2)}) collective-permute-start(bf16[4,16,128,128]{3,2,1,0:T(8,128)(2,1)} %collective-permute-done.6.rest_3_), channel_id=1, source_target_pairs={{8,0},{12,4},{16,8},{20,12},{24,16},{28,20},{32,24},{36,28},{40,32... | collective-permute-start | bytes 6291464 | tf_op jit(solution)/shard_map/ppermute | solution.py:510
  132.3 45.6 %all-to-all-start.1 = ((s16[32,336,128]{2,1,0:T(8,128)(2,1)}), s16[32,336,128]{2,1,0:T(8,128)(2,1)}, u32[]{:S(2)}, u32[]{:S(2)}) async-start(s16[32,336,128]{2,1,0:T(8,128)(2,1)} %bitcast.22), calls=%async_computation.1 | async-start | bytes 5505024 | tf_op jit(solution)/shard_map/all_to_all | solution.py:534
  142.6 24.4 %copy-start.3 = (bf16[8,528,128]{2,1,0:T(8,128)(2,1)S(1)}, bf16[8,528,128]{2,1,0:T(8,128)(2,1)}, u32[]{:S(2)}) copy-start(bf16[8,528,128]{2,1,0:T(8,128)(2,1)} %copy-done.1) | copy-start | bytes 3244036
  142.6 24.4 %copy-start.6 = (bf16[8,528,128]{2,1,0:T(8,128)(2,1)S(1)}, bf16[8,528,128]{2,1,0:T(8,128)(2,1)}, u32[]{:S(2)}) copy-start(bf16[8,528,128]{2,1,0:T(8,128)(2,1)} %copy-done.4) | copy-start | bytes 3244036
  161.6 23.4 %collective-permute-start.9 = (bf16[2,16,128,128]{3,2,1,0:T(8,128)(2,1)}, bf16[2,16,128,128]{3,2,1,0:T(8,128)(2,1)}, u32[]{:S(2)}, u32[]{:S(2)}) collective-permute-start(bf16[2,16,128,128]{3,2,1,0:T(8,128)(2,1)} %slice.33), channel_id=1, source_target_pairs={{0,8},{4,12},{8,16},{12,20},{16,24},{20,28},{24,32},{28,36},{32,40... | collective-permute-start | bytes 3145736 | tf_op jit(solution)/shard_map/ppermute | solution.py:510
  164.0 22.7 %collective-permute-start.11 = (bf16[2,16,128,128]{3,2,1,0:T(8,128)(2,1)}, bf16[2,16,128,128]{3,2,1,0:T(8,128)(2,1)}, u32[]{:S(2)}, u32[]{:S(2)}) collective-permute-start(bf16[2,16,128,128]{3,2,1,0:T(8,128)(2,1)} %slice.34), channel_id=1, source_target_pairs={{8,0},{12,4},{16,8},{20,12},{24,16},{28,20},{32,24},{36,28},{40,32... | collective-permute-start | bytes 3145736 | tf_op jit(solution)/shard_map/ppermute | solution.py:510
  177.9 8.8 %copy-start.7 = (bf16[8,528,128]{2,1,0:T(8,128)(2,1)S(1)}, bf16[8,528,128]{2,1,0:T(8,128)(2,1)}, u32[]{:S(2)}) copy-start(bf16[8,528,128]{2,1,0:T(8,128)(2,1)} %copy-done.4) | copy-start | bytes 3244036
  (5 other events, 6.9 us)
Sparse Core Ops, SparseCore 0:
  12.9 95.1 all-gather.2

commit v3 on v2

--- a/solution.py
+++ b/solution.py
@@ -16,6 +16,7 @@
 DEPTH = 3 * BATCH
 CODE_BITS = 13.0
 VMEM = 48 * 1024 * 1024
+VMEM_ALL = 61 * 1024 * 1024
 NOTHING = pl.CostEstimate(flops=1024, bytes_accessed=1024, transcendentals=0)
 
 
@@ -297,7 +298,7 @@
             pltpu.VMEM((NG, HEAD, WIDTH), jnp.int32),
             pltpu.SemaphoreType.DMA((DEPTH, 4)),
         ],
-        compiler_params=pltpu.CompilerParams(vmem_limit_bytes=VMEM),
+        compiler_params=pltpu.CompilerParams(vmem_limit_bytes=VMEM_ALL),
         cost_estimate=pl.CostEstimate(
             flops=most * 16 * TERMS * 2 * WIDTH**3, bytes_accessed=most * 2**20, transcendentals=0
         ),
@@ -312,9 +313,9 @@
     return origins
 
 
-def decode_kernel(chunks, last, place, route, rlim, clim, psi, vectors, *rest):
+def decode_kernel(chunks, later, place, route, rlim, clim, psi, vectors, *rest):
     returned, rest = rest[0], rest[1:]
-    before, rest = (rest[0], rest[1:]) if last else (None, rest)
+    before, rest = (rest[0], rest[1:]) if later else (None, rest)
     (sigma32, result), scales = rest[:2], rest[2:]
     first_row = place[2] * ROWS
     rows = lax.broadcasted_iota(jnp.int32, (ROWS, WIDTH), 0) + first_row
@@ -324,7 +325,7 @@
         top = origins[n] + len(deltas) * 2 * ROWS
         head = returned[:, top : top + HEAD].astype(jnp.int32).astype(jnp.float32)
         scales[n][...] = jnp.exp2(head - CODE_BITS)
-    if last:
+    if later:
         result[...] = before[...]
     else:
         result[...] = jnp.zeros_like(result)
@@ -336,7 +337,7 @@
         rank = slot & 1
         live = (rows < rlim[b]) & (cols < clim[b])
         amp = jnp.where(live, psi[b].astype(jnp.float32), 0.0)
-        if not last:
+        if not later:
             result[1] += amp * amp
         for n, deltas in enumerate(chunks):
             here = delta == deltas[0]
@@ -371,23 +372,23 @@
     for n in range(4):
         column = jnp.sum(sums[n], axis=0, keepdims=True)
         line = jnp.where(lane == n, jnp.sum(column, axis=1, keepdims=True), line)
-    spread[...] = jnp.broadcast_to(line, (DEVICES, WIDTH))
-
-
-def decode(chunks, place, route, rlim, clim, psi, vectors, returned, before=None):
+    spread[...] = jnp.broadcast_to(line[:, :8], (DEVICES, 8))
+
+
+def decode(chunks, place, route, rlim, clim, psi, vectors, returned, before=None, last=False):
     def whole(shape):
         return pl.BlockSpec(shape, lambda i, *_: (0,) * len(shape))
 
     part = (BLOCKS, ROWS, WIDTH)
-    last = before is not None
+    later = before is not None
     sums = (4, ROWS, WIDTH)
 
     def kernel(*refs):
         if not last:
-            decode_kernel(chunks, last, *refs)
+            decode_kernel(chunks, later, *refs)
             return
         tail = len(chunks) + 1
-        decode_kernel(chunks, last, *refs[: -tail - 1], refs[-1], *refs[-tail:-1])
+        decode_kernel(chunks, later, *refs[: -tail - 1], refs[-1], *refs[-tail:-1])
         spread_kernel(refs[-1], refs[-tail - 1])
 
     return pl.pallas_call(
@@ -400,27 +401,27 @@
                 pl.BlockSpec((2,) + part, lambda i, place, *_: (0, 0, place[2], 0)),
             ]
             + [whole(returned.shape)]
-            + ([whole(sums)] if last else []),
-            out_specs=[whole(part), whole((DEVICES, WIDTH)) if last else whole(sums)],
+            + ([whole(sums)] if later else []),
+            out_specs=[whole(part), whole((DEVICES, 8)) if last else whole(sums)],
             scratch_shapes=[pltpu.VMEM((NG * NY, HEAD, WIDTH), jnp.float32) for _ in chunks]
             + ([pltpu.VMEM(sums, jnp.float32)] if last else []),
         ),
         out_shape=[
             jax.ShapeDtypeStruct(part, jnp.float32),
-            jax.ShapeDtypeStruct((DEVICES, WIDTH) if last else sums, jnp.float32),
+            jax.ShapeDtypeStruct((DEVICES, 8) if last else sums, jnp.float32),
         ],
         compiler_params=pltpu.CompilerParams(vmem_limit_bytes=VMEM),
         cost_estimate=NOTHING,
         name="decode_last" if last else "decode",
-    )(place, route, rlim, clim, psi, vectors, returned, *([before] if last else []))
-
-
-def residual_kernel(place, route, rlim, clim, psi, near, distant, gathered, sigma16, out, products):
+    )(place, route, rlim, clim, psi, vectors, returned, *([before] if later else []))
+
+
+def residual_kernel(place, route, rlim, clim, psi, near, middle, far, gathered, sigma16, out, products):
     first_row = place[2] * ROWS
     rows = lax.broadcasted_iota(jnp.int32, (ROWS, WIDTH), 0) + first_row
     cols = lax.broadcasted_iota(jnp.int32, (ROWS, WIDTH), 1)
     line = jnp.sum(gathered[...], axis=0, keepdims=True)
-    lane = lax.broadcasted_iota(jnp.int32, (1, WIDTH), 1)
+    lane = lax.broadcasted_iota(jnp.int32, (1, 8), 1)
     cross = jnp.sum(jnp.where(lane == 0, line, 0.0), axis=1, keepdims=True)
     square = jnp.sum(jnp.where(lane == 1, line, 0.0), axis=1, keepdims=True)
     theta = jnp.broadcast_to(cross / square, (1, WIDTH))
@@ -428,9 +429,8 @@
 
     def one(b, carry):
         delta = lax.shift_right_logical(route[b], 1) & 7
-        early = delta == NEAR[0]
-        for d in NEAR[1:]:
-            early = early | (delta == d)
+        in_middle = (delta == MIDDLE[0]) | (delta == MIDDLE[1])
+        in_far = delta == FAR[0]
         live = (rows < rlim[b]) & (cols < clim[b])
         amp = jnp.where(live, psi[b].astype(jnp.float32), 0.0)
 
@@ -438,20 +438,24 @@
             sigma16[b] = value.astype(jnp.bfloat16)
             out[b] = (value - theta * amp).astype(jnp.bfloat16)
 
-        @pl.when(early)
+        @pl.when(in_far)
+        def _():
+            emit(far[b])
+
+        @pl.when(in_middle)
+        def _():
+            emit(middle[b])
+
+        @pl.when(jnp.logical_not(in_far | in_middle))
         def _():
             emit(near[b])
 
-        @pl.when(jnp.logical_not(early))
-        def _():
-            emit(distant[b])
-
         return carry
 
     lax.fori_loop(0, BLOCKS, one, 0)
 
 
-def make_residual(place, route, rlim, clim, psi, near, distant, gathered):
+def make_residual(place, route, rlim, clim, psi, near, middle, far, gathered):
     part = (BLOCKS, ROWS, WIDTH)
 
     def whole(shape):
@@ -466,19 +470,54 @@
                 pl.BlockSpec(part, lambda i, place, *_: (0, place[2], 0)),
                 whole(part),
                 whole(part),
-                whole((DEVICES, WIDTH)),
+                whole(part),
+                whole((DEVICES, 8)),
             ],
-            out_specs=[whole(part), whole(part), whole((1, WIDTH))],
+            out_specs=[whole(part), whole(part), whole((1, 8))],
         ),
         out_shape=[
             jax.ShapeDtypeStruct(part, jnp.bfloat16),
             jax.ShapeDtypeStruct(part, jnp.bfloat16),
-            jax.ShapeDtypeStruct((1, WIDTH), jnp.float32),
+            jax.ShapeDtypeStruct((1, 8), jnp.float32),
         ],
         compiler_params=pltpu.CompilerParams(vmem_limit_bytes=VMEM),
         cost_estimate=NOTHING,
         name="residual",
-    )(place, route, rlim, clim, psi, near, distant, gathered)
+    )(place, route, rlim, clim, psi, near, middle, far, gathered)
+
+
+def halve_kernel(up, down, low, high, buf, sems):
+    half = TERMS // 2
+    arrive, leave = [], []
+    for t in range(half):
+        for n, (source, first, target) in enumerate(((up, 0, low), (down, half, high))):
+            at = 2 * t + n
+            arrive.append(pltpu.make_async_copy(source.at[first + t], buf.at[at], sems.at[0, at]))
+            leave.append(pltpu.make_async_copy(buf.at[at], target.at[t], sems.at[1, at]))
+    for c in arrive:
+        c.start()
+    for c, d in zip(arrive, leave):
+        c.wait()
+        d.start()
+    for d in leave:
+        d.wait()
+
+
+def halve(up, down):
+    shape = jax.ShapeDtypeStruct((TERMS // 2,) + up.shape[1:], up.dtype)
+    return pl.pallas_call(
+        halve_kernel,
+        in_specs=[anywhere(), anywhere()],
+        out_specs=[anywhere(), anywhere()],
+        out_shape=[shape, shape],
+        scratch_shapes=[
+            pltpu.VMEM((TERMS,) + up.shape[1:], up.dtype),
+            pltpu.SemaphoreType.DMA((2, TERMS)),
+        ],
+        compiler_params=pltpu.CompilerParams(vmem_limit_bytes=VMEM),
+        cost_estimate=NOTHING,
+        name="halve",
+    )(up, down)
 
 
 def after(x, *others):
@@ -536,20 +575,20 @@
     near_codes = contract(NEAR, place, meta, pieces, left_all, [rights[d] for d in NEAR])
     rights[5], rights[3] = (up,), (down,)
     up, down = after(up, near_codes), after(down, near_codes)
-    rights[4] = ring(up[:2], down[2:])
-    near, sums = decode(
-        (NEAR,), place, route, rlim, clim, wavefunction, vectors, give_back(near_codes)
+    rights[4] = ring(*halve(up, down))
+    near_back = give_back(near_codes)
+    near, sums = decode((NEAR,), place, route, rlim, clim, wavefunction, vectors, near_back)
+    middle_codes = contract(MIDDLE, place, meta, pieces, left_all, [rights[d] for d in MIDDLE])
+    middle_back = give_back(after(middle_codes, near_back))
+    far_codes = contract(FAR, place, meta, pieces, left_all, [rights[d] for d in FAR])
+    middle, sums = decode(
+        (MIDDLE,), place, route, rlim, clim, wavefunction, vectors, middle_back, sums
     )
-    middle_codes = contract(MIDDLE, place, meta, pieces, left_all, [rights[d] for d in MIDDLE])
-    codes = contract(
-        FAR, place, after(meta, sums), pieces, left_all, [rights[d] for d in FAR], middle_codes
-    )
-    distant, spread = decode(
-        (FAR, MIDDLE), place, route, rlim, clim, wavefunction, vectors, give_back(codes), sums
-    )
+    far_back = give_back(after(far_codes, middle_back))
+    far, spread = decode((FAR,), place, route, rlim, clim, wavefunction, vectors, far_back, sums, True)
     gathered = lax.all_to_all(spread, ("sec", "op"), 0, 0, tiled=True)
     sigma16, residual, products = make_residual(
-        place, route, rlim, clim, wavefunction, near, distant, gathered
+        place, route, rlim, clim, wavefunction, near, middle, far, gathered
     )
     return (sigma16, residual, products[0, 2:4])
 

time: 266 us -> 253 us (0.951)
  blocking collectives: 82.8 us -> 46.8 us
  waiting for transfers between devices: 78.3 us -> 94.1 us
  starting transfers between devices: 28.4 us -> 35.2 us
  Pallas kernels: 40.8 us -> 46.8 us
  local copies, waits for them, and re-layouts: 13 us -> 7.3 us
    all_to_all x1 -> x0, blocking collectives: 33 us -> none  [give_back(): lax.all_to_all(coded, ('sec', 'op'), 0, 0, axis_index_groups=GROUP_XCY)]
    ppermute x4, waiting for transfers between devices: 22.1 us -> 31 us  [ring(): lax.ppermute(up, 'sec', RING_UP)]
    all_to_all x1 -> x3, starting transfers between devices: 10.3 us -> 18 us  [give_back(): lax.all_to_all(coded, ('sec', 'op'), 0, 0, axis_index_groups=GROUP_XCY)]
    all_to_all x1 -> x3, waiting for transfers between devices: 4.17 us -> 11.8 us  [give_back(): lax.all_to_all(coded, ('sec', 'op'), 0, 0, axis_index_groups=GROUP_XCY)]
    slice x2 -> x0, local copies, waits for them, and re-layouts: 4.68 us -> none  [body(): rights[4] = ring(up[:2], down[2:])]
    all_to_all x1, blocking collectives: 23.9 us -> 20.8 us  [body(): gathered = lax.all_to_all(spread, ('sec', 'op'), 0, 0, tiled=True)]
    pallas_call x2 -> x3, Pallas kernels: 8.21 us -> 11.1 us  [decode(): pl.pallas_call(kernel, grid_spec=pltpu.PrefetchScalarGridSpec(num_scalar_...]
  transfers between devices with their start and end apart: 14 -> 16, of which waited for: 10 -> 11; matrix products, arithmetic and copies ran while one was open for 4% -> 2% of each run, Pallas kernels for 11% -> 16%
where the time goes in v3:
time: 253 us; the launch traced here: 251 us
  waiting for transfers between devices  94.1 us (37%)
  Pallas kernels  46.8 us (18%)
  blocking collectives  46.8 us (18%)
  starting transfers between devices  35.2 us (14%)
  between operations  14.2 us (6%)
  local copies, waits for them, and re-layouts  7.3 us (3%)
  other arithmetic  6.35 us (3%)
    ppermute x4, waiting for transfers between devices, ring(): lax.ppermute(up, 'sec', RING_UP)  31 us
    pallas_call x3, Pallas kernels, contract(): pl.pallas_call(kernel, in_specs=[smem(), smem()] + [anywhere()] * (len(pi...  26.7 us
    all_to_all x1, blocking collectives, body(): own = lax.all_to_all(send, 'sec', 0, 0, axis_index_groups=GROUP_XC)  26.1 us
    ppermute x1, waiting for transfers between devices, body(): above = lax.ppermute(own, 'op', OP_DOWN)  22.2 us
    all_to_all x1, blocking collectives, body(): gathered = lax.all_to_all(spread, ('sec', 'op'), 0, 0, tiled=True)  20.8 us
    all_to_all x3, starting transfers between devices, give_back(): lax.all_to_all(coded, ('sec', 'op'), 0, 0, axis_index_groups=GROUP_XCY)  18 us
    ppermute x4, waiting for transfers between devices, ring(): lax.ppermute(down, 'sec', RING_DOWN)  16.6 us
    all_to_all x3, waiting for transfers between devices, give_back(): lax.all_to_all(coded, ('sec', 'op'), 0, 0, axis_index_groups=GROUP_XCY)  11.8 us
  transfers between devices with their start and end apart: 16, of which 11 were waited for; matrix products, arithmetic and copies ran while one was open for 2% of the time, Pallas kernels for 16%

profile of v3, /device:TPU:32, one launch (start us, length us, event | category | flops | bytes accessed | tf_op | source)
XLA Modules:
  0.0 250.8 jit_solution(10625786310549521845)
XLA Ops:
  7.9 3.3 %broadcast_multiply_fusion.1.rest_0_ = bf16[4,16,128,128]{3,2,1,0:T(8,128)(2,1)} fusion(bf16[4,16,128,128]{3,2,1,0:T(8,128)(2,1)} %param.13, bf16[4,16]{1,0:T(4,128)(2,1)S(1)} %convert_element_type.17), kind=kLoop, calls=%fused_computation.1 | loop fusion | flops 1048576 | bytes 4194432 | tf_op jit(solution)/shard_map/mul | solution.py:543
  15.0 3.3 %pack.1 = (bf16[8,528,128]{2,1,0:T(8,128)(2,1)S(1)}, s32[64]{0:T(128)S(1)}, s32[64]{0:T(128)S(1)}, s32[64]{0:T(128)S(1)}) custom-call(s32[3]{0:T(128)S(1)} %pad_add_fusion.place.refs_0_, s32[64]{0:T(128)S(1)} %copy-done.9, s32[4096]{0:T(1024)S(1)} %copy-done.7, s32[16]{0:T(128)S(1)} %copy-done.10, s32[1024]{0:T(1024)S(1)} %copy-done.8, ...), custom_call_target="tpu_custom_call" | custom-call | flops 1024 | bytes 1024 | tf_op jit(solution)/shard_map/pack/pallas_call | solution.py:105
  18.4 26.1 %all_to_all.31.own = bf16[8,528,128]{2,1,0:T(8,128)(2,1)S(1)} all-to-all(bf16[8,528,128]{2,1,0:T(8,128)(2,1)S(1)} %get-tuple-element.30), channel_id=1, replica_groups={{0,4,64,68,128,132,192,196},{8,12,72,76,136,140,200,204},{16,20,80,84,1..., dimensions={0} | all-to-all | bytes 2162688 | tf_op jit(solution)/shard_map/all_to_all | solution.py:554
  44.4 16.3 %collective-permute-done.4.rest_1_ = bf16[4,16,128,128]{3,2,1,0:T(8,128)(2,1)} collective-permute-done((bf16[4,16,128,128]{3,2,1,0:T(8,128)(2,1)}, bf16[4,16,128,128]{3,2,1,0:T(8,128)(2,1)}, u32[]{:S(2)}, u32[]{:S(2)}) %collective-permute-start.4) | collective-permute-done | bytes 2097184 | tf_op jit(solution)/shard_map/ppermute | solution.py:549
  60.8 3.3 %collective-permute-start.6 = (bf16[4,16,128,128]{3,2,1,0:T(8,128)(2,1)}, bf16[4,16,128,128]{3,2,1,0:T(8,128)(2,1)}, u32[]{:S(2)}, u32[]{:S(2)}) collective-permute-start(bf16[4,16,128,128]{3,2,1,0:T(8,128)(2,1)} %collective-permute-done.4.rest_1_), channel_id=1, source_target_pairs={{8,0},{12,4},{16,8},{20,12},{24,16},{28,20},{32,24},{36,28},{40,32... | collective-permute-start | bytes 6291464 | tf_op jit(solution)/shard_map/ppermute | solution.py:549
  67.6 22.2 %collective-permute-done.above = bf16[8,528,128]{2,1,0:T(8,128)(2,1)S(1)} collective-permute-done((bf16[8,528,128]{2,1,0:T(8,128)(2,1)S(1)}, bf16[8,528,128]{2,1,0:T(8,128)(2,1)S(1)}, u32[]{:S(2)}, u32[]{:S(2)}) %collective-permute-start) | collective-permute-done | bytes 1081376 | tf_op jit(solution)/shard_map/ppermute | solution.py:556
  90.7 3.7 %collective-permute-start.3 = (bf16[4,528,128]{2,1,0:T(8,128)(2,1)}, bf16[4,528,128]{2,1,0:T(8,128)(2,1)}, u32[]{:S(2)}, u32[]{:S(2)}) collective-permute-start(bf16[4,528,128]{2,1,0:T(8,128)(2,1)} %slice.31), channel_id=1, source_target_pairs={{1,0},{2,1},{3,2},{0,3},{5,4},{6,5},{7,6},{4,7},{9,8},{10,9},{11,1... | collective-permute-start | bytes 1622024 | tf_op jit(solution)/shard_map/ppermute | solution.py:562
  97.4 7.2 %collective-permute-done.3.far_high = bf16[4,528,128]{2,1,0:T(8,128)(2,1)} collective-permute-done((bf16[4,528,128]{2,1,0:T(8,128)(2,1)}, bf16[4,528,128]{2,1,0:T(8,128)(2,1)}, u32[]{:S(2)}, u32[]{:S(2)}) %collective-permute-start.3) | collective-permute-done | bytes 540704 | tf_op jit(solution)/shard_map/ppermute | solution.py:562
  104.6 5.3 %collective-permute-done.2.far_low = bf16[4,528,128]{2,1,0:T(8,128)(2,1)} collective-permute-done((bf16[4,528,128]{2,1,0:T(8,128)(2,1)}, bf16[4,528,128]{2,1,0:T(8,128)(2,1)}, u32[]{:S(2)}, u32[]{:S(2)}) %collective-permute-start.2) | collective-permute-done | bytes 540704 | tf_op jit(solution)/shard_map/ppermute | solution.py:561
  115.5 13.8 %contract.3 = s16[8,4,336,128]{3,2,1,0:T(8,128)(2,1)} custom-call(s32[3]{0:T(128)} %copy-done.5, s32[128]{0:T(128)} %reshape.28.meta, bf16[8,528,128]{2,1,0:T(8,128)(2,1)} %copy-done.11, bf16[8,528,128]{2,1,0:T(8,128)(2,1)} %copy-done.13, bf16[8,528,128]{2,1,0:T(8,128)(2,1)} %copy-done.12, bf16[4,528,128]{2,1,0:T(8,128)(2,1)} %collective-permute-done.2.far_low, ...), custom_call_target="tpu_custom_call" | custom-call | flops 21474836480 | bytes 83886080 | tf_op jit(solution)/shard_map/contract/pallas_call | solution.py:286
  129.3 6.6 %all-to-all-start.1 = ((s16[32,336,128]{2,1,0:T(8,128)(2,1)}), s16[32,336,128]{2,1,0:T(8,128)(2,1)}, u32[]{:S(2)}, u32[]{:S(2)}) async-start(s16[32,336,128]{2,1,0:T(8,128)(2,1)} %bitcast.22), calls=%async_computation.1 | async-start | bytes 5505024 | tf_op jit(solution)/shard_map/all_to_all | solution.py:573
  136.0 24.9 %collective-permute-done.9.rest_1_.up = bf16[4,16,128,128]{3,2,1,0:T(8,128)(2,1)} collective-permute-done((bf16[4,16,128,128]{3,2,1,0:T(8,128)(2,1)}, bf16[4,16,128,128]{3,2,1,0:T(8,128)(2,1)}, u32[]{:S(2)}, u32[]{:S(2)}) %collective-permute-start.9) | collective-permute-done | bytes 2097184 | tf_op jit(solution)/shard_map/ppermute | solution.py:549
  165.4 7.9 %contract.4 = s16[8,4,144,128]{3,2,1,0:T(8,128)(2,1)} custom-call(s32[3]{0:T(128)} %copy-done.5, s32[128]{0:T(128)} %reshape.28.meta, bf16[8,528,128]{2,1,0:T(8,128)(2,1)} %copy-done.11, bf16[8,528,128]{2,1,0:T(8,128)(2,1)} %copy-done.13, bf16[8,528,128]{2,1,0:T(8,128)(2,1)} %copy-done.12, bf16[4,528,128]{2,1,0:T(8,128)(2,1)} %collective-permute-done.2.far_low, ...), custom_call_target="tpu_custom_call" | custom-call | flops 8589934592 | bytes 33554432 | tf_op jit(solution)/shard_map/contract/pallas_call | solution.py:286
  173.3 7.4 %all-to-all-start.2 = ((s16[32,144,128]{2,1,0:T(8,128)(2,1)}), s16[32,144,128]{2,1,0:T(8,128)(2,1)}, u32[]{:S(2)}, u32[]{:S(2)}) async-start(s16[32,144,128]{2,1,0:T(8,128)(2,1)} %bitcast.24), calls=%async_computation.2 | async-start | bytes 2359296 | tf_op jit(solution)/shard_map/all_to_all | solution.py:573
  180.8 4.5 %collective-permute-done.10.rest_0_ = bf16[2,16,128,128]{3,2,1,0:T(8,128)(2,1)} collective-permute-done((bf16[2,16,128,128]{3,2,1,0:T(8,128)(2,1)}, bf16[2,16,128,128]{3,2,1,0:T(8,128)(2,1)}, u32[]{:S(2)}, u32[]{:S(2)}) %collective-permute-start.10) | collective-permute-done | bytes 1048608 | tf_op jit(solution)/shard_map/ppermute | solution.py:549
  185.6 5.0 %contract.5 = s16[8,4,80,128]{3,2,1,0:T(8,128)(2,1)} custom-call(s32[3]{0:T(128)} %copy-done.5, s32[128]{0:T(128)} %reshape.28.meta, bf16[8,528,128]{2,1,0:T(8,128)(2,1)} %copy-done.11, bf16[8,528,128]{2,1,0:T(8,128)(2,1)} %copy-done.13, bf16[8,528,128]{2,1,0:T(8,128)(2,1)} %copy-done.12, bf16[4,528,128]{2,1,0:T(8,128)(2,1)} %collective-permute-done.2.far_low, ...), custom_call_target="tpu_custom_call" | custom-call | flops 4294967296 | bytes 16777216 | tf_op jit(solution)/shard_map/contract/pallas_call | solution.py:286
  190.6 8.7 %all-to-all-done.2.refs_6_ = s16[32,144,128]{2,1,0:T(8,128)(2,1)} async-done(((s16[32,144,128]{2,1,0:T(8,128)(2,1)}), s16[32,144,128]{2,1,0:T(8,128)(2,1)}, u32[]{:S(2)}, u32[]{:S(2)}) %all-to-all-start.2) | async-done | bytes 1179680 | tf_op jit(solution)/shard_map/all_to_all | solution.py:573
  199.3 3.9 %all-to-all-start.3 = ((s16[32,80,128]{2,1,0:T(8,128)(2,1)}), s16[32,80,128]{2,1,0:T(8,128)(2,1)S(1)}, u32[]{:S(2)}, u32[]{:S(2)}) async-start(s16[32,80,128]{2,1,0:T(8,128)(2,1)} %bitcast.23), calls=%async_computation.3 | async-start | bytes 1310720 | tf_op jit(solution)/shard_map/all_to_all | solution.py:573
  203.2 4.5 %decode.2 = (f32[64,32,128]{2,1,0:T(8,128)S(1)}, f32[4,32,128]{2,1,0:T(8,128)S(1)}) custom-call(s32[3]{0:T(128)S(1)} %copy-done.6, s32[64]{0:T(128)S(1)} %get-tuple-element.27.refs_1_.route, s32[64]{0:T(128)S(1)} %get-tuple-element.28.refs_2_.rlim, s32[64]{0:T(128)S(1)} %get-tuple-element.29.refs_3_.clim, bf16[64,128,128]{2,1,0:T(8,128)(2,1)S(1)} %copy-done, ...), custom_call_target="tpu_custom_call" | custom-call | flops 1024 | bytes 1024 | tf_op jit(solution)/shard_map/decode/pallas_call | solution.py:394
  208.7 3.5 %decode.3 = (f32[64,32,128]{2,1,0:T(8,128)S(1)}, f32[4,32,128]{2,1,0:T(8,128)S(1)}) custom-call(s32[3]{0:T(128)S(1)} %copy-done.6, s32[64]{0:T(128)S(1)} %get-tuple-element.27.refs_1_.route, s32[64]{0:T(128)S(1)} %get-tuple-element.28.refs_2_.rlim, s32[64]{0:T(128)S(1)} %get-tuple-element.29.refs_3_.clim, bf16[64,128,128]{2,1,0:T(8,128)(2,1)S(1)} %copy-done, ...), custom_call_target="tpu_custom_call" | custom-call | flops 1024 | bytes 1024 | tf_op jit(solution)/shard_map/decode/pallas_call | solution.py:394
  213.2 3.1 %all-to-all-done.3.refs_6_ = s16[32,80,128]{2,1,0:T(8,128)(2,1)S(1)} async-done(((s16[32,80,128]{2,1,0:T(8,128)(2,1)}), s16[32,80,128]{2,1,0:T(8,128)(2,1)S(1)}, u32[]{:S(2)}, u32[]{:S(2)}) %all-to-all-start.3) | async-done | bytes 655392 | tf_op jit(solution)/shard_map/all_to_all | solution.py:573
  216.3 3.1 %decode_last.1 = (f32[64,32,128]{2,1,0:T(8,128)S(1)}, f32[256,8]{1,0:T(8,128)S(1)}) custom-call(s32[3]{0:T(128)S(1)} %copy-done.6, s32[64]{0:T(128)S(1)} %get-tuple-element.27.refs_1_.route, s32[64]{0:T(128)S(1)} %get-tuple-element.28.refs_2_.rlim, s32[64]{0:T(128)S(1)} %get-tuple-element.29.refs_3_.clim, bf16[64,128,128]{2,1,0:T(8,128)(2,1)S(1)} %copy-done, ...), custom_call_target="tpu_custom_call" | custom-call | flops 1024 | bytes 1024 | tf_op jit(solution)/shard_map/decode_last/pallas_call | solution.py:394
  219.4 20.8 %all_to_all.32 = f32[256,1,8]{2,1,0:T(1,128)S(1)} all-to-all(f32[256,1,8]{2,1,0:T(1,128)S(1)} %bitcast.18), channel_id=1, replica_groups=mesh['sec'=64,'op'=4] {'sec','op'}, dimensions={0} | all-to-all | bytes 16384 | tf_op jit(solution)/shard_map/all_to_all | solution.py:589
  240.1 3.3 %residual.1 = (bf16[64,32,128]{2,1,0:T(8,128)(2,1)}, bf16[64,32,128]{2,1,0:T(8,128)(2,1)}, f32[1,8]{1,0:T(1,128)S(1)}) custom-call(s32[3]{0:T(128)S(1)} %copy-done.6, s32[64]{0:T(128)S(1)} %get-tuple-element.27.refs_1_.route, s32[64]{0:T(128)S(1)} %get-tuple-element.28.refs_2_.rlim, s32[64]{0:T(128)S(1)} %get-tuple-element.29.refs_3_.clim, ...), custom_call_target="tpu_custom_call" | custom-call | flops 1024 | bytes 1024 | tf_op jit(solution)/shard_map/residual/pallas_call | solution.py:464
  (71 shorter events, 24.9 us)
Async XLA Ops:
  7.2 108.3 %all-gather.3.cloned.1.call-start = ((), (), s32[]{:S(2)}) async-start(), calls=%async_computation.5 | async-start | bytes 18874368 | tf_op jit(solution)/shard_map/all_gather | solution.py:552
  7.9 3.3 %copy-start.15 = (s32[4,16]{1,0:T(4,128)S(1)}, s32[4,16]{1,0:T(4,128)}, u32[]{:S(2)}) copy-start(s32[4,16]{1,0:T(4,128)} %param.14) | copy-start | bytes 772
  7.9 3.3 %copy-start.14 = (bf16[4,16,128,128]{3,2,1,0:T(8,128)(2,1)S(1)}, bf16[4,16,128,128]{3,2,1,0:T(8,128)(2,1)}, u32[]{:S(2)}) copy-start(bf16[4,16,128,128]{3,2,1,0:T(8,128)(2,1)} %param.12) | copy-start | bytes 6291460
  12.8 47.9 %collective-permute-start.4 = (bf16[4,16,128,128]{3,2,1,0:T(8,128)(2,1)}, bf16[4,16,128,128]{3,2,1,0:T(8,128)(2,1)}, u32[]{:S(2)}, u32[]{:S(2)}) collective-permute-start(bf16[4,16,128,128]{3,2,1,0:T(8,128)(2,1)} %broadcast_multiply_fusion.1.rest_0_), channel_id=1, source_target_pairs={{8,0},{12,4},{16,8},{20,12},{24,16},{28,20},{32,24},{36,28},{40,32... | collective-permute-start | bytes 6291464 | tf_op jit(solution)/shard_map/ppermute | solution.py:549
  14.7 49.8 %collective-permute-start.5 = (bf16[4,16,128,128]{3,2,1,0:T(8,128)(2,1)}, bf16[4,16,128,128]{3,2,1,0:T(8,128)(2,1)}, u32[]{:S(2)}, u32[]{:S(2)}) collective-permute-start(bf16[4,16,128,128]{3,2,1,0:T(8,128)(2,1)} %broadcast_multiply_fusion.1.rest_0_), channel_id=1, source_target_pairs={{0,8},{4,12},{8,16},{12,20},{16,24},{20,28},{24,32},{28,36},{32,40... | collective-permute-start | bytes 6291464 | tf_op jit(solution)/shard_map/ppermute | solution.py:549
  15.0 29.4 %copy-start.5 = (s32[3]{0:T(128)}, s32[3]{0:T(128)S(1)}, u32[]{:S(2)}) copy-start(s32[3]{0:T(128)S(1)} %pad_add_fusion.place.refs_0_) | copy-start | bytes 40
  44.4 51.9 %copy-start.11 = (bf16[8,528,128]{2,1,0:T(8,128)(2,1)}, bf16[8,528,128]{2,1,0:T(8,128)(2,1)S(1)}, u32[]{:S(2)}) copy-start(bf16[8,528,128]{2,1,0:T(8,128)(2,1)S(1)} %all_to_all.31.own) | copy-start | bytes 3244036
  60.8 50.7 %collective-permute-start.6 = (bf16[4,16,128,128]{3,2,1,0:T(8,128)(2,1)}, bf16[4,16,128,128]{3,2,1,0:T(8,128)(2,1)}, u32[]{:S(2)}, u32[]{:S(2)}) collective-permute-start(bf16[4,16,128,128]{3,2,1,0:T(8,128)(2,1)} %collective-permute-done.4.rest_1_), channel_id=1, source_target_pairs={{8,0},{12,4},{16,8},{20,12},{24,16},{28,20},{32,24},{36,28},{40,32... | collective-permute-start | bytes 6291464 | tf_op jit(solution)/shard_map/ppermute | solution.py:549
  64.5 48.0 %collective-permute-start.7 = (bf16[4,16,128,128]{3,2,1,0:T(8,128)(2,1)}, bf16[4,16,128,128]{3,2,1,0:T(8,128)(2,1)}, u32[]{:S(2)}, u32[]{:S(2)}) collective-permute-start(bf16[4,16,128,128]{3,2,1,0:T(8,128)(2,1)} %collective-permute-done.5.rest_2_), channel_id=1, source_target_pairs={{0,8},{4,12},{8,16},{12,20},{16,24},{20,28},{24,32},{28,36},{32,40... | collective-permute-start | bytes 6291464 | tf_op jit(solution)/shard_map/ppermute | solution.py:549
  64.5 25.3 %collective-permute-start = (bf16[8,528,128]{2,1,0:T(8,128)(2,1)S(1)}, bf16[8,528,128]{2,1,0:T(8,128)(2,1)S(1)}, u32[]{:S(2)}, u32[]{:S(2)}) collective-permute-start(bf16[8,528,128]{2,1,0:T(8,128)(2,1)S(1)} %all_to_all.31.own), channel_id=1, source_target_pairs={{1,0},{2,1},{3,2},{0,3},{5,4},{6,5},{7,6},{4,7},{9,8},{10,9},{11,1... | collective-permute-start | bytes 3244040 | tf_op jit(solution)/shard_map/ppermute | solution.py:556
  67.6 26.9 %collective-permute-start.1 = (bf16[8,528,128]{2,1,0:T(8,128)(2,1)S(1)}, bf16[8,528,128]{2,1,0:T(8,128)(2,1)S(1)}, u32[]{:S(2)}, u32[]{:S(2)}) collective-permute-start(bf16[8,528,128]{2,1,0:T(8,128)(2,1)S(1)} %all_to_all.31.own), channel_id=1, source_target_pairs={{0,1},{1,2},{2,3},{3,0},{4,5},{5,6},{6,7},{7,4},{8,9},{9,10},{10,1... | collective-permute-start | bytes 3244040 | tf_op jit(solution)/shard_map/ppermute | solution.py:555
  89.8 7.5 %copy-start.12 = (bf16[8,528,128]{2,1,0:T(8,128)(2,1)}, bf16[8,528,128]{2,1,0:T(8,128)(2,1)S(1)}, u32[]{:S(2)}) copy-start(bf16[8,528,128]{2,1,0:T(8,128)(2,1)S(1)} %collective-permute-done.above) | copy-start | bytes 3244036
  90.7 13.9 %collective-permute-start.3 = (bf16[4,528,128]{2,1,0:T(8,128)(2,1)}, bf16[4,528,128]{2,1,0:T(8,128)(2,1)}, u32[]{:S(2)}, u32[]{:S(2)}) collective-permute-start(bf16[4,528,128]{2,1,0:T(8,128)(2,1)} %slice.31), channel_id=1, source_target_pairs={{1,0},{2,1},{3,2},{0,3},{5,4},{6,5},{7,6},{4,7},{9,8},{10,9},{11,1... | collective-permute-start | bytes 1622024 | tf_op jit(solution)/shard_map/ppermute | solution.py:562
  96.3 13.6 %collective-permute-start.2 = (bf16[4,528,128]{2,1,0:T(8,128)(2,1)}, bf16[4,528,128]{2,1,0:T(8,128)(2,1)}, u32[]{:S(2)}, u32[]{:S(2)}) collective-permute-start(bf16[4,528,128]{2,1,0:T(8,128)(2,1)} %slice.30), channel_id=1, source_target_pairs={{0,1},{1,2},{2,3},{3,0},{4,5},{5,6},{6,7},{7,4},{8,9},{9,10},{10,1... | collective-permute-start | bytes 1622024 | tf_op jit(solution)/shard_map/ppermute | solution.py:561
  112.5 48.3 %collective-permute-start.8 = (bf16[4,16,128,128]{3,2,1,0:T(8,128)(2,1)}, bf16[4,16,128,128]{3,2,1,0:T(8,128)(2,1)}, u32[]{:S(2)}, u32[]{:S(2)}) collective-permute-start(bf16[4,16,128,128]{3,2,1,0:T(8,128)(2,1)} %collective-permute-done.6.rest_3_), channel_id=1, source_target_pairs={{8,0},{12,4},{16,8},{20,12},{24,16},{28,20},{32,24},{36,28},{40,32... | collective-permute-start | bytes 6291464 | tf_op jit(solution)/shard_map/ppermute | solution.py:549
  115.5 45.3 %collective-permute-start.9 = (bf16[4,16,128,128]{3,2,1,0:T(8,128)(2,1)}, bf16[4,16,128,128]{3,2,1,0:T(8,128)(2,1)}, u32[]{:S(2)}, u32[]{:S(2)}) collective-permute-start(bf16[4,16,128,128]{3,2,1,0:T(8,128)(2,1)} %collective-permute-done.7.rest_4_), channel_id=1, source_target_pairs={{0,8},{4,12},{8,16},{12,20},{16,24},{20,28},{24,32},{28,36},{32,40... | collective-permute-start | bytes 6291464 | tf_op jit(solution)/shard_map/ppermute | solution.py:549
  129.3 43.9 %all-to-all-start.1 = ((s16[32,336,128]{2,1,0:T(8,128)(2,1)}), s16[32,336,128]{2,1,0:T(8,128)(2,1)}, u32[]{:S(2)}, u32[]{:S(2)}) async-start(s16[32,336,128]{2,1,0:T(8,128)(2,1)} %bitcast.22), calls=%async_computation.1 | async-start | bytes 5505024 | tf_op jit(solution)/shard_map/all_to_all | solution.py:573
  163.3 22.0 %collective-permute-start.10 = (bf16[2,16,128,128]{3,2,1,0:T(8,128)(2,1)}, bf16[2,16,128,128]{3,2,1,0:T(8,128)(2,1)}, u32[]{:S(2)}, u32[]{:S(2)}) collective-permute-start(bf16[2,16,128,128]{3,2,1,0:T(8,128)(2,1)} %get-tuple-element.42), channel_id=1, source_target_pairs={{0,8},{4,12},{8,16},{12,20},{16,24},{20,28},{24,32},{28,36},{32,40... | collective-permute-start | bytes 3145736 | tf_op jit(solution)/shard_map/ppermute | solution.py:549
  163.6 21.9 %collective-permute-start.11 = (bf16[2,16,128,128]{3,2,1,0:T(8,128)(2,1)}, bf16[2,16,128,128]{3,2,1,0:T(8,128)(2,1)}, u32[]{:S(2)}, u32[]{:S(2)}) collective-permute-start(bf16[2,16,128,128]{3,2,1,0:T(8,128)(2,1)} %get-tuple-element.43), channel_id=1, source_target_pairs={{8,0},{12,4},{16,8},{20,12},{24,16},{28,20},{32,24},{36,28},{40,32... | collective-permute-start | bytes 3145736 | tf_op jit(solution)/shard_map/ppermute | solution.py:549
  173.3 26.0 %all-to-all-start.2 = ((s16[32,144,128]{2,1,0:T(8,128)(2,1)}), s16[32,144,128]{2,1,0:T(8,128)(2,1)}, u32[]{:S(2)}, u32[]{:S(2)}) async-start(s16[32,144,128]{2,1,0:T(8,128)(2,1)} %bitcast.24), calls=%async_computation.2 | async-start | bytes 2359296 | tf_op jit(solution)/shard_map/all_to_all | solution.py:573
  180.7 22.5 %copy-start.6 = (s32[3]{0:T(128)S(1)}, s32[3]{0:T(128)}, u32[]{:S(2)}) copy-start(s32[3]{0:T(128)} %copy-done.5) | copy-start | bytes 40
  199.3 17.0 %all-to-all-start.3 = ((s16[32,80,128]{2,1,0:T(8,128)(2,1)}), s16[32,80,128]{2,1,0:T(8,128)(2,1)S(1)}, u32[]{:S(2)}, u32[]{:S(2)}) async-start(s16[32,80,128]{2,1,0:T(8,128)(2,1)} %bitcast.23), calls=%async_computation.3 | async-start | bytes 1310720 | tf_op jit(solution)/shard_map/all_to_all | solution.py:573
  216.3 23.8 %copy-start.2 = (f32[64,32,128]{2,1,0:T(8,128)S(1)}, f32[64,32,128]{2,1,0:T(8,128)}, u32[]{:S(2)}) copy-start(f32[64,32,128]{2,1,0:T(8,128)} %copy-done.1) | copy-start | bytes 3145732
  216.3 23.8 %copy-start.4 = (f32[64,32,128]{2,1,0:T(8,128)S(1)}, f32[64,32,128]{2,1,0:T(8,128)}, u32[]{:S(2)}) copy-start(f32[64,32,128]{2,1,0:T(8,128)} %copy-done.3) | copy-start | bytes 3145732
  (8 other events, 14.1 us)
Sparse Core Ops, SparseCore 0:
  12.9 95.1 all-gather.2

commit v4 on v3

--- a/solution.py
+++ b/solution.py
@@ -12,7 +12,7 @@
 ROWS = WIDTH // NY
 PIECE = 4 * WIDTH
 HEAD = 16
-BATCH = 4
+BATCH = 8
 DEPTH = 3 * BATCH
 CODE_BITS = 13.0
 VMEM = 48 * 1024 * 1024
@@ -416,27 +416,21 @@
     )(place, route, rlim, clim, psi, vectors, returned, *([before] if later else []))
 
 
-def residual_kernel(place, route, rlim, clim, psi, near, middle, far, gathered, sigma16, out, products):
+def prepare_kernel(place, route, rlim, clim, psi, near, middle, far, sigma16, sigma32, amplitude):
     first_row = place[2] * ROWS
     rows = lax.broadcasted_iota(jnp.int32, (ROWS, WIDTH), 0) + first_row
     cols = lax.broadcasted_iota(jnp.int32, (ROWS, WIDTH), 1)
-    line = jnp.sum(gathered[...], axis=0, keepdims=True)
-    lane = lax.broadcasted_iota(jnp.int32, (1, 8), 1)
-    cross = jnp.sum(jnp.where(lane == 0, line, 0.0), axis=1, keepdims=True)
-    square = jnp.sum(jnp.where(lane == 1, line, 0.0), axis=1, keepdims=True)
-    theta = jnp.broadcast_to(cross / square, (1, WIDTH))
-    products[...] = line
 
     def one(b, carry):
         delta = lax.shift_right_logical(route[b], 1) & 7
         in_middle = (delta == MIDDLE[0]) | (delta == MIDDLE[1])
         in_far = delta == FAR[0]
         live = (rows < rlim[b]) & (cols < clim[b])
-        amp = jnp.where(live, psi[b].astype(jnp.float32), 0.0)
+        amplitude[b] = jnp.where(live, psi[b].astype(jnp.float32), 0.0).astype(jnp.bfloat16)
 
         def emit(value):
+            sigma32[b] = value
             sigma16[b] = value.astype(jnp.bfloat16)
-            out[b] = (value - theta * amp).astype(jnp.bfloat16)
 
         @pl.when(in_far)
         def _():
@@ -455,35 +449,61 @@
     lax.fori_loop(0, BLOCKS, one, 0)
 
 
-def make_residual(place, route, rlim, clim, psi, near, middle, far, gathered):
+def prepare(place, route, rlim, clim, psi, near, middle, far):
     part = (BLOCKS, ROWS, WIDTH)
-
-    def whole(shape):
-        return pl.BlockSpec(shape, lambda i, *_: (0,) * len(shape))
-
+    whole = pl.BlockSpec(part, lambda i, *_: (0, 0, 0))
     return pl.pallas_call(
-        residual_kernel,
+        prepare_kernel,
         grid_spec=pltpu.PrefetchScalarGridSpec(
             num_scalar_prefetch=4,
             grid=(1,),
-            in_specs=[
-                pl.BlockSpec(part, lambda i, place, *_: (0, place[2], 0)),
-                whole(part),
-                whole(part),
-                whole(part),
-                whole((DEVICES, 8)),
-            ],
-            out_specs=[whole(part), whole(part), whole((1, 8))],
+            in_specs=[pl.BlockSpec(part, lambda i, place, *_: (0, place[2], 0)), whole, whole, whole],
+            out_specs=[whole, whole, whole],
         ),
         out_shape=[
             jax.ShapeDtypeStruct(part, jnp.bfloat16),
+            jax.ShapeDtypeStruct(part, jnp.float32),
             jax.ShapeDtypeStruct(part, jnp.bfloat16),
-            jax.ShapeDtypeStruct((1, 8), jnp.float32),
+        ],
+        compiler_params=pltpu.CompilerParams(vmem_limit_bytes=VMEM),
+        cost_estimate=pl.CostEstimate(flops=0, bytes_accessed=20 * 2**20, transcendentals=0),
+        name="prepare",
+    )(place, route, rlim, clim, psi, near, middle, far)
+
+
+def residual_kernel(sigma32, amplitude, gathered, out, products):
+    line = jnp.sum(gathered[...], axis=0, keepdims=True)
+    lane = lax.broadcasted_iota(jnp.int32, (1, 8), 1)
+
+    def pick(n):
+        return jnp.sum(jnp.where(lane == n, line, 0.0), axis=1, keepdims=True)
+
+    theta = jnp.broadcast_to(pick(0) / pick(1), (1, WIDTH))
+    products[0] = jnp.sum(jnp.where(lane == 2, line, 0.0))
+    products[1] = jnp.sum(jnp.where(lane == 3, line, 0.0))
+
+    def one(n, carry):
+        for q in range(8):
+            b = n * 8 + q
+            out[b] = (sigma32[b] - theta * amplitude[b].astype(jnp.float32)).astype(jnp.bfloat16)
+        return carry
+
+    lax.fori_loop(0, BLOCKS // 8, one, 0)
+
+
+def make_residual(sigma32, amplitude, gathered):
+    return pl.pallas_call(
+        residual_kernel,
+        in_specs=[vmem(), vmem(), vmem()],
+        out_specs=[vmem(), smem()],
+        out_shape=[
+            jax.ShapeDtypeStruct((BLOCKS, ROWS, WIDTH), jnp.bfloat16),
+            jax.ShapeDtypeStruct((2,), jnp.float32),
         ],
         compiler_params=pltpu.CompilerParams(vmem_limit_bytes=VMEM),
         cost_estimate=NOTHING,
         name="residual",
-    )(place, route, rlim, clim, psi, near, middle, far, gathered)
+    )(sigma32, amplitude, gathered)
 
 
 def halve_kernel(up, down, low, high, buf, sems):
@@ -575,11 +595,12 @@
     near_codes = contract(NEAR, place, meta, pieces, left_all, [rights[d] for d in NEAR])
     rights[5], rights[3] = (up,), (down,)
     up, down = after(up, near_codes), after(down, near_codes)
-    rights[4] = ring(*halve(up, down))
+    low, high = halve(up, down)
+    rights[4] = ring(low, high)
     near_back = give_back(near_codes)
     near, sums = decode((NEAR,), place, route, rlim, clim, wavefunction, vectors, near_back)
     middle_codes = contract(MIDDLE, place, meta, pieces, left_all, [rights[d] for d in MIDDLE])
-    middle_back = give_back(after(middle_codes, near_back))
+    middle_back = give_back(after(middle_codes, near_back, low, high))
     far_codes = contract(FAR, place, meta, pieces, left_all, [rights[d] for d in FAR])
     middle, sums = decode(
         (MIDDLE,), place, route, rlim, clim, wavefunction, vectors, middle_back, sums
@@ -587,10 +608,11 @@
     far_back = give_back(after(far_codes, middle_back))
     far, spread = decode((FAR,), place, route, rlim, clim, wavefunction, vectors, far_back, sums, True)
     gathered = lax.all_to_all(spread, ("sec", "op"), 0, 0, tiled=True)
-    sigma16, residual, products = make_residual(
-        place, route, rlim, clim, wavefunction, near, middle, far, gathered
+    sigma16, sigma32, amplitude = prepare(
+        place, route, rlim, clim, wavefunction, near, middle, far
     )
-    return (sigma16, residual, products[0, 2:4])
+    residual, products = make_residual(sigma32, amplitude, gathered)
+    return (sigma16, residual, products)
 
 
 def solution(mesh):

time: 253 us -> 254 us (level)
  blocking collectives: 46.8 us -> 26.1 us
  starting transfers between devices: 35.2 us -> 46.1 us
  waiting for transfers between devices: 94.1 us -> 98.2 us
  local copies, waits for them, and re-layouts: 7.3 us -> 11.3 us
    all_to_all x1 -> x0, blocking collectives: 20.8 us -> none  [body(): gathered = lax.all_to_all(spread, ('sec', 'op'), 0, 0, tiled=True)]
    all_to_all x0 -> x1, starting transfers between devices: none -> 10.4 us  [body(): gathered = lax.all_to_all(spread, ('sec', 'op'), 0, 0, tiled=True)]
    all_to_all x0 -> x1, waiting for transfers between devices: none -> 5 us  [body(): gathered = lax.all_to_all(spread, ('sec', 'op'), 0, 0, tiled=True)]
    unnamed x32 -> x36, local copies, waits for them, and re-layouts: 2.99 us -> 7.64 us
    pallas_call x1 -> x2, Pallas kernels: 3.26 us -> 5.1 us  [the longest x1 3.98 us: prepare(): pl.pallas_call(prepare_kernel, grid_spec=pltpu.PrefetchScalarGridSpec(num...]
  transfers between devices with their start and end apart: 16 -> 17, of which waited for: 11 -> 12; matrix products, arithmetic and copies ran while one was open for 2% -> 2% of each run, Pallas kernels for 16% -> 17%
where the time goes in v4:
time: 254 us; the launch traced here: 251 us
  waiting for transfers between devices  98.2 us (39%)
  Pallas kernels  48.7 us (19%)
  starting transfers between devices  46.1 us (18%)
  blocking collectives  26.1 us (10%)
  between operations  14.3 us (6%)
  local copies, waits for them, and re-layouts  11.3 us (4%)
  other arithmetic  6.33 us (2%)
    ppermute x4, waiting for transfers between devices, ring(): lax.ppermute(up, 'sec', RING_UP)  32.6 us
    pallas_call x3, Pallas kernels, contract(): pl.pallas_call(kernel, in_specs=[smem(), smem()] + [anywhere()] * (len(pi...  26.1 us
    all_to_all x1, blocking collectives, body(): own = lax.all_to_all(send, 'sec', 0, 0, axis_index_groups=GROUP_XC)  26.1 us
    ppermute x1, waiting for transfers between devices, body(): above = lax.ppermute(own, 'op', OP_DOWN)  22.2 us
    all_to_all x3, starting transfers between devices, give_back(): lax.all_to_all(coded, ('sec', 'op'), 0, 0, axis_index_groups=GROUP_XCY)  18.5 us
    ppermute x4, waiting for transfers between devices, ring(): lax.ppermute(down, 'sec', RING_DOWN)  16.6 us
    pallas_call x3, Pallas kernels, decode(): pl.pallas_call(kernel, grid_spec=pltpu.PrefetchScalarGridSpec(num_scalar_...  11.7 us
    all_to_all x1, starting transfers between devices, body(): gathered = lax.all_to_all(spread, ('sec', 'op'), 0, 0, tiled=True)  10.4 us
  transfers between devices with their start and end apart: 17, of which 12 were waited for; matrix products, arithmetic and copies ran while one was open for 2% of the time, Pallas kernels for 17%

profile of v4, /device:TPU:32, one launch (start us, length us, event | category | flops | bytes accessed | tf_op | source)
XLA Modules:
  0.0 251.0 jit_solution(1326953220261671669)
XLA Ops:
  7.9 3.3 %broadcast_multiply_fusion.1.rest_0_ = bf16[4,16,128,128]{3,2,1,0:T(8,128)(2,1)} fusion(bf16[4,16,128,128]{3,2,1,0:T(8,128)(2,1)} %param.13, bf16[4,16]{1,0:T(4,128)(2,1)S(1)} %convert_element_type.17), kind=kLoop, calls=%fused_computation.1 | loop fusion | flops 1048576 | bytes 4194432 | tf_op jit(solution)/shard_map/mul | solution.py:563
  15.0 3.4 %pack.1 = (bf16[8,528,128]{2,1,0:T(8,128)(2,1)S(1)}, s32[64]{0:T(128)S(1)}, s32[64]{0:T(128)S(1)}, s32[64]{0:T(128)S(1)}) custom-call(s32[3]{0:T(128)S(1)} %pad_add_fusion.place.refs_0_, s32[64]{0:T(128)S(1)} %copy-done.11, s32[4096]{0:T(1024)S(1)} %copy-done.9, s32[16]{0:T(128)S(1)} %copy-done.12, s32[1024]{0:T(1024)S(1)} %copy-done.10, ...), custom_call_target="tpu_custom_call" | custom-call | flops 1024 | bytes 1024 | tf_op jit(solution)/shard_map/pack/pallas_call | solution.py:105
  18.4 26.1 %all_to_all.31.own = bf16[8,528,128]{2,1,0:T(8,128)(2,1)S(1)} all-to-all(bf16[8,528,128]{2,1,0:T(8,128)(2,1)S(1)} %get-tuple-element.32), channel_id=1, replica_groups={{0,4,64,68,128,132,192,196},{8,12,72,76,136,140,200,204},{16,20,80,84,1..., dimensions={0} | all-to-all | bytes 2162688 | tf_op jit(solution)/shard_map/all_to_all | solution.py:574
  44.4 16.3 %collective-permute-done.4.rest_1_ = bf16[4,16,128,128]{3,2,1,0:T(8,128)(2,1)} collective-permute-done((bf16[4,16,128,128]{3,2,1,0:T(8,128)(2,1)}, bf16[4,16,128,128]{3,2,1,0:T(8,128)(2,1)}, u32[]{:S(2)}, u32[]{:S(2)}) %collective-permute-start.4) | collective-permute-done | bytes 2097184 | tf_op jit(solution)/shard_map/ppermute | solution.py:569
  60.7 3.3 %collective-permute-start.6 = (bf16[4,16,128,128]{3,2,1,0:T(8,128)(2,1)}, bf16[4,16,128,128]{3,2,1,0:T(8,128)(2,1)}, u32[]{:S(2)}, u32[]{:S(2)}) collective-permute-start(bf16[4,16,128,128]{3,2,1,0:T(8,128)(2,1)} %collective-permute-done.4.rest_1_), channel_id=1, source_target_pairs={{8,0},{12,4},{16,8},{20,12},{24,16},{28,20},{32,24},{36,28},{40,32... | collective-permute-start | bytes 6291464 | tf_op jit(solution)/shard_map/ppermute | solution.py:569
  67.6 22.2 %collective-permute-done.above = bf16[8,528,128]{2,1,0:T(8,128)(2,1)S(1)} collective-permute-done((bf16[8,528,128]{2,1,0:T(8,128)(2,1)S(1)}, bf16[8,528,128]{2,1,0:T(8,128)(2,1)S(1)}, u32[]{:S(2)}, u32[]{:S(2)}) %collective-permute-start) | collective-permute-done | bytes 1081376 | tf_op jit(solution)/shard_map/ppermute | solution.py:576
  90.7 3.7 %collective-permute-start.3 = (bf16[4,528,128]{2,1,0:T(8,128)(2,1)}, bf16[4,528,128]{2,1,0:T(8,128)(2,1)}, u32[]{:S(2)}, u32[]{:S(2)}) collective-permute-start(bf16[4,528,128]{2,1,0:T(8,128)(2,1)} %slice.27), channel_id=1, source_target_pairs={{1,0},{2,1},{3,2},{0,3},{5,4},{6,5},{7,6},{4,7},{9,8},{10,9},{11,1... | collective-permute-start | bytes 1622024 | tf_op jit(solution)/shard_map/ppermute | solution.py:582
  97.3 7.2 %collective-permute-done.3.far_high = bf16[4,528,128]{2,1,0:T(8,128)(2,1)} collective-permute-done((bf16[4,528,128]{2,1,0:T(8,128)(2,1)}, bf16[4,528,128]{2,1,0:T(8,128)(2,1)}, u32[]{:S(2)}, u32[]{:S(2)}) %collective-permute-start.3) | collective-permute-done | bytes 540704 | tf_op jit(solution)/shard_map/ppermute | solution.py:582
  104.5 5.3 %collective-permute-done.2.far_low = bf16[4,528,128]{2,1,0:T(8,128)(2,1)} collective-permute-done((bf16[4,528,128]{2,1,0:T(8,128)(2,1)}, bf16[4,528,128]{2,1,0:T(8,128)(2,1)}, u32[]{:S(2)}, u32[]{:S(2)}) %collective-permute-start.2) | collective-permute-done | bytes 540704 | tf_op jit(solution)/shard_map/ppermute | solution.py:581
  115.5 11.4 %contract.3 = s16[8,4,336,128]{3,2,1,0:T(8,128)(2,1)} custom-call(s32[3]{0:T(128)} %copy-done.7, s32[128]{0:T(128)} %reshape.28.meta, bf16[8,528,128]{2,1,0:T(8,128)(2,1)} %copy-done.13, bf16[8,528,128]{2,1,0:T(8,128)(2,1)} %copy-done.15, bf16[8,528,128]{2,1,0:T(8,128)(2,1)} %copy-done.14, bf16[4,528,128]{2,1,0:T(8,128)(2,1)} %collective-permute-done.2.far_low, ...), custom_call_target="tpu_custom_call" | custom-call | flops 21474836480 | bytes 83886080 | tf_op jit(solution)/shard_map/contract/pallas_call | solution.py:286
  126.9 8.4 %all-to-all-start.1 = ((s16[32,336,128]{2,1,0:T(8,128)(2,1)}), s16[32,336,128]{2,1,0:T(8,128)(2,1)}, u32[]{:S(2)}, u32[]{:S(2)}) async-start(s16[32,336,128]{2,1,0:T(8,128)(2,1)} %bitcast.19), calls=%async_computation.1 | async-start | bytes 5505024 | tf_op jit(solution)/shard_map/all_to_all | solution.py:593
  135.3 25.5 %collective-permute-done.9.rest_1_.up = bf16[4,16,128,128]{3,2,1,0:T(8,128)(2,1)} collective-permute-done((bf16[4,16,128,128]{3,2,1,0:T(8,128)(2,1)}, bf16[4,16,128,128]{3,2,1,0:T(8,128)(2,1)}, u32[]{:S(2)}, u32[]{:S(2)}) %collective-permute-start.9) | collective-permute-done | bytes 2097184 | tf_op jit(solution)/shard_map/ppermute | solution.py:569
  165.4 8.2 %contract.4 = s16[8,4,144,128]{3,2,1,0:T(8,128)(2,1)} custom-call(s32[3]{0:T(128)} %copy-done.7, s32[128]{0:T(128)} %reshape.28.meta, bf16[8,528,128]{2,1,0:T(8,128)(2,1)} %copy-done.13, bf16[8,528,128]{2,1,0:T(8,128)(2,1)} %copy-done.15, bf16[8,528,128]{2,1,0:T(8,128)(2,1)} %copy-done.14, bf16[4,528,128]{2,1,0:T(8,128)(2,1)} %collective-permute-done.2.far_low, ...), custom_call_target="tpu_custom_call" | custom-call | flops 8589934592 | bytes 33554432 | tf_op jit(solution)/shard_map/contract/pallas_call | solution.py:286
  173.6 6.2 %all-to-all-start.2 = ((s16[32,144,128]{2,1,0:T(8,128)(2,1)}), s16[32,144,128]{2,1,0:T(8,128)(2,1)}, u32[]{:S(2)}, u32[]{:S(2)}) async-start(s16[32,144,128]{2,1,0:T(8,128)(2,1)} %bitcast.21), calls=%async_computation.2 | async-start | bytes 2359296 | tf_op jit(solution)/shard_map/all_to_all | solution.py:593
  179.8 5.5 %collective-permute-done.10.rest_0_ = bf16[2,16,128,128]{3,2,1,0:T(8,128)(2,1)} collective-permute-done((bf16[2,16,128,128]{3,2,1,0:T(8,128)(2,1)}, bf16[2,16,128,128]{3,2,1,0:T(8,128)(2,1)}, u32[]{:S(2)}, u32[]{:S(2)}) %collective-permute-start.10) | collective-permute-done | bytes 1048608 | tf_op jit(solution)/shard_map/ppermute | solution.py:569
  185.6 6.5 %contract.5 = s16[8,4,80,128]{3,2,1,0:T(8,128)(2,1)} custom-call(s32[3]{0:T(128)} %copy-done.7, s32[128]{0:T(128)} %reshape.28.meta, bf16[8,528,128]{2,1,0:T(8,128)(2,1)} %copy-done.13, bf16[8,528,128]{2,1,0:T(8,128)(2,1)} %copy-done.15, bf16[8,528,128]{2,1,0:T(8,128)(2,1)} %copy-done.14, bf16[4,528,128]{2,1,0:T(8,128)(2,1)} %collective-permute-done.2.far_low, ...), custom_call_target="tpu_custom_call" | custom-call | flops 4294967296 | bytes 16777216 | tf_op jit(solution)/shard_map/contract/pallas_call | solution.py:286
  192.1 6.3 %all-to-all-done.2.refs_6_ = s16[32,144,128]{2,1,0:T(8,128)(2,1)} async-done(((s16[32,144,128]{2,1,0:T(8,128)(2,1)}), s16[32,144,128]{2,1,0:T(8,128)(2,1)}, u32[]{:S(2)}, u32[]{:S(2)}) %all-to-all-start.2) | async-done | bytes 1179680 | tf_op jit(solution)/shard_map/all_to_all | solution.py:593
  198.3 3.9 %all-to-all-start.3 = ((s16[32,80,128]{2,1,0:T(8,128)(2,1)}), s16[32,80,128]{2,1,0:T(8,128)(2,1)S(1)}, u32[]{:S(2)}, u32[]{:S(2)}) async-start(s16[32,80,128]{2,1,0:T(8,128)(2,1)} %bitcast.20), calls=%async_computation.3 | async-start | bytes 1310720 | tf_op jit(solution)/shard_map/all_to_all | solution.py:593
  202.2 4.6 %decode.2 = (f32[64,32,128]{2,1,0:T(8,128)S(1)}, f32[4,32,128]{2,1,0:T(8,128)S(1)}) custom-call(s32[3]{0:T(128)S(1)} %copy-done.8, s32[64]{0:T(128)S(1)} %get-tuple-element.29.refs_1_.route, s32[64]{0:T(128)S(1)} %get-tuple-element.30.refs_2_.rlim, s32[64]{0:T(128)S(1)} %get-tuple-element.31.refs_3_.clim, bf16[64,128,128]{2,1,0:T(8,128)(2,1)S(1)} %copy-done, ...), custom_call_target="tpu_custom_call" | custom-call | flops 1024 | bytes 1024 | tf_op jit(solution)/shard_map/decode/pallas_call | solution.py:394
  207.8 3.5 %decode.3 = (f32[64,32,128]{2,1,0:T(8,128)S(1)}, f32[4,32,128]{2,1,0:T(8,128)S(1)}) custom-call(s32[3]{0:T(128)S(1)} %copy-done.8, s32[64]{0:T(128)S(1)} %get-tuple-element.29.refs_1_.route, s32[64]{0:T(128)S(1)} %get-tuple-element.30.refs_2_.rlim, s32[64]{0:T(128)S(1)} %get-tuple-element.31.refs_3_.clim, bf16[64,128,128]{2,1,0:T(8,128)(2,1)S(1)} %copy-done, ...), custom_call_target="tpu_custom_call" | custom-call | flops 1024 | bytes 1024 | tf_op jit(solution)/shard_map/decode/pallas_call | solution.py:394
  215.3 3.7 %decode_last.1 = (f32[64,32,128]{2,1,0:T(8,128)S(1)}, f32[256,8]{1,0:T(8,128)}) custom-call(s32[3]{0:T(128)S(1)} %copy-done.8, s32[64]{0:T(128)S(1)} %get-tuple-element.29.refs_1_.route, s32[64]{0:T(128)S(1)} %get-tuple-element.30.refs_2_.rlim, s32[64]{0:T(128)S(1)} %get-tuple-element.31.refs_3_.clim, bf16[64,128,128]{2,1,0:T(8,128)(2,1)S(1)} %copy-done, ...), custom_call_target="tpu_custom_call" | custom-call | flops 1024 | bytes 1024 | tf_op jit(solution)/shard_map/decode_last/pallas_call | solution.py:394
  220.0 10.4 %all-to-all-start.4 = ((f32[256,1,8]{2,1,0:T(1,128)}), f32[256,1,8]{2,1,0:T(1,128)S(1)}, u32[]{:S(2)}, u32[]{:S(2)}) async-start(f32[256,1,8]{2,1,0:T(1,128)} %bitcast.12), calls=%async_computation.4 | async-start | bytes 262144 | tf_op jit(solution)/shard_map/all_to_all | solution.py:610
  234.0 4.0 %prepare.1 = (bf16[64,32,128]{2,1,0:T(8,128)(2,1)}, f32[64,32,128]{2,1,0:T(8,128)S(1)}, bf16[64,32,128]{2,1,0:T(8,128)(2,1)S(1)}) custom-call(s32[3]{0:T(128)S(1)} %copy-done.8, s32[64]{0:T(128)S(1)} %get-tuple-element.29.refs_1_.route, s32[64]{0:T(128)S(1)} %get-tuple-element.30.refs_2_.rlim, s32[64]{0:T(128)S(1)} %get-tuple-element.31.refs_3_.clim, ...), custom_call_target="tpu_custom_call" | custom-call | bytes 20971520 | tf_op jit(solution)/shard_map/prepare/pallas_call | solution.py:455
  238.0 5.0 %all-to-all-done.4 = f32[256,1,8]{2,1,0:T(1,128)S(1)} async-done(((f32[256,1,8]{2,1,0:T(1,128)}), f32[256,1,8]{2,1,0:T(1,128)S(1)}, u32[]{:S(2)}, u32[]{:S(2)}) %all-to-all-start.4) | async-done | bytes 8224 | tf_op jit(solution)/shard_map/all_to_all | solution.py:610
  (76 shorter events, 33.1 us)
Async XLA Ops:
  7.2 108.3 %all-gather.3.cloned.1.call-start = ((), (), s32[]{:S(2)}) async-start(), calls=%async_computation.5 | async-start | bytes 18874368 | tf_op jit(solution)/shard_map/all_gather | solution.py:572
  7.9 3.3 %copy-start.17 = (s32[4,16]{1,0:T(4,128)S(1)}, s32[4,16]{1,0:T(4,128)}, u32[]{:S(2)}) copy-start(s32[4,16]{1,0:T(4,128)} %param.14) | copy-start | bytes 772
  7.9 3.3 %copy-start.16 = (bf16[4,16,128,128]{3,2,1,0:T(8,128)(2,1)S(1)}, bf16[4,16,128,128]{3,2,1,0:T(8,128)(2,1)}, u32[]{:S(2)}) copy-start(bf16[4,16,128,128]{3,2,1,0:T(8,128)(2,1)} %param.12) | copy-start | bytes 6291460
  12.8 2.2 copy-start.12
  12.8 47.9 %collective-permute-start.4 = (bf16[4,16,128,128]{3,2,1,0:T(8,128)(2,1)}, bf16[4,16,128,128]{3,2,1,0:T(8,128)(2,1)}, u32[]{:S(2)}, u32[]{:S(2)}) collective-permute-start(bf16[4,16,128,128]{3,2,1,0:T(8,128)(2,1)} %broadcast_multiply_fusion.1.rest_0_), channel_id=1, source_target_pairs={{8,0},{12,4},{16,8},{20,12},{24,16},{28,20},{32,24},{36,28},{40,32... | collective-permute-start | bytes 6291464 | tf_op jit(solution)/shard_map/ppermute | solution.py:569
  14.7 49.8 %collective-permute-start.5 = (bf16[4,16,128,128]{3,2,1,0:T(8,128)(2,1)}, bf16[4,16,128,128]{3,2,1,0:T(8,128)(2,1)}, u32[]{:S(2)}, u32[]{:S(2)}) collective-permute-start(bf16[4,16,128,128]{3,2,1,0:T(8,128)(2,1)} %broadcast_multiply_fusion.1.rest_0_), channel_id=1, source_target_pairs={{0,8},{4,12},{8,16},{12,20},{16,24},{20,28},{24,32},{28,36},{32,40... | collective-permute-start | bytes 6291464 | tf_op jit(solution)/shard_map/ppermute | solution.py:569
  15.0 29.4 %copy-start.7 = (s32[3]{0:T(128)}, s32[3]{0:T(128)S(1)}, u32[]{:S(2)}) copy-start(s32[3]{0:T(128)S(1)} %pad_add_fusion.place.refs_0_) | copy-start | bytes 40
  44.4 51.8 %copy-start.13 = (bf16[8,528,128]{2,1,0:T(8,128)(2,1)}, bf16[8,528,128]{2,1,0:T(8,128)(2,1)S(1)}, u32[]{:S(2)}) copy-start(bf16[8,528,128]{2,1,0:T(8,128)(2,1)S(1)} %all_to_all.31.own) | copy-start | bytes 3244036
  60.7 50.7 %collective-permute-start.6 = (bf16[4,16,128,128]{3,2,1,0:T(8,128)(2,1)}, bf16[4,16,128,128]{3,2,1,0:T(8,128)(2,1)}, u32[]{:S(2)}, u32[]{:S(2)}) collective-permute-start(bf16[4,16,128,128]{3,2,1,0:T(8,128)(2,1)} %collective-permute-done.4.rest_1_), channel_id=1, source_target_pairs={{8,0},{12,4},{16,8},{20,12},{24,16},{28,20},{32,24},{36,28},{40,32... | collective-permute-start | bytes 6291464 | tf_op jit(solution)/shard_map/ppermute | solution.py:569
  64.5 48.0 %collective-permute-start.7 = (bf16[4,16,128,128]{3,2,1,0:T(8,128)(2,1)}, bf16[4,16,128,128]{3,2,1,0:T(8,128)(2,1)}, u32[]{:S(2)}, u32[]{:S(2)}) collective-permute-start(bf16[4,16,128,128]{3,2,1,0:T(8,128)(2,1)} %collective-permute-done.5.rest_2_), channel_id=1, source_target_pairs={{0,8},{4,12},{8,16},{12,20},{16,24},{20,28},{24,32},{28,36},{32,40... | collective-permute-start | bytes 6291464 | tf_op jit(solution)/shard_map/ppermute | solution.py:569
  64.5 25.3 %collective-permute-start = (bf16[8,528,128]{2,1,0:T(8,128)(2,1)S(1)}, bf16[8,528,128]{2,1,0:T(8,128)(2,1)S(1)}, u32[]{:S(2)}, u32[]{:S(2)}) collective-permute-start(bf16[8,528,128]{2,1,0:T(8,128)(2,1)S(1)} %all_to_all.31.own), channel_id=1, source_target_pairs={{1,0},{2,1},{3,2},{0,3},{5,4},{6,5},{7,6},{4,7},{9,8},{10,9},{11,1... | collective-permute-start | bytes 3244040 | tf_op jit(solution)/shard_map/ppermute | solution.py:576
  67.5 26.8 %collective-permute-start.1 = (bf16[8,528,128]{2,1,0:T(8,128)(2,1)S(1)}, bf16[8,528,128]{2,1,0:T(8,128)(2,1)S(1)}, u32[]{:S(2)}, u32[]{:S(2)}) collective-permute-start(bf16[8,528,128]{2,1,0:T(8,128)(2,1)S(1)} %all_to_all.31.own), channel_id=1, source_target_pairs={{0,1},{1,2},{2,3},{3,0},{4,5},{5,6},{6,7},{7,4},{8,9},{9,10},{10,1... | collective-permute-start | bytes 3244040 | tf_op jit(solution)/shard_map/ppermute | solution.py:575
  89.8 7.4 %copy-start.14 = (bf16[8,528,128]{2,1,0:T(8,128)(2,1)}, bf16[8,528,128]{2,1,0:T(8,128)(2,1)S(1)}, u32[]{:S(2)}) copy-start(bf16[8,528,128]{2,1,0:T(8,128)(2,1)S(1)} %collective-permute-done.above) | copy-start | bytes 3244036
  90.7 13.9 %collective-permute-start.3 = (bf16[4,528,128]{2,1,0:T(8,128)(2,1)}, bf16[4,528,128]{2,1,0:T(8,128)(2,1)}, u32[]{:S(2)}, u32[]{:S(2)}) collective-permute-start(bf16[4,528,128]{2,1,0:T(8,128)(2,1)} %slice.27), channel_id=1, source_target_pairs={{1,0},{2,1},{3,2},{0,3},{5,4},{6,5},{7,6},{4,7},{9,8},{10,9},{11,1... | collective-permute-start | bytes 1622024 | tf_op jit(solution)/shard_map/ppermute | solution.py:582
  96.2 13.6 %collective-permute-start.2 = (bf16[4,528,128]{2,1,0:T(8,128)(2,1)}, bf16[4,528,128]{2,1,0:T(8,128)(2,1)}, u32[]{:S(2)}, u32[]{:S(2)}) collective-permute-start(bf16[4,528,128]{2,1,0:T(8,128)(2,1)} %slice.26), channel_id=1, source_target_pairs={{0,1},{1,2},{2,3},{3,0},{4,5},{5,6},{6,7},{7,4},{8,9},{9,10},{10,1... | collective-permute-start | bytes 1622024 | tf_op jit(solution)/shard_map/ppermute | solution.py:581
  112.5 48.3 %collective-permute-start.8 = (bf16[4,16,128,128]{3,2,1,0:T(8,128)(2,1)}, bf16[4,16,128,128]{3,2,1,0:T(8,128)(2,1)}, u32[]{:S(2)}, u32[]{:S(2)}) collective-permute-start(bf16[4,16,128,128]{3,2,1,0:T(8,128)(2,1)} %collective-permute-done.6.rest_3_), channel_id=1, source_target_pairs={{8,0},{12,4},{16,8},{20,12},{24,16},{28,20},{32,24},{36,28},{40,32... | collective-permute-start | bytes 6291464 | tf_op jit(solution)/shard_map/ppermute | solution.py:569
  115.5 45.3 %collective-permute-start.9 = (bf16[4,16,128,128]{3,2,1,0:T(8,128)(2,1)}, bf16[4,16,128,128]{3,2,1,0:T(8,128)(2,1)}, u32[]{:S(2)}, u32[]{:S(2)}) collective-permute-start(bf16[4,16,128,128]{3,2,1,0:T(8,128)(2,1)} %collective-permute-done.7.rest_4_), channel_id=1, source_target_pairs={{0,8},{4,12},{8,16},{12,20},{16,24},{20,28},{24,32},{28,36},{32,40... | collective-permute-start | bytes 6291464 | tf_op jit(solution)/shard_map/ppermute | solution.py:569
  126.9 46.7 %all-to-all-start.1 = ((s16[32,336,128]{2,1,0:T(8,128)(2,1)}), s16[32,336,128]{2,1,0:T(8,128)(2,1)}, u32[]{:S(2)}, u32[]{:S(2)}) async-start(s16[32,336,128]{2,1,0:T(8,128)(2,1)} %bitcast.19), calls=%async_computation.1 | async-start | bytes 5505024 | tf_op jit(solution)/shard_map/all_to_all | solution.py:593
  163.2 22.0 %collective-permute-start.10 = (bf16[2,16,128,128]{3,2,1,0:T(8,128)(2,1)}, bf16[2,16,128,128]{3,2,1,0:T(8,128)(2,1)}, u32[]{:S(2)}, u32[]{:S(2)}) collective-permute-start(bf16[2,16,128,128]{3,2,1,0:T(8,128)(2,1)} %get-tuple-element.41), channel_id=1, source_target_pairs={{0,8},{4,12},{8,16},{12,20},{16,24},{20,28},{24,32},{28,36},{32,40... | collective-permute-start | bytes 3145736 | tf_op jit(solution)/shard_map/ppermute | solution.py:569
  163.6 21.9 %collective-permute-start.11 = (bf16[2,16,128,128]{3,2,1,0:T(8,128)(2,1)}, bf16[2,16,128,128]{3,2,1,0:T(8,128)(2,1)}, u32[]{:S(2)}, u32[]{:S(2)}) collective-permute-start(bf16[2,16,128,128]{3,2,1,0:T(8,128)(2,1)} %get-tuple-element.42), channel_id=1, source_target_pairs={{8,0},{12,4},{16,8},{20,12},{24,16},{28,20},{32,24},{36,28},{40,32... | collective-permute-start | bytes 3145736 | tf_op jit(solution)/shard_map/ppermute | solution.py:569
  173.6 24.7 %all-to-all-start.2 = ((s16[32,144,128]{2,1,0:T(8,128)(2,1)}), s16[32,144,128]{2,1,0:T(8,128)(2,1)}, u32[]{:S(2)}, u32[]{:S(2)}) async-start(s16[32,144,128]{2,1,0:T(8,128)(2,1)} %bitcast.21), calls=%async_computation.2 | async-start | bytes 2359296 | tf_op jit(solution)/shard_map/all_to_all | solution.py:593
  179.8 22.5 %copy-start.8 = (s32[3]{0:T(128)S(1)}, s32[3]{0:T(128)}, u32[]{:S(2)}) copy-start(s32[3]{0:T(128)} %copy-done.7) | copy-start | bytes 40
  198.3 17.0 %all-to-all-start.3 = ((s16[32,80,128]{2,1,0:T(8,128)(2,1)}), s16[32,80,128]{2,1,0:T(8,128)(2,1)S(1)}, u32[]{:S(2)}, u32[]{:S(2)}) async-start(s16[32,80,128]{2,1,0:T(8,128)(2,1)} %bitcast.20), calls=%async_computation.3 | async-start | bytes 1310720 | tf_op jit(solution)/shard_map/all_to_all | solution.py:593
  220.0 23.0 %all-to-all-start.4 = ((f32[256,1,8]{2,1,0:T(1,128)}), f32[256,1,8]{2,1,0:T(1,128)S(1)}, u32[]{:S(2)}, u32[]{:S(2)}) async-start(f32[256,1,8]{2,1,0:T(1,128)} %bitcast.12), calls=%async_computation.4 | async-start | bytes 262144 | tf_op jit(solution)/shard_map/all_to_all | solution.py:610
  (11 other events, 16.5 us)
Sparse Core Ops, SparseCore 0:
  12.9 95.1 all-gather.2

commit v5 on v4

--- a/solution.py
+++ b/solution.py
@@ -122,14 +122,14 @@
     )(place, block_left, block_right, left_dims, right_dims, psi)
 
 
-def contract(deltas, place, meta, pieces, left_all, rights, carried=None):
+def contract(deltas, place, meta, acts, pieces, left_all, rights, carried=None):
     slots = len(deltas) * 2
     most = NG * slots
     rows_own = slots * ROWS + HEAD
     rows_out = rows_own + (0 if carried is None else carried.shape[2])
     split = [len(r) for r in rights]
 
-    def kernel(place, meta, own, below, above, far_low, far_high, left, *rest):
+    def kernel(place, meta, acts, own, below, above, far_low, far_high, left, *rest):
         right_refs, rest = rest[: sum(split)], rest[sum(split) :]
         if carried is not None:
             earlier, rest = rest[0], rest[1:]
@@ -251,17 +251,20 @@
                 n = jnp.minimum(m * BATCH + q, count - 1)
                 at = lax.rem(n, DEPTH)
                 i, j, g, s, sub, relative = fields(listed[n])
-                terms = lax.dot_general(
+                product = lax.dot_general(
                     left_buf[at].reshape(TERMS * WIDTH, WIDTH),
                     psi_buf[at],
                     (((1,), (0,)), ((), ())),
                     preferred_element_type=jnp.float32,
-                ).astype(jnp.bfloat16)
+                )
+                terms = []
+                for a in range(TERMS):
+                    act = jnp.full((WIDTH, WIDTH), acts[(g * TERMS + a) * SECTORS + i], jnp.int32)
+                    term = jnp.where(act != 0, product[a * WIDTH : (a + 1) * WIDTH], 0.0)
+                    terms.append(term.astype(jnp.bfloat16))
                 total = None
                 for a in range(0, TERMS, 2):
-                    lhs = jnp.concatenate(
-                        [terms[a * WIDTH : (a + 1) * WIDTH], terms[(a + 1) * WIDTH : (a + 2) * WIDTH]], axis=1
-                    )
+                    lhs = jnp.concatenate([terms[a], terms[a + 1]], axis=1)
                     rhs = jnp.concatenate([right_buf[at, a], right_buf[at, a + 1]], axis=1)
                     part = lax.dot_general(
                         lhs, rhs, (((1,), (1,)), ((), ())), preferred_element_type=jnp.float32
@@ -285,7 +288,7 @@
     flat = [part for r in rights for part in r]
     return pl.pallas_call(
         kernel,
-        in_specs=[smem(), smem()]
+        in_specs=[smem(), smem(), smem()]
         + [anywhere()] * (len(pieces) + 1 + len(flat))
         + ([] if carried is None else [vmem()]),
         out_specs=vmem(),
@@ -303,7 +306,7 @@
             flops=most * 16 * TERMS * 2 * WIDTH**3, bytes_accessed=most * 2**20, transcendentals=0
         ),
         name="contract",
-    )(place, meta, *pieces, left_all, *flat, *([] if carried is None else [carried]))
+    )(place, meta, acts, *pieces, left_all, *flat, *([] if carried is None else [carried]))
 
 
 def first_rows(chunks):
@@ -561,20 +564,20 @@
     place = jnp.stack([sec, (sec // NC) % NZ, op]).astype(jnp.int32)
 
     right_table = right_env * right_pattern[:, :, None, None].astype(jnp.bfloat16)
-    left_env = after(left_env, right_table)
-    left_table = left_env * left_pattern[:, :, None, None].astype(jnp.bfloat16)
     rights = {0: (right_table,)}
 
     def ring(up, down):
         return lax.ppermute(up, "sec", RING_UP), lax.ppermute(down, "sec", RING_DOWN)
 
     up, down = ring(right_table, right_table)
-    left_all = lax.all_gather(left_table, "sec", axis_index_groups=GROUP_XC)
+    left_all = lax.all_gather(left_env, "sec", axis_index_groups=GROUP_XC)
     send, route, rlim, clim = pack(place, block_left, block_right, left_dims, right_dims, wavefunction)
     own = lax.all_to_all(send, "sec", 0, 0, axis_index_groups=GROUP_XC)
     below = lax.ppermute(own, "op", OP_UP)
     above = lax.ppermute(own, "op", OP_DOWN)
-    up, down = after(up, own), after(down, own)
+    acts = jnp.broadcast_to(after(left_pattern, own)[None], (NG,) + left_pattern.shape)
+    acts = lax.all_to_all(acts, "sec", 0, 0, axis_index_groups=GROUP_XC).reshape(-1)
+    up, down = after(up, own, acts), after(down, own, acts)
     rights[7], rights[1] = (up,), (down,)
 
     up, down = ring(up, down)
@@ -592,16 +595,16 @@
         coded = coded.reshape((NG * NY,) + coded.shape[2:])
         return lax.all_to_all(coded, ("sec", "op"), 0, 0, axis_index_groups=GROUP_XCY)
 
-    near_codes = contract(NEAR, place, meta, pieces, left_all, [rights[d] for d in NEAR])
+    near_codes = contract(NEAR, place, meta, acts, pieces, left_all, [rights[d] for d in NEAR])
     rights[5], rights[3] = (up,), (down,)
     up, down = after(up, near_codes), after(down, near_codes)
     low, high = halve(up, down)
     rights[4] = ring(low, high)
     near_back = give_back(near_codes)
     near, sums = decode((NEAR,), place, route, rlim, clim, wavefunction, vectors, near_back)
-    middle_codes = contract(MIDDLE, place, meta, pieces, left_all, [rights[d] for d in MIDDLE])
+    middle_codes = contract(MIDDLE, place, meta, acts, pieces, left_all, [rights[d] for d in MIDDLE])
     middle_back = give_back(after(middle_codes, near_back, low, high))
-    far_codes = contract(FAR, place, meta, pieces, left_all, [rights[d] for d in FAR])
+    far_codes = contract(FAR, place, meta, acts, pieces, left_all, [rights[d] for d in FAR])
     middle, sums = decode(
         (MIDDLE,), place, route, rlim, clim, wavefunction, vectors, middle_back, sums
     )

time: 254 us -> 251 us (0.988)
  blocking collectives: 26.1 us -> 35.3 us
  waiting for transfers between devices: 98.2 us -> 90.2 us
    ppermute x4, waiting for transfers between devices: 16.6 us -> 6.6 us  [ring(): lax.ppermute(down, 'sec', RING_DOWN)]
    all_to_all x0 -> x1, blocking collectives: none -> 7.86 us  [body(): lax.all_to_all(acts, 'sec', 0, 0, axis_index_groups=GROUP_XC).reshape(-1)]
    all_to_all x3, waiting for transfers between devices: 9.3 us -> 12 us  [give_back(): lax.all_to_all(coded, ('sec', 'op'), 0, 0, axis_index_groups=GROUP_XCY)]
  transfers between devices with their start and end apart: 17 -> 17, of which waited for: 12 -> 12; matrix products, arithmetic and copies ran while one was open for 2% -> 4% of each run, Pallas kernels for 17% -> 17%
where the time goes in v5:
time: 251 us; the launch traced here: 248 us
  waiting for transfers between devices  90.2 us (36%)
  Pallas kernels  46.3 us (18%)
  starting transfers between devices  46.1 us (18%)
  blocking collectives  35.3 us (14%)
  between operations  14.3 us (6%)
  local copies, waits for them, and re-layouts  12 us (5%)
  other arithmetic  4.09 us (2%)
    ppermute x4, waiting for transfers between devices, ring(): lax.ppermute(up, 'sec', RING_UP)  31.9 us
    all_to_all x1, blocking collectives, body(): own = lax.all_to_all(send, 'sec', 0, 0, axis_index_groups=GROUP_XC)  27.4 us
    pallas_call x3, Pallas kernels, contract(): pl.pallas_call(kernel, in_specs=[smem(), smem(), smem()] + [anywhere()] *...  23.6 us
    ppermute x1, waiting for transfers between devices, body(): above = lax.ppermute(own, 'op', OP_DOWN)  22.2 us
    all_to_all x3, starting transfers between devices, give_back(): lax.all_to_all(coded, ('sec', 'op'), 0, 0, axis_index_groups=GROUP_XCY)  21 us
    all_to_all x3, waiting for transfers between devices, give_back(): lax.all_to_all(coded, ('sec', 'op'), 0, 0, axis_index_groups=GROUP_XCY)  12 us
    pallas_call x3, Pallas kernels, decode(): pl.pallas_call(kernel, grid_spec=pltpu.PrefetchScalarGridSpec(num_scalar_...  11.7 us
    ppermute x4, starting transfers between devices, ring(): lax.ppermute(down, 'sec', RING_DOWN)  9.87 us
  transfers between devices with their start and end apart: 17, of which 12 were waited for; matrix products, arithmetic and copies ran while one was open for 4% of the time, Pallas kernels for 17%

profile of v5, /device:TPU:32, one launch (start us, length us, event | category | flops | bytes accessed | tf_op | source)
XLA Modules:
  0.0 248.3 jit_solution(12644590456874737470)
XLA Ops:
  13.4 3.4 %pack.1 = (bf16[8,528,128]{2,1,0:T(8,128)(2,1)S(1)}, s32[64]{0:T(128)S(1)}, s32[64]{0:T(128)S(1)}, s32[64]{0:T(128)S(1)}) custom-call(s32[3]{0:T(128)S(1)} %pad_add_fusion.place.refs_0_, s32[64]{0:T(128)S(1)} %copy-done.11, s32[4096]{0:T(1024)S(1)} %copy-done.9, s32[16]{0:T(128)S(1)} %copy-done.12, s32[1024]{0:T(1024)S(1)} %copy-done.10, ...), custom_call_target="tpu_custom_call" | custom-call | flops 1024 | bytes 1024 | tf_op jit(solution)/shard_map/pack/pallas_call | solution.py:105
  16.8 27.4 %all_to_all.36.own = bf16[8,528,128]{2,1,0:T(8,128)(2,1)S(1)} all-to-all(bf16[8,528,128]{2,1,0:T(8,128)(2,1)S(1)} %get-tuple-element.32), channel_id=1, replica_groups={{0,4,64,68,128,132,192,196},{8,12,72,76,136,140,200,204},{16,20,80,84,1..., dimensions={0} | all-to-all | bytes 2162688 | tf_op jit(solution)/shard_map/all_to_all | solution.py:575
  44.2 7.9 %all_to_all.37 = s32[8,4,16]{2,1,0:T(4,128)S(1)} all-to-all(s32[8,4,16]{2,1,0:T(4,128)S(1)} %broadcast_in_dim.2), channel_id=1, replica_groups={{0,4,64,68,128,132,192,196},{8,12,72,76,136,140,200,204},{16,20,80,84,1..., dimensions={0} | all-to-all | bytes 4096 | tf_op jit(solution)/shard_map/all_to_all | solution.py:579
  52.8 6.4 %collective-permute-done.4.rest_1_ = bf16[4,16,128,128]{3,2,1,0:T(8,128)(2,1)} collective-permute-done((bf16[4,16,128,128]{3,2,1,0:T(8,128)(2,1)}, bf16[4,16,128,128]{3,2,1,0:T(8,128)(2,1)}, u32[]{:S(2)}, u32[]{:S(2)}) %collective-permute-start.4) | collective-permute-done | bytes 2097184 | tf_op jit(solution)/shard_map/ppermute | solution.py:570
  59.1 3.3 %collective-permute-start.6 = (bf16[4,16,128,128]{3,2,1,0:T(8,128)(2,1)}, bf16[4,16,128,128]{3,2,1,0:T(8,128)(2,1)}, u32[]{:S(2)}, u32[]{:S(2)}) collective-permute-start(bf16[4,16,128,128]{3,2,1,0:T(8,128)(2,1)} %collective-permute-done.4.rest_1_), channel_id=1, source_target_pairs={{8,0},{12,4},{16,8},{20,12},{24,16},{28,20},{32,24},{36,28},{40,32... | collective-permute-start | bytes 6291464 | tf_op jit(solution)/shard_map/ppermute | solution.py:570
  65.9 22.2 %collective-permute-done.above = bf16[8,528,128]{2,1,0:T(8,128)(2,1)S(1)} collective-permute-done((bf16[8,528,128]{2,1,0:T(8,128)(2,1)S(1)}, bf16[8,528,128]{2,1,0:T(8,128)(2,1)S(1)}, u32[]{:S(2)}, u32[]{:S(2)}) %collective-permute-start) | collective-permute-done | bytes 1081376 | tf_op jit(solution)/shard_map/ppermute | solution.py:577
  89.1 3.7 %collective-permute-start.3 = (bf16[4,528,128]{2,1,0:T(8,128)(2,1)}, bf16[4,528,128]{2,1,0:T(8,128)(2,1)}, u32[]{:S(2)}, u32[]{:S(2)}) collective-permute-start(bf16[4,528,128]{2,1,0:T(8,128)(2,1)} %slice.27), channel_id=1, source_target_pairs={{1,0},{2,1},{3,2},{0,3},{5,4},{6,5},{7,6},{4,7},{9,8},{10,9},{11,1... | collective-permute-start | bytes 1622024 | tf_op jit(solution)/shard_map/ppermute | solution.py:585
  95.8 7.2 %collective-permute-done.3.far_high = bf16[4,528,128]{2,1,0:T(8,128)(2,1)} collective-permute-done((bf16[4,528,128]{2,1,0:T(8,128)(2,1)}, bf16[4,528,128]{2,1,0:T(8,128)(2,1)}, u32[]{:S(2)}, u32[]{:S(2)}) %collective-permute-start.3) | collective-permute-done | bytes 540704 | tf_op jit(solution)/shard_map/ppermute | solution.py:585
  103.0 4.6 %collective-permute-done.2.far_low = bf16[4,528,128]{2,1,0:T(8,128)(2,1)} collective-permute-done((bf16[4,528,128]{2,1,0:T(8,128)(2,1)}, bf16[4,528,128]{2,1,0:T(8,128)(2,1)}, u32[]{:S(2)}, u32[]{:S(2)}) %collective-permute-start.2) | collective-permute-done | bytes 540704 | tf_op jit(solution)/shard_map/ppermute | solution.py:584
  113.9 11.5 %contract.3 = s16[8,4,336,128]{3,2,1,0:T(8,128)(2,1)} custom-call(s32[3]{0:T(128)} %copy-done.7, s32[128]{0:T(128)} %reshape.31.meta, s32[512]{0:T(512)} %reshape.27.acts, bf16[8,528,128]{2,1,0:T(8,128)(2,1)} %copy-done.13, bf16[8,528,128]{2,1,0:T(8,128)(2,1)} %copy-done.15, bf16[8,528,128]{2,1,0:T(8,128)(2,1)} %copy-done.14, ...), custom_call_target="tpu_custom_call" | custom-call | flops 21474836480 | bytes 83886080 | tf_op jit(solution)/shard_map/contract/pallas_call | solution.py:289
  125.4 8.4 %all-to-all-start.2 = ((s16[32,336,128]{2,1,0:T(8,128)(2,1)}), s16[32,336,128]{2,1,0:T(8,128)(2,1)}, u32[]{:S(2)}, u32[]{:S(2)}) async-start(s16[32,336,128]{2,1,0:T(8,128)(2,1)} %bitcast.19), calls=%async_computation.2 | async-start | bytes 5505024 | tf_op jit(solution)/shard_map/all_to_all | solution.py:596
  133.8 25.4 %collective-permute-done.9.rest_1_.up = bf16[4,16,128,128]{3,2,1,0:T(8,128)(2,1)} collective-permute-done((bf16[4,16,128,128]{3,2,1,0:T(8,128)(2,1)}, bf16[4,16,128,128]{3,2,1,0:T(8,128)(2,1)}, u32[]{:S(2)}, u32[]{:S(2)}) %collective-permute-start.9) | collective-permute-done | bytes 2097184 | tf_op jit(solution)/shard_map/ppermute | solution.py:570
  163.8 7.0 %contract.4 = s16[8,4,144,128]{3,2,1,0:T(8,128)(2,1)} custom-call(s32[3]{0:T(128)} %copy-done.7, s32[128]{0:T(128)} %reshape.31.meta, s32[512]{0:T(512)} %reshape.27.acts, bf16[8,528,128]{2,1,0:T(8,128)(2,1)} %copy-done.13, bf16[8,528,128]{2,1,0:T(8,128)(2,1)} %copy-done.15, bf16[8,528,128]{2,1,0:T(8,128)(2,1)} %copy-done.14, ...), custom_call_target="tpu_custom_call" | custom-call | flops 8589934592 | bytes 33554432 | tf_op jit(solution)/shard_map/contract/pallas_call | solution.py:289
  170.7 8.7 %all-to-all-start.3 = ((s16[32,144,128]{2,1,0:T(8,128)(2,1)}), s16[32,144,128]{2,1,0:T(8,128)(2,1)}, u32[]{:S(2)}, u32[]{:S(2)}) async-start(s16[32,144,128]{2,1,0:T(8,128)(2,1)} %bitcast.21), calls=%async_computation.3 | async-start | bytes 2359296 | tf_op jit(solution)/shard_map/all_to_all | solution.py:596
  179.5 4.2 %collective-permute-done.10.rest_0_ = bf16[2,16,128,128]{3,2,1,0:T(8,128)(2,1)} collective-permute-done((bf16[2,16,128,128]{3,2,1,0:T(8,128)(2,1)}, bf16[2,16,128,128]{3,2,1,0:T(8,128)(2,1)}, u32[]{:S(2)}, u32[]{:S(2)}) %collective-permute-start.10) | collective-permute-done | bytes 1048608 | tf_op jit(solution)/shard_map/ppermute | solution.py:570
  183.9 5.1 %contract.5 = s16[8,4,80,128]{3,2,1,0:T(8,128)(2,1)} custom-call(s32[3]{0:T(128)} %copy-done.7, s32[128]{0:T(128)} %reshape.31.meta, s32[512]{0:T(512)} %reshape.27.acts, bf16[8,528,128]{2,1,0:T(8,128)(2,1)} %copy-done.13, bf16[8,528,128]{2,1,0:T(8,128)(2,1)} %copy-done.15, bf16[8,528,128]{2,1,0:T(8,128)(2,1)} %copy-done.14, ...), custom_call_target="tpu_custom_call" | custom-call | flops 4294967296 | bytes 16777216 | tf_op jit(solution)/shard_map/contract/pallas_call | solution.py:289
  189.1 8.9 %all-to-all-done.3.refs_6_ = s16[32,144,128]{2,1,0:T(8,128)(2,1)} async-done(((s16[32,144,128]{2,1,0:T(8,128)(2,1)}), s16[32,144,128]{2,1,0:T(8,128)(2,1)}, u32[]{:S(2)}, u32[]{:S(2)}) %all-to-all-start.3) | async-done | bytes 1179680 | tf_op jit(solution)/shard_map/all_to_all | solution.py:596
  198.0 3.9 %all-to-all-start.4 = ((s16[32,80,128]{2,1,0:T(8,128)(2,1)}), s16[32,80,128]{2,1,0:T(8,128)(2,1)S(1)}, u32[]{:S(2)}, u32[]{:S(2)}) async-start(s16[32,80,128]{2,1,0:T(8,128)(2,1)} %bitcast.20), calls=%async_computation.4 | async-start | bytes 1310720 | tf_op jit(solution)/shard_map/all_to_all | solution.py:596
  201.9 4.5 %decode.2 = (f32[64,32,128]{2,1,0:T(8,128)S(1)}, f32[4,32,128]{2,1,0:T(8,128)S(1)}) custom-call(s32[3]{0:T(128)S(1)} %copy-done.8, s32[64]{0:T(128)S(1)} %get-tuple-element.29.refs_1_.route, s32[64]{0:T(128)S(1)} %get-tuple-element.30.refs_2_.rlim, s32[64]{0:T(128)S(1)} %get-tuple-element.31.refs_3_.clim, bf16[64,128,128]{2,1,0:T(8,128)(2,1)S(1)} %copy-done, ...), custom_call_target="tpu_custom_call" | custom-call | flops 1024 | bytes 1024 | tf_op jit(solution)/shard_map/decode/pallas_call | solution.py:397
  207.5 3.5 %decode.3 = (f32[64,32,128]{2,1,0:T(8,128)S(1)}, f32[4,32,128]{2,1,0:T(8,128)S(1)}) custom-call(s32[3]{0:T(128)S(1)} %copy-done.8, s32[64]{0:T(128)S(1)} %get-tuple-element.29.refs_1_.route, s32[64]{0:T(128)S(1)} %get-tuple-element.30.refs_2_.rlim, s32[64]{0:T(128)S(1)} %get-tuple-element.31.refs_3_.clim, bf16[64,128,128]{2,1,0:T(8,128)(2,1)S(1)} %copy-done, ...), custom_call_target="tpu_custom_call" | custom-call | flops 1024 | bytes 1024 | tf_op jit(solution)/shard_map/decode/pallas_call | solution.py:397
  215.0 3.7 %decode_last.1 = (f32[64,32,128]{2,1,0:T(8,128)S(1)}, f32[256,8]{1,0:T(8,128)}) custom-call(s32[3]{0:T(128)S(1)} %copy-done.8, s32[64]{0:T(128)S(1)} %get-tuple-element.29.refs_1_.route, s32[64]{0:T(128)S(1)} %get-tuple-element.30.refs_2_.rlim, s32[64]{0:T(128)S(1)} %get-tuple-element.31.refs_3_.clim, bf16[64,128,128]{2,1,0:T(8,128)(2,1)S(1)} %copy-done, ...), custom_call_target="tpu_custom_call" | custom-call | flops 1024 | bytes 1024 | tf_op jit(solution)/shard_map/decode_last/pallas_call | solution.py:397
  219.7 7.9 %all-to-all-start.5 = ((f32[256,1,8]{2,1,0:T(1,128)}), f32[256,1,8]{2,1,0:T(1,128)S(1)}, u32[]{:S(2)}, u32[]{:S(2)}) async-start(f32[256,1,8]{2,1,0:T(1,128)} %bitcast.12), calls=%async_computation.5 | async-start | bytes 262144 | tf_op jit(solution)/shard_map/all_to_all | solution.py:613
  231.3 4.0 %prepare.1 = (bf16[64,32,128]{2,1,0:T(8,128)(2,1)}, f32[64,32,128]{2,1,0:T(8,128)S(1)}, bf16[64,32,128]{2,1,0:T(8,128)(2,1)S(1)}) custom-call(s32[3]{0:T(128)S(1)} %copy-done.8, s32[64]{0:T(128)S(1)} %get-tuple-element.29.refs_1_.route, s32[64]{0:T(128)S(1)} %get-tuple-element.30.refs_2_.rlim, s32[64]{0:T(128)S(1)} %get-tuple-element.31.refs_3_.clim, ...), custom_call_target="tpu_custom_call" | custom-call | bytes 20971520 | tf_op jit(solution)/shard_map/prepare/pallas_call | solution.py:458
  235.3 5.0 %all-to-all-done.5 = f32[256,1,8]{2,1,0:T(1,128)S(1)} async-done(((f32[256,1,8]{2,1,0:T(1,128)}), f32[256,1,8]{2,1,0:T(1,128)S(1)}, u32[]{:S(2)}, u32[]{:S(2)}) %all-to-all-start.5) | async-done | bytes 8224 | tf_op jit(solution)/shard_map/all_to_all | solution.py:613
  (77 shorter events, 36.1 us)
Async XLA Ops:
  7.2 106.7 %all-gather.3.cloned.1.call-start = ((), (), s32[]{:S(2)}) async-start(), calls=%async_computation.6 | async-start | bytes 18874368 | tf_op jit(solution)/shard_map/all_gather | solution.py:573
  7.9 5.4 %copy-start = (bf16[64,128,128]{2,1,0:T(8,128)(2,1)S(1)}, bf16[64,128,128]{2,1,0:T(8,128)(2,1)}, u32[]{:S(2)}) copy-start(bf16[64,128,128]{2,1,0:T(8,128)(2,1)} %psi.3) | copy-start | bytes 6291460
  7.9 5.4 %copy-start.9 = (s32[4096]{0:T(1024)S(1)}, s32[4096]{0:T(1024)}, u32[]{:S(2)}) copy-start(s32[4096]{0:T(1024)} %block_right.1) | copy-start | bytes 49156
  8.0 5.4 %copy-start.10 = (s32[1024]{0:T(1024)S(1)}, s32[1024]{0:T(1024)}, u32[]{:S(2)}) copy-start(s32[1024]{0:T(1024)} %right_dims.1) | copy-start | bytes 12292
  11.3 47.9 %collective-permute-start.4 = (bf16[4,16,128,128]{3,2,1,0:T(8,128)(2,1)}, bf16[4,16,128,128]{3,2,1,0:T(8,128)(2,1)}, u32[]{:S(2)}, u32[]{:S(2)}) collective-permute-start(bf16[4,16,128,128]{3,2,1,0:T(8,128)(2,1)} %broadcast_multiply_fusion.rest_0_), channel_id=1, source_target_pairs={{8,0},{12,4},{16,8},{20,12},{24,16},{28,20},{32,24},{36,28},{40,32... | collective-permute-start | bytes 6291464 | tf_op jit(solution)/shard_map/ppermute | solution.py:570
  13.1 49.8 %collective-permute-start.5 = (bf16[4,16,128,128]{3,2,1,0:T(8,128)(2,1)}, bf16[4,16,128,128]{3,2,1,0:T(8,128)(2,1)}, u32[]{:S(2)}, u32[]{:S(2)}) collective-permute-start(bf16[4,16,128,128]{3,2,1,0:T(8,128)(2,1)} %broadcast_multiply_fusion.rest_0_), channel_id=1, source_target_pairs={{0,8},{4,12},{8,16},{12,20},{16,24},{20,28},{24,32},{28,36},{32,40... | collective-permute-start | bytes 6291464 | tf_op jit(solution)/shard_map/ppermute | solution.py:570
  13.4 30.8 %copy-start.7 = (s32[3]{0:T(128)}, s32[3]{0:T(128)S(1)}, u32[]{:S(2)}) copy-start(s32[3]{0:T(128)S(1)} %pad_add_fusion.place.refs_0_) | copy-start | bytes 40
  13.4 30.8 %copy-start.16 = (s32[4,16]{1,0:T(4,128)S(1)}, s32[4,16]{1,0:T(4,128)}, u32[]{:S(2)}) copy-start(s32[4,16]{1,0:T(4,128)} %param.14) | copy-start | bytes 772
  44.2 49.7 %copy-start.13 = (bf16[8,528,128]{2,1,0:T(8,128)(2,1)}, bf16[8,528,128]{2,1,0:T(8,128)(2,1)S(1)}, u32[]{:S(2)}) copy-start(bf16[8,528,128]{2,1,0:T(8,128)(2,1)S(1)} %all_to_all.36.own) | copy-start | bytes 3244036
  59.1 50.0 %collective-permute-start.6 = (bf16[4,16,128,128]{3,2,1,0:T(8,128)(2,1)}, bf16[4,16,128,128]{3,2,1,0:T(8,128)(2,1)}, u32[]{:S(2)}, u32[]{:S(2)}) collective-permute-start(bf16[4,16,128,128]{3,2,1,0:T(8,128)(2,1)} %collective-permute-done.4.rest_1_), channel_id=1, source_target_pairs={{8,0},{12,4},{16,8},{20,12},{24,16},{28,20},{32,24},{36,28},{40,32... | collective-permute-start | bytes 6291464 | tf_op jit(solution)/shard_map/ppermute | solution.py:570
  62.9 48.0 %collective-permute-start.7 = (bf16[4,16,128,128]{3,2,1,0:T(8,128)(2,1)}, bf16[4,16,128,128]{3,2,1,0:T(8,128)(2,1)}, u32[]{:S(2)}, u32[]{:S(2)}) collective-permute-start(bf16[4,16,128,128]{3,2,1,0:T(8,128)(2,1)} %collective-permute-done.5.rest_2_), channel_id=1, source_target_pairs={{0,8},{4,12},{8,16},{12,20},{16,24},{20,28},{24,32},{28,36},{32,40... | collective-permute-start | bytes 6291464 | tf_op jit(solution)/shard_map/ppermute | solution.py:570
  62.9 25.3 %collective-permute-start = (bf16[8,528,128]{2,1,0:T(8,128)(2,1)S(1)}, bf16[8,528,128]{2,1,0:T(8,128)(2,1)S(1)}, u32[]{:S(2)}, u32[]{:S(2)}) collective-permute-start(bf16[8,528,128]{2,1,0:T(8,128)(2,1)S(1)} %all_to_all.36.own), channel_id=1, source_target_pairs={{1,0},{2,1},{3,2},{0,3},{5,4},{6,5},{7,6},{4,7},{9,8},{10,9},{11,1... | collective-permute-start | bytes 3244040 | tf_op jit(solution)/shard_map/ppermute | solution.py:577
  65.9 26.8 %collective-permute-start.1 = (bf16[8,528,128]{2,1,0:T(8,128)(2,1)S(1)}, bf16[8,528,128]{2,1,0:T(8,128)(2,1)S(1)}, u32[]{:S(2)}, u32[]{:S(2)}) collective-permute-start(bf16[8,528,128]{2,1,0:T(8,128)(2,1)S(1)} %all_to_all.36.own), channel_id=1, source_target_pairs={{0,1},{1,2},{2,3},{3,0},{4,5},{5,6},{6,7},{7,4},{8,9},{9,10},{10,1... | collective-permute-start | bytes 3244040 | tf_op jit(solution)/shard_map/ppermute | solution.py:576
  89.1 13.9 %collective-permute-start.3 = (bf16[4,528,128]{2,1,0:T(8,128)(2,1)}, bf16[4,528,128]{2,1,0:T(8,128)(2,1)}, u32[]{:S(2)}, u32[]{:S(2)}) collective-permute-start(bf16[4,528,128]{2,1,0:T(8,128)(2,1)} %slice.27), channel_id=1, source_target_pairs={{1,0},{2,1},{3,2},{0,3},{5,4},{6,5},{7,6},{4,7},{9,8},{10,9},{11,1... | collective-permute-start | bytes 1622024 | tf_op jit(solution)/shard_map/ppermute | solution.py:585
  93.9 13.6 %collective-permute-start.2 = (bf16[4,528,128]{2,1,0:T(8,128)(2,1)}, bf16[4,528,128]{2,1,0:T(8,128)(2,1)}, u32[]{:S(2)}, u32[]{:S(2)}) collective-permute-start(bf16[4,528,128]{2,1,0:T(8,128)(2,1)} %slice.26), channel_id=1, source_target_pairs={{0,1},{1,2},{2,3},{3,0},{4,5},{5,6},{6,7},{7,4},{8,9},{9,10},{10,1... | collective-permute-start | bytes 1622024 | tf_op jit(solution)/shard_map/ppermute | solution.py:584
  110.9 48.3 %collective-permute-start.8 = (bf16[4,16,128,128]{3,2,1,0:T(8,128)(2,1)}, bf16[4,16,128,128]{3,2,1,0:T(8,128)(2,1)}, u32[]{:S(2)}, u32[]{:S(2)}) collective-permute-start(bf16[4,16,128,128]{3,2,1,0:T(8,128)(2,1)} %collective-permute-done.6.rest_3_), channel_id=1, source_target_pairs={{8,0},{12,4},{16,8},{20,12},{24,16},{28,20},{32,24},{36,28},{40,32... | collective-permute-start | bytes 6291464 | tf_op jit(solution)/shard_map/ppermute | solution.py:570
  113.9 45.3 %collective-permute-start.9 = (bf16[4,16,128,128]{3,2,1,0:T(8,128)(2,1)}, bf16[4,16,128,128]{3,2,1,0:T(8,128)(2,1)}, u32[]{:S(2)}, u32[]{:S(2)}) collective-permute-start(bf16[4,16,128,128]{3,2,1,0:T(8,128)(2,1)} %collective-permute-done.7.rest_4_), channel_id=1, source_target_pairs={{0,8},{4,12},{8,16},{12,20},{16,24},{20,28},{24,32},{28,36},{32,40... | collective-permute-start | bytes 6291464 | tf_op jit(solution)/shard_map/ppermute | solution.py:570
  125.4 45.3 %all-to-all-start.2 = ((s16[32,336,128]{2,1,0:T(8,128)(2,1)}), s16[32,336,128]{2,1,0:T(8,128)(2,1)}, u32[]{:S(2)}, u32[]{:S(2)}) async-start(s16[32,336,128]{2,1,0:T(8,128)(2,1)} %bitcast.19), calls=%async_computation.2 | async-start | bytes 5505024 | tf_op jit(solution)/shard_map/all_to_all | solution.py:596
  161.6 22.1 %collective-permute-start.10 = (bf16[2,16,128,128]{3,2,1,0:T(8,128)(2,1)}, bf16[2,16,128,128]{3,2,1,0:T(8,128)(2,1)}, u32[]{:S(2)}, u32[]{:S(2)}) collective-permute-start(bf16[2,16,128,128]{3,2,1,0:T(8,128)(2,1)} %get-tuple-element.41), channel_id=1, source_target_pairs={{0,8},{4,12},{8,16},{12,20},{16,24},{20,28},{24,32},{28,36},{32,40... | collective-permute-start | bytes 3145736 | tf_op jit(solution)/shard_map/ppermute | solution.py:570
  162.0 21.9 %collective-permute-start.11 = (bf16[2,16,128,128]{3,2,1,0:T(8,128)(2,1)}, bf16[2,16,128,128]{3,2,1,0:T(8,128)(2,1)}, u32[]{:S(2)}, u32[]{:S(2)}) collective-permute-start(bf16[2,16,128,128]{3,2,1,0:T(8,128)(2,1)} %get-tuple-element.42), channel_id=1, source_target_pairs={{8,0},{12,4},{16,8},{20,12},{24,16},{28,20},{32,24},{36,28},{40,32... | collective-permute-start | bytes 3145736 | tf_op jit(solution)/shard_map/ppermute | solution.py:570
  170.7 27.3 %all-to-all-start.3 = ((s16[32,144,128]{2,1,0:T(8,128)(2,1)}), s16[32,144,128]{2,1,0:T(8,128)(2,1)}, u32[]{:S(2)}, u32[]{:S(2)}) async-start(s16[32,144,128]{2,1,0:T(8,128)(2,1)} %bitcast.21), calls=%async_computation.3 | async-start | bytes 2359296 | tf_op jit(solution)/shard_map/all_to_all | solution.py:596
  179.5 22.5 %copy-start.8 = (s32[3]{0:T(128)S(1)}, s32[3]{0:T(128)}, u32[]{:S(2)}) copy-start(s32[3]{0:T(128)} %copy-done.7) | copy-start | bytes 40
  198.0 17.0 %all-to-all-start.4 = ((s16[32,80,128]{2,1,0:T(8,128)(2,1)}), s16[32,80,128]{2,1,0:T(8,128)(2,1)S(1)}, u32[]{:S(2)}, u32[]{:S(2)}) async-start(s16[32,80,128]{2,1,0:T(8,128)(2,1)} %bitcast.20), calls=%async_computation.4 | async-start | bytes 1310720 | tf_op jit(solution)/shard_map/all_to_all | solution.py:596
  219.7 20.6 %all-to-all-start.5 = ((f32[256,1,8]{2,1,0:T(1,128)}), f32[256,1,8]{2,1,0:T(1,128)S(1)}, u32[]{:S(2)}, u32[]{:S(2)}) async-start(f32[256,1,8]{2,1,0:T(1,128)} %bitcast.12), calls=%async_computation.5 | async-start | bytes 262144 | tf_op jit(solution)/shard_map/all_to_all | solution.py:613
  (11 other events, 24.0 us)
Sparse Core Ops, SparseCore 0:
  9.9 96.7 all-gather.2
